TPU v7x, 32 devices: a whole 2x2x4 slice. The times are simulated.
32 devices in a mesh: grp: 4 (over y, x), dom: 8 (over z, core).
Axes of the slice: x: 2, y: 2, z: 4, core: 2. Of those that a mesh axis runs over, the one named last changes fastest.
Arguments:
- pert_fcst: bfloat16 [8, 8, 2, 8, 512], P('grp', None, None, 'dom'), may hold values from -6 to 6
- control: float32 [8, 8, 32, 128], P('grp', None, 'dom'), may hold values from -6 to 6
- departures: float32 [8, 2, 32, 128], P(None, None, 'dom'), may hold values from -6 to 6
- obs_weight: float32 [8, 2, 32, 128], P(None, None, 'dom'), may hold values from 0.3 to 3
- diff_rate: float32 [8], replicated, may hold values from 0.05 to 0.24
- step_counts: int32 [8], replicated, may hold values from 1 to 4, as said below
Outputs:
- increment: float32 [8, 2, 32, 128], P(None, None, 'dom')
- gradient: float32 [8, 8, 32, 128], P('grp', None, 'dom')
Inputs may be any that keep to these rules, and one draw needn't show every extreme that they name: `step_counts`: some level has exactly 4 sweeps.
All inputs are finite; a program needn't handle non-finite values.
Results may differ from a plain program's by a relative error of at most 0.0003.
Values may be sent and summed in bfloat16 or wider, within the bound.
No kernel may reach another device: no remote copies, remote signals or barrier semaphores. Data moves between devices by JAX's collectives and lax.ppermute only.
A program may use at most 64 MiB of HBM per device.

v0:
```python
import math

import jax
import jax.numpy as jnp
from jax import lax
from jax.sharding import PartitionSpec as P

NSTEP = 4


def extended(block, sides, width):
    for axis, dim in sides:
        count = lax.axis_size(axis)
        forward = [(i, i + 1) for i in range(count - 1)]
        backward = [(target, source) for source, target in forward]
        low = lax.ppermute(
            lax.slice_in_dim(block, block.shape[dim] - width, None, axis=dim), axis, forward
        )
        high = lax.ppermute(lax.slice_in_dim(block, 0, width, axis=dim), axis, backward)
        block = jnp.concatenate([low, block, high], axis=dim)
    return block


def sweep_once(padded, center, rate_grid):
    laplace = (
        padded[:, :, 2:]
        + padded[:, :, :-2]
        + jnp.roll(center, 1, axis=3)
        + jnp.roll(center, -1, axis=3)
        - 4.0 * center
    )
    return center + rate_grid * laplace


def diffuse(field_now, diff_rate, step_counts):
    rate_grid = diff_rate[None, :, None, None]
    active_all = step_counts[None, :, None, None]
    for sweep_index in range(NSTEP):
        padded = extended(field_now, (("dom", 2),), 1)
        updated = sweep_once(padded, field_now, rate_grid)
        field_now = jnp.where(sweep_index < active_all, updated, field_now)
    return field_now


def from_blocks(blocks, strip_rows, lon_cells):
    leading, dom_count = (blocks.shape[0], blocks.shape[1])
    block_lon = lon_cells // dom_count
    return (
        blocks.reshape(leading, dom_count, strip_rows, block_lon)
        .transpose(0, 2, 1, 3)
        .reshape(leading, strip_rows, lon_cells)
    )


def per_device(pert_fcst, control, departures, obs_weight, diff_rate, step_counts):
    members_dev, levels, variables = (pert_fcst.shape[0], pert_fcst.shape[1], pert_fcst.shape[2])
    strip_rows, lon_cells = (control.shape[2], control.shape[3])
    dom_count = lax.axis_size("dom")
    member_count = members_dev * lax.axis_size("grp")
    factor = 1.0 / math.sqrt(member_count - 1)
    localized = diffuse(control, diff_rate, step_counts)
    received = lax.all_to_all(
        pert_fcst.reshape(members_dev * levels * variables, dom_count, -1),
        "dom",
        split_axis=1,
        concat_axis=1,
        tiled=True,
    )
    perturb = from_blocks(received, strip_rows, lon_cells).reshape(
        members_dev, levels, variables, strip_rows, lon_cells
    )
    partial_sum = jnp.sum(perturb.astype(jnp.float32) * localized[:, :, None], axis=0)
    increment = lax.psum(partial_sum, "grp") * factor
    residual = obs_weight * (increment - departures)
    adjoint = jnp.sum(perturb.astype(jnp.float32) * residual[None], axis=2) * factor
    gradient = control + diffuse(adjoint, diff_rate, step_counts)
    return (increment, gradient)


def solution(mesh):
    in_specs = (
        P("grp", None, None, "dom", None),
        P("grp", None, "dom", None),
        P(None, None, "dom", None),
        P(None, None, "dom", None),
        P(),
        P(),
    )
    out_specs = (P(None, None, "dom", None), P("grp", None, "dom", None))
    return jax.shard_map(
        per_device, mesh=mesh, in_specs=in_specs, out_specs=out_specs, check_vma=False
    )
```

profile of v0, /device:TPU:1, one launch (start us, length us, event | category | flops | bytes accessed | tf_op | source)
XLA Modules:
  0.0 86.9 jit_solution(9826910794845826519)
XLA Ops:
  0.6 0.9 %reshape.23 = bf16[32,8,64]{2,1,0:T(8,128)(2,1)S(1)} reshape(bf16[2,8,2,1,512]{4,2,3,1,0:T(2,128)(2,1)} %param.6) | data formatting | bytes 65536 | tf_op jit(solution)/shard_map/reshape | solution.py:63
  1.5 0.7 reshape.26
  2.3 6.5 %all-to-all-start = ((bf16[8,2,1024]{2,1,0:T(2,128)(2,1)}), bf16[8,2,1024]{2,1,0:T(2,128)(2,1)S(1)}, u32[]{:S(2)}, u32[]{:S(2)}) async-start(bf16[8,2,1024]{2,1,0:T(2,128)(2,1)} %reshape.26), calls=%async_computation | async-start | bytes 65536 | tf_op jit(solution)/shard_map/all_to_all | solution.py:62
  8.8 3.5 %collective-permute-start.1 = (f32[2,8,1,128]{3,2,1,0:T(1,128)S(1)}, f32[2,8,1,128]{3,2,1,0:T(1,128)S(1)}, u32[]{:S(2)}, u32[]{:S(2)}) collective-permute-start(f32[2,8,1,128]{3,2,1,0:T(1,128)S(1)} %get-tuple-element.51), channel_id=1, source_target_pairs={{0,1},{1,2},{2,3},{3,4},{4,5},{5,6},{6,7},{8,9},{9,10},{10,11},{11... | collective-permute-start | bytes 24584 | tf_op jit(solution)/shard_map/ppermute | solution.py:16
  12.3 1.9 %collective-permute-start = (f32[2,8,1,128]{3,2,1,0:T(1,128)S(1)}, f32[2,8,1,128]{3,2,1,0:T(1,128)S(1)}, u32[]{:S(2)}, u32[]{:S(2)}) collective-permute-start(f32[2,8,1,128]{3,2,1,0:T(1,128)S(1)} %get-tuple-element.50), channel_id=1, source_target_pairs={{1,0},{2,1},{3,2},{4,3},{5,4},{6,5},{7,6},{9,8},{10,9},{11,10},{12... | collective-permute-start | bytes 24584 | tf_op jit(solution)/shard_map/ppermute | solution.py:19
  14.4 0.6 copy-done.4
  15.0 2.3 %collective-permute-done = f32[2,8,1,128]{3,2,1,0:T(1,128)S(1)} collective-permute-done((f32[2,8,1,128]{3,2,1,0:T(1,128)S(1)}, f32[2,8,1,128]{3,2,1,0:T(1,128)S(1)}, u32[]{:S(2)}, u32[]{:S(2)}) %collective-permute-start) | collective-permute-done | bytes 8224 | tf_op jit(solution)/shard_map/ppermute | solution.py:19
  17.3 0.7 copy-done.1
  18.2 1.9 %collective-permute-start.3 = (f32[2,8,1,128]{3,2,1,0:T(1,128)S(1)}, f32[2,8,1,128]{3,2,1,0:T(1,128)S(1)}, u32[]{:S(2)}, u32[]{:S(2)}) collective-permute-start(f32[2,8,1,128]{3,2,1,0:T(1,128)S(1)} %get-tuple-element.45), channel_id=1, source_target_pairs={{0,1},{1,2},{2,3},{3,4},{4,5},{5,6},{6,7},{8,9},{9,10},{10,11},{11... | collective-permute-start | bytes 24584 | tf_op jit(solution)/shard_map/ppermute | solution.py:16
  20.1 2.4 %collective-permute-start.2 = (f32[2,8,1,128]{3,2,1,0:T(1,128)S(1)}, f32[2,8,1,128]{3,2,1,0:T(1,128)S(1)}, u32[]{:S(2)}, u32[]{:S(2)}) collective-permute-start(f32[2,8,1,128]{3,2,1,0:T(1,128)S(1)} %get-tuple-element.44), channel_id=1, source_target_pairs={{1,0},{2,1},{3,2},{4,3},{5,4},{6,5},{7,6},{9,8},{10,9},{11,10},{12... | collective-permute-start | bytes 24584 | tf_op jit(solution)/shard_map/ppermute | solution.py:19
  22.6 2.5 %collective-permute-done.2 = f32[2,8,1,128]{3,2,1,0:T(1,128)S(1)} collective-permute-done((f32[2,8,1,128]{3,2,1,0:T(1,128)S(1)}, f32[2,8,1,128]{3,2,1,0:T(1,128)S(1)}, u32[]{:S(2)}, u32[]{:S(2)}) %collective-permute-start.2) | collective-permute-done | bytes 8224 | tf_op jit(solution)/shard_map/ppermute | solution.py:19
  25.3 1.9 %collective-permute-start.5 = (f32[2,8,1,128]{3,2,1,0:T(1,128)S(1)}, f32[2,8,1,128]{3,2,1,0:T(1,128)S(1)}, u32[]{:S(2)}, u32[]{:S(2)}) collective-permute-start(f32[2,8,1,128]{3,2,1,0:T(1,128)S(1)} %get-tuple-element.39), channel_id=1, source_target_pairs={{0,1},{1,2},{2,3},{3,4},{4,5},{5,6},{6,7},{8,9},{9,10},{10,11},{11... | collective-permute-start | bytes 24584 | tf_op jit(solution)/shard_map/ppermute | solution.py:16
  27.3 2.4 %collective-permute-start.4 = (f32[2,8,1,128]{3,2,1,0:T(1,128)S(1)}, f32[2,8,1,128]{3,2,1,0:T(1,128)S(1)}, u32[]{:S(2)}, u32[]{:S(2)}) collective-permute-start(f32[2,8,1,128]{3,2,1,0:T(1,128)S(1)} %get-tuple-element.38), channel_id=1, source_target_pairs={{1,0},{2,1},{3,2},{4,3},{5,4},{6,5},{7,6},{9,8},{10,9},{11,10},{12... | collective-permute-start | bytes 24584 | tf_op jit(solution)/shard_map/ppermute | solution.py:19
  29.8 2.5 %collective-permute-done.4 = f32[2,8,1,128]{3,2,1,0:T(1,128)S(1)} collective-permute-done((f32[2,8,1,128]{3,2,1,0:T(1,128)S(1)}, f32[2,8,1,128]{3,2,1,0:T(1,128)S(1)}, u32[]{:S(2)}, u32[]{:S(2)}) %collective-permute-start.4) | collective-permute-done | bytes 8224 | tf_op jit(solution)/shard_map/ppermute | solution.py:19
  32.5 1.9 %collective-permute-start.7 = (f32[2,8,1,128]{3,2,1,0:T(1,128)S(1)}, f32[2,8,1,128]{3,2,1,0:T(1,128)S(1)}, u32[]{:S(2)}, u32[]{:S(2)}) collective-permute-start(f32[2,8,1,128]{3,2,1,0:T(1,128)S(1)} %get-tuple-element.33), channel_id=1, source_target_pairs={{0,1},{1,2},{2,3},{3,4},{4,5},{5,6},{6,7},{8,9},{9,10},{10,11},{11... | collective-permute-start | bytes 24584 | tf_op jit(solution)/shard_map/ppermute | solution.py:16
  34.4 2.4 %collective-permute-start.6 = (f32[2,8,1,128]{3,2,1,0:T(1,128)S(1)}, f32[2,8,1,128]{3,2,1,0:T(1,128)S(1)}, u32[]{:S(2)}, u32[]{:S(2)}) collective-permute-start(f32[2,8,1,128]{3,2,1,0:T(1,128)S(1)} %get-tuple-element.32), channel_id=1, source_target_pairs={{1,0},{2,1},{3,2},{4,3},{5,4},{6,5},{7,6},{9,8},{10,9},{11,10},{12... | collective-permute-start | bytes 24584 | tf_op jit(solution)/shard_map/ppermute | solution.py:19
  36.9 2.5 %collective-permute-done.6 = f32[2,8,1,128]{3,2,1,0:T(1,128)S(1)} collective-permute-done((f32[2,8,1,128]{3,2,1,0:T(1,128)S(1)}, f32[2,8,1,128]{3,2,1,0:T(1,128)S(1)}, u32[]{:S(2)}, u32[]{:S(2)}) %collective-permute-start.6) | collective-permute-done | bytes 8224 | tf_op jit(solution)/shard_map/ppermute | solution.py:19
  40.6 12.7 %psum.7 = f32[8,2,4,128]{3,2,1,0:T(4,128)S(1)} all-reduce(f32[8,2,4,128]{3,2,1,0:T(4,128)S(1)} %multiply_reduce_fusion.1), channel_id=1, replica_groups=mesh['grp'=4,'dom'=8] {'grp'}, use_global_device_ids=true, to_apply=%region_1.2 | all-reduce | flops 8192 | bytes 65536 | tf_op jit(solution)/shard_map/psum | solution.py:73
  53.3 0.6 subtract_multiply_fusion
  54.1 5.6 %collective-permute-start.9 = (f32[2,8,1,128]{3,2,1,0:T(1,128)S(1)}, f32[2,8,1,128]{3,2,1,0:T(1,128)S(1)}, u32[]{:S(2)}, u32[]{:S(2)}) collective-permute-start(f32[2,8,1,128]{3,2,1,0:T(1,128)S(1)} %get-tuple-element.27), channel_id=1, source_target_pairs={{0,1},{1,2},{2,3},{3,4},{4,5},{5,6},{6,7},{8,9},{9,10},{10,11},{11... | collective-permute-start | bytes 24584 | tf_op jit(solution)/shard_map/ppermute | solution.py:16
  59.7 1.9 %collective-permute-start.8 = (f32[2,8,1,128]{3,2,1,0:T(1,128)S(1)}, f32[2,8,1,128]{3,2,1,0:T(1,128)S(1)}, u32[]{:S(2)}, u32[]{:S(2)}) collective-permute-start(f32[2,8,1,128]{3,2,1,0:T(1,128)S(1)} %get-tuple-element.26), channel_id=1, source_target_pairs={{1,0},{2,1},{3,2},{4,3},{5,4},{6,5},{7,6},{9,8},{10,9},{11,10},{12... | collective-permute-start | bytes 24584 | tf_op jit(solution)/shard_map/ppermute | solution.py:19
  61.7 3.0 %collective-permute-done.8 = f32[2,8,1,128]{3,2,1,0:T(1,128)S(1)} collective-permute-done((f32[2,8,1,128]{3,2,1,0:T(1,128)S(1)}, f32[2,8,1,128]{3,2,1,0:T(1,128)S(1)}, u32[]{:S(2)}, u32[]{:S(2)}) %collective-permute-start.8) | collective-permute-done | bytes 8224 | tf_op jit(solution)/shard_map/ppermute | solution.py:19
  64.9 1.9 %collective-permute-start.11 = (f32[2,8,1,128]{3,2,1,0:T(1,128)S(1)}, f32[2,8,1,128]{3,2,1,0:T(1,128)S(1)}, u32[]{:S(2)}, u32[]{:S(2)}) collective-permute-start(f32[2,8,1,128]{3,2,1,0:T(1,128)S(1)} %get-tuple-element.21), channel_id=1, source_target_pairs={{0,1},{1,2},{2,3},{3,4},{4,5},{5,6},{6,7},{8,9},{9,10},{10,11},{11... | collective-permute-start | bytes 24584 | tf_op jit(solution)/shard_map/ppermute | solution.py:16
  66.9 2.4 %collective-permute-start.10 = (f32[2,8,1,128]{3,2,1,0:T(1,128)S(1)}, f32[2,8,1,128]{3,2,1,0:T(1,128)S(1)}, u32[]{:S(2)}, u32[]{:S(2)}) collective-permute-start(f32[2,8,1,128]{3,2,1,0:T(1,128)S(1)} %get-tuple-element.20), channel_id=1, source_target_pairs={{1,0},{2,1},{3,2},{4,3},{5,4},{6,5},{7,6},{9,8},{10,9},{11,10},{12... | collective-permute-start | bytes 24584 | tf_op jit(solution)/shard_map/ppermute | solution.py:19
  69.3 2.5 %collective-permute-done.10 = f32[2,8,1,128]{3,2,1,0:T(1,128)S(1)} collective-permute-done((f32[2,8,1,128]{3,2,1,0:T(1,128)S(1)}, f32[2,8,1,128]{3,2,1,0:T(1,128)S(1)}, u32[]{:S(2)}, u32[]{:S(2)}) %collective-permute-start.10) | collective-permute-done | bytes 8224 | tf_op jit(solution)/shard_map/ppermute | solution.py:19
  72.1 1.9 %collective-permute-start.13 = (f32[2,8,1,128]{3,2,1,0:T(1,128)S(1)}, f32[2,8,1,128]{3,2,1,0:T(1,128)S(1)}, u32[]{:S(2)}, u32[]{:S(2)}) collective-permute-start(f32[2,8,1,128]{3,2,1,0:T(1,128)S(1)} %get-tuple-element.15), channel_id=1, source_target_pairs={{0,1},{1,2},{2,3},{3,4},{4,5},{5,6},{6,7},{8,9},{9,10},{10,11},{11... | collective-permute-start | bytes 24584 | tf_op jit(solution)/shard_map/ppermute | solution.py:16
  74.0 2.4 %collective-permute-start.12 = (f32[2,8,1,128]{3,2,1,0:T(1,128)S(1)}, f32[2,8,1,128]{3,2,1,0:T(1,128)S(1)}, u32[]{:S(2)}, u32[]{:S(2)}) collective-permute-start(f32[2,8,1,128]{3,2,1,0:T(1,128)S(1)} %get-tuple-element.14), channel_id=1, source_target_pairs={{1,0},{2,1},{3,2},{4,3},{5,4},{6,5},{7,6},{9,8},{10,9},{11,10},{12... | collective-permute-start | bytes 24584 | tf_op jit(solution)/shard_map/ppermute | solution.py:19
  76.5 2.5 %collective-permute-done.12 = f32[2,8,1,128]{3,2,1,0:T(1,128)S(1)} collective-permute-done((f32[2,8,1,128]{3,2,1,0:T(1,128)S(1)}, f32[2,8,1,128]{3,2,1,0:T(1,128)S(1)}, u32[]{:S(2)}, u32[]{:S(2)}) %collective-permute-start.12) | collective-permute-done | bytes 8224 | tf_op jit(solution)/shard_map/ppermute | solution.py:19
  79.2 1.9 %collective-permute-start.15 = (f32[2,8,1,128]{3,2,1,0:T(1,128)S(1)}, f32[2,8,1,128]{3,2,1,0:T(1,128)S(1)}, u32[]{:S(2)}, u32[]{:S(2)}) collective-permute-start(f32[2,8,1,128]{3,2,1,0:T(1,128)S(1)} %get-tuple-element.9), channel_id=1, source_target_pairs={{0,1},{1,2},{2,3},{3,4},{4,5},{5,6},{6,7},{8,9},{9,10},{10,11},{11... | collective-permute-start | bytes 24584 | tf_op jit(solution)/shard_map/ppermute | solution.py:16
  81.2 2.4 %collective-permute-start.14 = (f32[2,8,1,128]{3,2,1,0:T(1,128)S(1)}, f32[2,8,1,128]{3,2,1,0:T(1,128)S(1)}, u32[]{:S(2)}, u32[]{:S(2)}) collective-permute-start(f32[2,8,1,128]{3,2,1,0:T(1,128)S(1)} %get-tuple-element.8), channel_id=1, source_target_pairs={{1,0},{2,1},{3,2},{4,3},{5,4},{6,5},{7,6},{9,8},{10,9},{11,10},{12... | collective-permute-start | bytes 24584 | tf_op jit(solution)/shard_map/ppermute | solution.py:19
  83.6 2.5 %collective-permute-done.14 = f32[2,8,1,128]{3,2,1,0:T(1,128)S(1)} collective-permute-done((f32[2,8,1,128]{3,2,1,0:T(1,128)S(1)}, f32[2,8,1,128]{3,2,1,0:T(1,128)S(1)}, u32[]{:S(2)}, u32[]{:S(2)}) %collective-permute-start.14) | collective-permute-done | bytes 8224 | tf_op jit(solution)/shard_map/ppermute | solution.py:19
  86.1 0.7 fusion
  (58 shorter events, 3.3 us)
Async XLA Ops:
  2.3 6.5 %copy-start = (f32[2,8,4,128]{3,2,1,0:T(4,128)S(1)}, f32[2,8,4,128]{3,2,1,0:T(4,128)}, u32[]{:S(2)}) copy-start(f32[2,8,4,128]{3,2,1,0:T(4,128)} %param.7) | copy-start | bytes 98308
  2.3 37.3 %all-to-all-start = ((bf16[8,2,1024]{2,1,0:T(2,128)(2,1)}), bf16[8,2,1024]{2,1,0:T(2,128)(2,1)S(1)}, u32[]{:S(2)}, u32[]{:S(2)}) async-start(bf16[8,2,1024]{2,1,0:T(2,128)(2,1)} %reshape.26), calls=%async_computation | async-start | bytes 65536 | tf_op jit(solution)/shard_map/all_to_all | solution.py:62
  8.8 6.2 %collective-permute-start.1 = (f32[2,8,1,128]{3,2,1,0:T(1,128)S(1)}, f32[2,8,1,128]{3,2,1,0:T(1,128)S(1)}, u32[]{:S(2)}, u32[]{:S(2)}) collective-permute-start(f32[2,8,1,128]{3,2,1,0:T(1,128)S(1)} %get-tuple-element.51), channel_id=1, source_target_pairs={{0,1},{1,2},{2,3},{3,4},{4,5},{5,6},{6,7},{8,9},{9,10},{10,11},{11... | collective-permute-start | bytes 24584 | tf_op jit(solution)/shard_map/ppermute | solution.py:16
  12.3 5.0 %collective-permute-start = (f32[2,8,1,128]{3,2,1,0:T(1,128)S(1)}, f32[2,8,1,128]{3,2,1,0:T(1,128)S(1)}, u32[]{:S(2)}, u32[]{:S(2)}) collective-permute-start(f32[2,8,1,128]{3,2,1,0:T(1,128)S(1)} %get-tuple-element.50), channel_id=1, source_target_pairs={{1,0},{2,1},{3,2},{4,3},{5,4},{6,5},{7,6},{9,8},{10,9},{11,10},{12... | collective-permute-start | bytes 24584 | tf_op jit(solution)/shard_map/ppermute | solution.py:19
  14.3 0.7 copy-start.4
  17.3 0.7 copy-start.1
  18.2 4.4 %collective-permute-start.3 = (f32[2,8,1,128]{3,2,1,0:T(1,128)S(1)}, f32[2,8,1,128]{3,2,1,0:T(1,128)S(1)}, u32[]{:S(2)}, u32[]{:S(2)}) collective-permute-start(f32[2,8,1,128]{3,2,1,0:T(1,128)S(1)} %get-tuple-element.45), channel_id=1, source_target_pairs={{0,1},{1,2},{2,3},{3,4},{4,5},{5,6},{6,7},{8,9},{9,10},{10,11},{11... | collective-permute-start | bytes 24584 | tf_op jit(solution)/shard_map/ppermute | solution.py:16
  20.1 5.0 %collective-permute-start.2 = (f32[2,8,1,128]{3,2,1,0:T(1,128)S(1)}, f32[2,8,1,128]{3,2,1,0:T(1,128)S(1)}, u32[]{:S(2)}, u32[]{:S(2)}) collective-permute-start(f32[2,8,1,128]{3,2,1,0:T(1,128)S(1)} %get-tuple-element.44), channel_id=1, source_target_pairs={{1,0},{2,1},{3,2},{4,3},{5,4},{6,5},{7,6},{9,8},{10,9},{11,10},{12... | collective-permute-start | bytes 24584 | tf_op jit(solution)/shard_map/ppermute | solution.py:19
  25.3 4.4 %collective-permute-start.5 = (f32[2,8,1,128]{3,2,1,0:T(1,128)S(1)}, f32[2,8,1,128]{3,2,1,0:T(1,128)S(1)}, u32[]{:S(2)}, u32[]{:S(2)}) collective-permute-start(f32[2,8,1,128]{3,2,1,0:T(1,128)S(1)} %get-tuple-element.39), channel_id=1, source_target_pairs={{0,1},{1,2},{2,3},{3,4},{4,5},{5,6},{6,7},{8,9},{9,10},{10,11},{11... | collective-permute-start | bytes 24584 | tf_op jit(solution)/shard_map/ppermute | solution.py:16
  27.3 5.0 %collective-permute-start.4 = (f32[2,8,1,128]{3,2,1,0:T(1,128)S(1)}, f32[2,8,1,128]{3,2,1,0:T(1,128)S(1)}, u32[]{:S(2)}, u32[]{:S(2)}) collective-permute-start(f32[2,8,1,128]{3,2,1,0:T(1,128)S(1)} %get-tuple-element.38), channel_id=1, source_target_pairs={{1,0},{2,1},{3,2},{4,3},{5,4},{6,5},{7,6},{9,8},{10,9},{11,10},{12... | collective-permute-start | bytes 24584 | tf_op jit(solution)/shard_map/ppermute | solution.py:19
  32.5 4.4 %collective-permute-start.7 = (f32[2,8,1,128]{3,2,1,0:T(1,128)S(1)}, f32[2,8,1,128]{3,2,1,0:T(1,128)S(1)}, u32[]{:S(2)}, u32[]{:S(2)}) collective-permute-start(f32[2,8,1,128]{3,2,1,0:T(1,128)S(1)} %get-tuple-element.33), channel_id=1, source_target_pairs={{0,1},{1,2},{2,3},{3,4},{4,5},{5,6},{6,7},{8,9},{9,10},{10,11},{11... | collective-permute-start | bytes 24584 | tf_op jit(solution)/shard_map/ppermute | solution.py:16
  34.4 5.0 %collective-permute-start.6 = (f32[2,8,1,128]{3,2,1,0:T(1,128)S(1)}, f32[2,8,1,128]{3,2,1,0:T(1,128)S(1)}, u32[]{:S(2)}, u32[]{:S(2)}) collective-permute-start(f32[2,8,1,128]{3,2,1,0:T(1,128)S(1)} %get-tuple-element.32), channel_id=1, source_target_pairs={{1,0},{2,1},{3,2},{4,3},{5,4},{6,5},{7,6},{9,8},{10,9},{11,10},{12... | collective-permute-start | bytes 24584 | tf_op jit(solution)/shard_map/ppermute | solution.py:19
  40.5 12.8 %copy-start.2 = (f32[8,2,4,128]{3,2,1,0:T(4,128)S(1)}, f32[8,2,4,128]{3,2,1,0:T(4,128)}, u32[]{:S(2)}) copy-start(f32[8,2,4,128]{3,2,1,0:T(4,128)} %param.9) | copy-start | bytes 98308
  40.6 12.8 %copy-start.3 = (f32[8,2,4,128]{3,2,1,0:T(4,128)S(1)}, f32[8,2,4,128]{3,2,1,0:T(4,128)}, u32[]{:S(2)}) copy-start(f32[8,2,4,128]{3,2,1,0:T(4,128)} %param.8) | copy-start | bytes 98308
  54.1 7.6 %collective-permute-start.9 = (f32[2,8,1,128]{3,2,1,0:T(1,128)S(1)}, f32[2,8,1,128]{3,2,1,0:T(1,128)S(1)}, u32[]{:S(2)}, u32[]{:S(2)}) collective-permute-start(f32[2,8,1,128]{3,2,1,0:T(1,128)S(1)} %get-tuple-element.27), channel_id=1, source_target_pairs={{0,1},{1,2},{2,3},{3,4},{4,5},{5,6},{6,7},{8,9},{9,10},{10,11},{11... | collective-permute-start | bytes 24584 | tf_op jit(solution)/shard_map/ppermute | solution.py:16
  59.7 5.0 %collective-permute-start.8 = (f32[2,8,1,128]{3,2,1,0:T(1,128)S(1)}, f32[2,8,1,128]{3,2,1,0:T(1,128)S(1)}, u32[]{:S(2)}, u32[]{:S(2)}) collective-permute-start(f32[2,8,1,128]{3,2,1,0:T(1,128)S(1)} %get-tuple-element.26), channel_id=1, source_target_pairs={{1,0},{2,1},{3,2},{4,3},{5,4},{6,5},{7,6},{9,8},{10,9},{11,10},{12... | collective-permute-start | bytes 24584 | tf_op jit(solution)/shard_map/ppermute | solution.py:19
  64.9 4.4 %collective-permute-start.11 = (f32[2,8,1,128]{3,2,1,0:T(1,128)S(1)}, f32[2,8,1,128]{3,2,1,0:T(1,128)S(1)}, u32[]{:S(2)}, u32[]{:S(2)}) collective-permute-start(f32[2,8,1,128]{3,2,1,0:T(1,128)S(1)} %get-tuple-element.21), channel_id=1, source_target_pairs={{0,1},{1,2},{2,3},{3,4},{4,5},{5,6},{6,7},{8,9},{9,10},{10,11},{11... | collective-permute-start | bytes 24584 | tf_op jit(solution)/shard_map/ppermute | solution.py:16
  66.9 5.0 %collective-permute-start.10 = (f32[2,8,1,128]{3,2,1,0:T(1,128)S(1)}, f32[2,8,1,128]{3,2,1,0:T(1,128)S(1)}, u32[]{:S(2)}, u32[]{:S(2)}) collective-permute-start(f32[2,8,1,128]{3,2,1,0:T(1,128)S(1)} %get-tuple-element.20), channel_id=1, source_target_pairs={{1,0},{2,1},{3,2},{4,3},{5,4},{6,5},{7,6},{9,8},{10,9},{11,10},{12... | collective-permute-start | bytes 24584 | tf_op jit(solution)/shard_map/ppermute | solution.py:19
  72.1 4.4 %collective-permute-start.13 = (f32[2,8,1,128]{3,2,1,0:T(1,128)S(1)}, f32[2,8,1,128]{3,2,1,0:T(1,128)S(1)}, u32[]{:S(2)}, u32[]{:S(2)}) collective-permute-start(f32[2,8,1,128]{3,2,1,0:T(1,128)S(1)} %get-tuple-element.15), channel_id=1, source_target_pairs={{0,1},{1,2},{2,3},{3,4},{4,5},{5,6},{6,7},{8,9},{9,10},{10,11},{11... | collective-permute-start | bytes 24584 | tf_op jit(solution)/shard_map/ppermute | solution.py:16
  74.0 5.0 %collective-permute-start.12 = (f32[2,8,1,128]{3,2,1,0:T(1,128)S(1)}, f32[2,8,1,128]{3,2,1,0:T(1,128)S(1)}, u32[]{:S(2)}, u32[]{:S(2)}) collective-permute-start(f32[2,8,1,128]{3,2,1,0:T(1,128)S(1)} %get-tuple-element.14), channel_id=1, source_target_pairs={{1,0},{2,1},{3,2},{4,3},{5,4},{6,5},{7,6},{9,8},{10,9},{11,10},{12... | collective-permute-start | bytes 24584 | tf_op jit(solution)/shard_map/ppermute | solution.py:19
  79.2 4.4 %collective-permute-start.15 = (f32[2,8,1,128]{3,2,1,0:T(1,128)S(1)}, f32[2,8,1,128]{3,2,1,0:T(1,128)S(1)}, u32[]{:S(2)}, u32[]{:S(2)}) collective-permute-start(f32[2,8,1,128]{3,2,1,0:T(1,128)S(1)} %get-tuple-element.9), channel_id=1, source_target_pairs={{0,1},{1,2},{2,3},{3,4},{4,5},{5,6},{6,7},{8,9},{9,10},{10,11},{11... | collective-permute-start | bytes 24584 | tf_op jit(solution)/shard_map/ppermute | solution.py:16
  81.2 5.0 %collective-permute-start.14 = (f32[2,8,1,128]{3,2,1,0:T(1,128)S(1)}, f32[2,8,1,128]{3,2,1,0:T(1,128)S(1)}, u32[]{:S(2)}, u32[]{:S(2)}) collective-permute-start(f32[2,8,1,128]{3,2,1,0:T(1,128)S(1)} %get-tuple-element.8), channel_id=1, source_target_pairs={{1,0},{2,1},{3,2},{4,3},{5,4},{6,5},{7,6},{9,8},{10,9},{11,10},{12... | collective-permute-start | bytes 24584 | tf_op jit(solution)/shard_map/ppermute | solution.py:19
where the time goes:
time: 87.7 us; the launch traced here: 86.9 us
  starting transfers between devices  45.4 us (52%)
  waiting for transfers between devices  20.2 us (23%)
  blocking collectives  12.7 us (14%)
  local copies, waits for them, and re-layouts  5.18 us (6%)
  other arithmetic  2.29 us (3%)
  between operations  1.03 us (1%)
    ppermute x8, starting transfers between devices, extended(): lax.ppermute(lax.slice_in_dim(block, block.shape[dim] - width, None, axis...  20.8 us
    ppermute x8, waiting for transfers between devices, extended(): lax.ppermute(lax.slice_in_dim(block, 0, width, axis=dim), axis, backward)  20.2 us
    ppermute x8, starting transfers between devices, extended(): lax.ppermute(lax.slice_in_dim(block, 0, width, axis=dim), axis, backward)  18.1 us
    psum x1, blocking collectives, per_device(): increment = lax.psum(partial_sum, 'grp') * factor  12.7 us
    all_to_all x1, starting transfers between devices, per_device(): lax.all_to_all(pert_fcst.reshape(members_dev * levels * variables, dom_co...  6.51 us
    unnamed x12, local copies, waits for them, and re-layouts  2.09 us
  transfers between devices with their start and end apart: 17, of which 8 were waited for; matrix products, arithmetic and copies ran while one was open for 2% of the time, Pallas kernels for 0%

commit v1 on v0

v1 whole, which is shorter than its diff:
```python
import functools
import math

import jax
import jax.numpy as jnp
from jax import lax
from jax.experimental import pallas as pl
from jax.experimental.pallas import tpu as pltpu
from jax.sharding import PartitionSpec as P

NSTEP = 4
VMEM = pl.BlockSpec(memory_space=pltpu.VMEM)
SMEM = pl.BlockSpec(memory_space=pltpu.SMEM)


def in_vmem(x):
    return pltpu.with_memory_space_constraint(x, pltpu.VMEM)


def pack_kernel(doms, rows, groups, pert_ref, out_ref):
    pairs, variables, cells = pert_ref.shape
    lons = cells // (doms * rows)
    pert = pert_ref[...].astype(jnp.float32)
    fields = jnp.concatenate([pert[:, v, :] for v in range(variables)], axis=0)
    row_of = lax.rem(lax.broadcasted_iota(jnp.int32, fields.shape, 1) // lons, rows)
    spread = jnp.concatenate(
        [jnp.where(row_of == r, fields, 0.0) for r in range(rows)], axis=0
    ).astype(jnp.bfloat16)
    target = lax.broadcasted_iota(jnp.int32, (doms * lons, cells), 0)
    source = lax.broadcasted_iota(jnp.int32, (doms * lons, cells), 1)
    chosen = (target // lons == source // (rows * lons)) & (
        lax.rem(target, lons) == lax.rem(source, lons)
    )
    tiles = lax.dot_general(
        chosen.astype(jnp.float32).astype(jnp.bfloat16),
        spread,
        (((1,), (1,)), ((), ())),
        preferred_element_type=jnp.float32,
    )
    tiles = tiles.astype(jnp.bfloat16).reshape(doms, lons, spread.shape[0])
    for g in range(groups):
        out_ref[pl.ds(g * doms, doms)] = tiles


def sweeps(extended, rates, low_on, high_on, tile):
    rows = list(extended)
    lons = rows[0].shape[1]
    for step in range(NSTEP):
        new = list(rows)
        for i in range(step + 1, len(rows) - 1 - step):
            if i < NSTEP:
                rate = rates[step] * low_on
            elif i >= NSTEP + tile:
                rate = rates[step] * high_on
            else:
                rate = rates[step]
            mid = rows[i]
            laplace = (
                rows[i + 1]
                + rows[i - 1]
                + pltpu.roll(mid, 1, 1)
                + pltpu.roll(mid, lons - 1, 1)
                - 4.0 * mid
            )
            new[i] = mid + rate * laplace
        rows = new
    return rows[NSTEP : NSTEP + tile]


def edges():
    me, count = lax.axis_index("dom"), lax.axis_size("dom")
    odd = lax.rem(me, 2) == 1
    return odd, me > 0, me < count - 1


def with_halo(own, near, far, odd, low, high):
    below = [jnp.where(low, jnp.where(odd, n, f), 0.0) for n, f in zip(near, far)]
    above = [jnp.where(high, jnp.where(odd, f, n), 0.0) for n, f in zip(near, far)]
    return below + own + above


def localize_kernel(members, tile, rate_ref, count_ref, own_ref, near_ref, far_ref, out_ref, rates_ref):
    levels = rate_ref.shape[0]
    shape = (levels, own_ref.shape[1])
    odd, low, high = edges()
    low_on, high_on = low.astype(jnp.float32), high.astype(jnp.float32)
    level_of = lax.broadcasted_iota(jnp.int32, shape, 0)
    rate, count = jnp.zeros(shape, jnp.float32), jnp.zeros(shape, jnp.int32)
    for l in range(levels):
        rate = jnp.where(level_of == l, rate_ref[l], rate)
        count = jnp.where(level_of == l, count_ref[l], count)
    rates = [jnp.where(step < count, rate, 0.0) for step in range(NSTEP)]
    for step in range(NSTEP):
        rates_ref[step] = rates[step]
    for m in range(members):
        own, near, far = (
            [ref[pl.ds(m * levels * tile + r, levels, stride=tile), :] for r in range(tile)]
            for ref in (own_ref, near_ref, far_ref)
        )
        done = sweeps(with_halo(own, near, far, odd, low, high), rates, low_on, high_on, tile)
        for r in range(tile):
            out_ref[pl.ds((m * tile + r) * levels, levels), :] = done[r]


def adjoint_kernel(
    members, levels, variables, tile, groups, factor, tiles_ref, *refs
):
    local_refs, (weight_ref, depart_ref, inc_ref, adj_ref) = refs[:groups], refs[groups:]
    doms = tiles_ref.shape[0] // groups
    lons = inc_ref.shape[1]
    mine = lax.axis_index("grp")
    sums, first = {}, None
    for j in range(groups):
        block = tiles_ref[pl.ds(jnp.bitwise_xor(mine, j) * doms, doms)]
        fields = block.reshape(lons, -1).astype(jnp.float32).T
        if j == 0:
            first = fields
        for r in range(tile):
            for v in range(variables):
                for m in range(members):
                    at = ((r * variables + v) * members + m) * levels
                    term = (
                        fields[at : at + levels]
                        * local_refs[j][pl.ds((m * tile + r) * levels, levels), :]
                    )
                    sums[r, v] = sums[r, v] + term if (r, v) in sums else term
    for r in range(tile):
        residual = []
        for v in range(variables):
            rows = pl.ds(v * tile + r, levels, stride=variables * tile)
            increment = sums[r, v] * factor
            inc_ref[rows, :] = increment
            residual.append(weight_ref[rows, :] * (increment - depart_ref[rows, :]))
        for m in range(members):
            total = None
            for v in range(variables):
                at = ((r * variables + v) * members + m) * levels
                term = first[at : at + levels] * residual[v]
                total = term if total is None else total + term
            adj_ref[pl.ds((m * tile + r) * levels, levels), :] = total * factor


def gradient_kernel(members, tile, rates_ref, own_ref, near_ref, far_ref, control_ref, out_ref):
    levels = rates_ref.shape[1]
    odd, low, high = edges()
    low_on, high_on = low.astype(jnp.float32), high.astype(jnp.float32)
    rates = [rates_ref[step] for step in range(NSTEP)]
    for m in range(members):
        own, near, far = (
            [ref[pl.ds((m * tile + r) * levels, levels), :] for r in range(tile)]
            for ref in (own_ref, near_ref, far_ref)
        )
        done = sweeps(with_halo(own, near, far, odd, low, high), rates, low_on, high_on, tile)
        for r in range(tile):
            rows = pl.ds(m * levels * tile + r, levels, stride=tile)
            out_ref[rows, :] = control_ref[rows, :] + done[r]


def near_pairs(doms):
    return [(i, i ^ 1) for i in range(doms)]


def far_pairs(groups, doms):
    pairs = []
    for g in range(groups):
        for d in range(doms):
            if d in (0, doms - 1):
                pairs.append((g * doms + d, (g ^ 1) * doms + d))
            else:
                pairs.append((g * doms + d, g * doms + (d + 1 if d % 2 else d - 1)))
    return pairs


def beside(x, groups, doms):
    near = lax.ppermute(x, "dom", near_pairs(doms))
    far = lax.ppermute(x, ("grp", "dom"), far_pairs(groups, doms))
    return near, far


def small_device(pert_fcst, control, departures, obs_weight, diff_rate, step_counts):
    members, levels, variables = pert_fcst.shape[:3]
    tile, lons = control.shape[2], control.shape[3]
    groups, doms = lax.axis_size("grp"), lax.axis_size("dom")
    factor = 1.0 / math.sqrt(members * groups - 1)
    fields = members * levels * variables * tile
    flat = control.reshape(-1, lons)
    near, far = beside(flat, groups, doms)
    tiles = pl.pallas_call(
        functools.partial(pack_kernel, doms, tile, groups),
        out_shape=pltpu.VMEM((groups * doms, lons // doms, fields), jnp.bfloat16),
        in_specs=[VMEM],
        out_specs=VMEM,
    )(pert_fcst.reshape(members * levels, variables, -1))
    tiles = lax.all_to_all(tiles, ("grp", "dom"), split_axis=0, concat_axis=0, tiled=True)
    local, rates = pl.pallas_call(
        functools.partial(localize_kernel, members, tile),
        out_shape=[
            pltpu.VMEM(flat.shape, jnp.float32),
            pltpu.VMEM((NSTEP, levels, lons), jnp.float32),
        ],
        in_specs=[SMEM, SMEM, VMEM, VMEM, VMEM],
        out_specs=[VMEM, VMEM],
    )(diff_rate, step_counts, in_vmem(flat), in_vmem(near), in_vmem(far))
    locals_ = [local] + [
        lax.ppermute(local, "grp", [(i, i ^ j) for i in range(groups)]) for j in range(1, groups)
    ]
    increment, adjoint = pl.pallas_call(
        functools.partial(adjoint_kernel, members, levels, variables, tile, groups, factor),
        out_shape=[
            jax.ShapeDtypeStruct((levels * variables * tile, lons), jnp.float32),
            pltpu.VMEM(flat.shape, jnp.float32),
        ],
        in_specs=[VMEM] * (groups + 3),
        out_specs=[VMEM, VMEM],
    )(
        in_vmem(tiles),
        *[in_vmem(x) for x in locals_],
        in_vmem(obs_weight.reshape(-1, lons)),
        in_vmem(departures.reshape(-1, lons)),
    )
    near, far = beside(adjoint, groups, doms)
    gradient = pl.pallas_call(
        functools.partial(gradient_kernel, members, tile),
        out_shape=jax.ShapeDtypeStruct(flat.shape, jnp.float32),
        in_specs=[VMEM] * 5,
        out_specs=VMEM,
    )(in_vmem(rates), in_vmem(adjoint), in_vmem(near), in_vmem(far), in_vmem(flat))
    return increment.reshape(departures.shape), gradient.reshape(control.shape)


def diffuse(field, diff_rate, step_counts):
    count, me = lax.axis_size("dom"), lax.axis_index("dom")
    forward = [(i, i + 1) for i in range(count - 1)]
    backward = [(target, source) for source, target in forward]
    tile = field.shape[2]
    low = lax.ppermute(field[:, :, tile - NSTEP :], "dom", forward)
    high = lax.ppermute(field[:, :, :NSTEP], "dom", backward)
    wide = jnp.concatenate([low, field, high], axis=2)
    row = lax.broadcasted_iota(jnp.int32, (1, 1, wide.shape[2], 1), 2)
    inside = ((row >= NSTEP) | (me > 0)) & ((row < NSTEP + tile) | (me < count - 1))
    for step in range(NSTEP):
        on = (step < step_counts)[None, :, None, None] & inside
        padded = jnp.pad(wide, ((0, 0), (0, 0), (1, 1), (0, 0)))
        laplace = (
            padded[:, :, 2:]
            + padded[:, :, :-2]
            + jnp.roll(wide, 1, axis=3)
            + jnp.roll(wide, -1, axis=3)
            - 4.0 * wide
        )
        wide = jnp.where(on, wide + diff_rate[None, :, None, None] * laplace, wide)
    return wide[:, :, NSTEP : NSTEP + tile]


def any_device(pert_fcst, control, departures, obs_weight, diff_rate, step_counts):
    members, levels, variables = pert_fcst.shape[:3]
    tile, lons = control.shape[2], control.shape[3]
    doms = lax.axis_size("dom")
    factor = 1.0 / math.sqrt(members * lax.axis_size("grp") - 1)
    localized = diffuse(control, diff_rate, step_counts)
    received = lax.all_to_all(
        pert_fcst.reshape(members * levels * variables, doms, -1),
        "dom",
        split_axis=1,
        concat_axis=1,
        tiled=True,
    )
    perturb = (
        received.reshape(-1, doms, tile, lons // doms)
        .transpose(0, 2, 1, 3)
        .reshape(members, levels, variables, tile, lons)
        .astype(jnp.float32)
    )
    increment = lax.psum(jnp.sum(perturb * localized[:, :, None], axis=0), "grp") * factor
    residual = obs_weight * (increment - departures)
    adjoint = jnp.sum(perturb * residual[None], axis=2) * factor
    return increment, control + diffuse(adjoint, diff_rate, step_counts)


def per_device(pert_fcst, control, departures, obs_weight, diff_rate, step_counts):
    members, levels, variables = pert_fcst.shape[:3]
    tile, lons = control.shape[2], control.shape[3]
    groups, doms = lax.axis_size("grp"), lax.axis_size("dom")
    small = (
        lons == 128
        and levels == 8
        and tile == NSTEP
        and members * levels * variables * tile == 128
        and doms % 2 == 0
        and lons // doms == 16
        and groups == 4
    )
    run = small_device if small else any_device
    return run(pert_fcst, control, departures, obs_weight, diff_rate, step_counts)


def solution(mesh):
    in_specs = (
        P("grp", None, None, "dom", None),
        P("grp", None, "dom", None),
        P(None, None, "dom", None),
        P(None, None, "dom", None),
        P(),
        P(),
    )
    out_specs = (P(None, None, "dom", None), P("grp", None, "dom", None))
    return jax.shard_map(
        per_device, mesh=mesh, in_specs=in_specs, out_specs=out_specs, check_vma=False
    )
```

time: 87.7 us -> 28.8 us (0.33)
  the two profiles are of different devices: /device:TPU:1 before, /device:TPU:0 now
where the time goes in v1:
time: 28.8 us; the launch traced here: 28.5 us
  starting transfers between devices  13.5 us (47%)
  waiting for transfers between devices  10 us (35%)
  Pallas kernels  4.3 us (15%)
  between operations  0.68 us (2%)
    all_to_all x1, starting transfers between devices, small_device(): lax.all_to_all(tiles, ('grp', 'dom'), split_axis=0, concat_axis=0, tiled=...  7.3 us
    ppermute x2, waiting for transfers between devices, beside(): far = lax.ppermute(x, ('grp', 'dom'), far_pairs(groups, doms))  5.15 us
    ppermute x3, waiting for transfers between devices, small_device(): lax.ppermute(local, 'grp', [(i, i ^ j) for i in range(groups)])  4.33 us
    ppermute x3, starting transfers between devices, small_device(): lax.ppermute(local, 'grp', [(i, i ^ j) for i in range(groups)])  3.55 us
    ppermute x2, starting transfers between devices, beside(): far = lax.ppermute(x, ('grp', 'dom'), far_pairs(groups, doms))  2.33 us
    pallas_call x1, Pallas kernels, small_device(): pl.pallas_call(functools.partial(pack_kernel, doms, tile, groups), out_sh...  1.62 us
    pallas_call x1, Pallas kernels, small_device(): pl.pallas_call(functools.partial(localize_kernel, members, tile), out_sha...  1 us
    pallas_call x1, Pallas kernels, small_device(): pl.pallas_call(functools.partial(gradient_kernel, members, tile), out_sha...  0.94 us
  transfers between devices with their start and end apart: 8, of which 6 were waited for; matrix products, arithmetic and copies ran while one was open for 0% of the time, Pallas kernels for 3%

profile of v1, /device:TPU:0, one launch (start us, length us, event | category | flops | bytes accessed | tf_op | source)
XLA Modules:
  0.0 28.5 jit_solution(10154050990850993058)
XLA Ops:
  0.6 1.6 %shard_map.77 = bf16[32,16,128]{2,1,0:T(8,128)(2,1)} custom-call(bf16[16,2,512]{2,1,0:T(2,128)(2,1)} %bitcast.12), custom_call_target="tpu_custom_call" | custom-call | tf_op jit(solution)/shard_map/pallas_call | solution.py:188
  2.3 0.0 copy-start
  2.3 7.3 %all-to-all-start = ((bf16[32,16,128]{2,1,0:T(8,128)(2,1)}), bf16[32,16,128]{2,1,0:T(8,128)(2,1)S(1)}, u32[]{:S(2)}, u32[]{:S(2)}) async-start(bf16[32,16,128]{2,1,0:T(8,128)(2,1)} %shard_map.77), calls=%async_computation | async-start | bytes 262144 | tf_op jit(solution)/shard_map/all_to_all | solution.py:194
  9.6 0.0 copy-done
  9.6 0.0 copy-start.1
  9.6 0.0 copy-start.2
  9.6 0.3 %collective-permute-start = (f32[64,128]{1,0:T(8,128)S(1)}, f32[64,128]{1,0:T(8,128)S(1)}, u32[]{:S(2)}, u32[]{:S(2)}) collective-permute-start(f32[64,128]{1,0:T(8,128)S(1)} %bitcast.6), channel_id=1, source_target_pairs={{0,1},{1,0},{2,3},{3,2},{4,5},{5,4},{6,7},{7,6},{8,9},{9,8},{10,11... | collective-permute-start | bytes 98312 | tf_op jit(solution)/shard_map/ppermute | solution.py:175
  9.9 1.7 %collective-permute-start.1 = (f32[64,128]{1,0:T(8,128)S(1)}, f32[64,128]{1,0:T(8,128)S(1)}, u32[]{:S(2)}, u32[]{:S(2)}) collective-permute-start(f32[64,128]{1,0:T(8,128)S(1)} %bitcast.7), channel_id=1, source_target_pairs={{0,8},{1,2},{2,1},{3,4},{4,3},{5,6},{6,5},{7,15},{8,0},{9,10},{10,... | collective-permute-start | bytes 98312 | tf_op jit(solution)/shard_map/ppermute | solution.py:176
  11.6 0.0 collective-permute-done.near_ref
  11.6 2.4 %collective-permute-done.1.far_ref = f32[64,128]{1,0:T(8,128)S(1)} collective-permute-done((f32[64,128]{1,0:T(8,128)S(1)}, f32[64,128]{1,0:T(8,128)S(1)}, u32[]{:S(2)}, u32[]{:S(2)}) %collective-permute-start.1) | collective-permute-done | bytes 32800 | tf_op jit(solution)/shard_map/ppermute | solution.py:176
  14.0 1.0 %shard_map.78 = (f32[64,128]{1,0:T(8,128)S(1)}, f32[4,8,128]{2,1,0:T(8,128)S(1)}) custom-call(f32[8]{0:T(128)} %rate_ref.1, s32[8]{0:T(128)} %count_ref.1, f32[64,128]{1,0:T(8,128)S(1)} %bitcast.8, f32[64,128]{1,0:T(8,128)S(1)} %collective-permute-done.near_ref, f32[64,128]{1,0:T(8,128)S(1)} %collective-permute-done.1.far_ref), custom_call_target="tpu_custom_call" | custom-call | tf_op jit(solution)/shard_map/pallas_call | solution.py:195
  15.0 1.6 %collective-permute-start.2 = (f32[64,128]{1,0:T(8,128)S(1)}, f32[64,128]{1,0:T(8,128)S(1)}, u32[]{:S(2)}, u32[]{:S(2)}) collective-permute-start(f32[64,128]{1,0:T(8,128)S(1)} %get-tuple-element.6.refs_0_), channel_id=1, source_target_pairs={{0,8},{8,0},{16,24},{24,16},{1,9},{9,1},{17,25},{25,17},{2,10},{10... | collective-permute-start | bytes 98312 | tf_op jit(solution)/shard_map/ppermute | solution.py:205
  16.6 1.5 %collective-permute-start.3 = (f32[64,128]{1,0:T(8,128)S(1)}, f32[64,128]{1,0:T(8,128)S(1)}, u32[]{:S(2)}, u32[]{:S(2)}) collective-permute-start(f32[64,128]{1,0:T(8,128)S(1)} %get-tuple-element.6.refs_0_), channel_id=1, source_target_pairs={{0,16},{8,24},{16,0},{24,8},{1,17},{9,25},{17,1},{25,9},{2,18},{10... | collective-permute-start | bytes 98312 | tf_op jit(solution)/shard_map/ppermute | solution.py:205
  18.1 0.5 %collective-permute-start.4 = (f32[64,128]{1,0:T(8,128)S(1)}, f32[64,128]{1,0:T(8,128)S(1)}, u32[]{:S(2)}, u32[]{:S(2)}) collective-permute-start(f32[64,128]{1,0:T(8,128)S(1)} %get-tuple-element.6.refs_0_), channel_id=1, source_target_pairs={{0,24},{8,16},{16,8},{24,0},{1,25},{9,17},{17,9},{25,1},{2,26},{10... | collective-permute-start | bytes 98312 | tf_op jit(solution)/shard_map/ppermute | solution.py:205
  18.6 0.4 %collective-permute-done.2.refs_1_ = f32[64,128]{1,0:T(8,128)S(1)} collective-permute-done((f32[64,128]{1,0:T(8,128)S(1)}, f32[64,128]{1,0:T(8,128)S(1)}, u32[]{:S(2)}, u32[]{:S(2)}) %collective-permute-start.2) | collective-permute-done | bytes 32800 | tf_op jit(solution)/shard_map/ppermute | solution.py:205
  19.0 1.5 %collective-permute-done.3.refs_2_ = f32[64,128]{1,0:T(8,128)S(1)} collective-permute-done((f32[64,128]{1,0:T(8,128)S(1)}, f32[64,128]{1,0:T(8,128)S(1)}, u32[]{:S(2)}, u32[]{:S(2)}) %collective-permute-start.3) | collective-permute-done | bytes 32800 | tf_op jit(solution)/shard_map/ppermute | solution.py:205
  20.5 2.4 %collective-permute-done.4.refs_3_ = f32[64,128]{1,0:T(8,128)S(1)} collective-permute-done((f32[64,128]{1,0:T(8,128)S(1)}, f32[64,128]{1,0:T(8,128)S(1)}, u32[]{:S(2)}, u32[]{:S(2)}) %collective-permute-start.4) | collective-permute-done | bytes 32800 | tf_op jit(solution)/shard_map/ppermute | solution.py:205
  22.9 0.0 all-to-all-done.tiles_ref
  22.9 0.0 copy-done.1
  22.9 0.0 copy-done.2
  22.9 0.7 %shard_map.79 = (f32[64,128]{1,0:T(8,128)}, f32[64,128]{1,0:T(8,128)S(1)}) custom-call(bf16[32,16,128]{2,1,0:T(8,128)(2,1)S(1)} %all-to-all-done.tiles_ref, f32[64,128]{1,0:T(8,128)S(1)} %get-tuple-element.6.refs_0_, f32[64,128]{1,0:T(8,128)S(1)} %collective-permute-done.2.refs_1_, f32[64,128]{1,0:T(8,128)S(1)} %collective-permute-done.3.refs_2_, ...), custom_call_target="tpu_custom_call" | custom-call | tf_op jit(solution)/shard_map/pallas_call | solution.py:207
  23.7 0.0 collective-permute-start.5
  23.7 0.7 %collective-permute-start.6 = (f32[64,128]{1,0:T(8,128)S(1)}, f32[64,128]{1,0:T(8,128)S(1)}, u32[]{:S(2)}, u32[]{:S(2)}) collective-permute-start(f32[64,128]{1,0:T(8,128)S(1)} %get-tuple-element.9.own_ref), channel_id=1, source_target_pairs={{0,8},{1,2},{2,1},{3,4},{4,3},{5,6},{6,5},{7,15},{8,0},{9,10},{10,... | collective-permute-start | bytes 98312 | tf_op jit(solution)/shard_map/ppermute | solution.py:176
  24.3 0.5 %collective-permute-done.5.near_ref = f32[64,128]{1,0:T(8,128)S(1)} collective-permute-done((f32[64,128]{1,0:T(8,128)S(1)}, f32[64,128]{1,0:T(8,128)S(1)}, u32[]{:S(2)}, u32[]{:S(2)}) %collective-permute-start.5) | collective-permute-done | bytes 32800 | tf_op jit(solution)/shard_map/ppermute | solution.py:175
  24.9 2.7 %collective-permute-done.6.far_ref = f32[64,128]{1,0:T(8,128)S(1)} collective-permute-done((f32[64,128]{1,0:T(8,128)S(1)}, f32[64,128]{1,0:T(8,128)S(1)}, u32[]{:S(2)}, u32[]{:S(2)}) %collective-permute-start.6) | collective-permute-done | bytes 32800 | tf_op jit(solution)/shard_map/ppermute | solution.py:176
  27.6 0.9 %shard_map.80 = f32[64,128]{1,0:T(8,128)} custom-call(f32[4,8,128]{2,1,0:T(8,128)S(1)} %get-tuple-element.8.rates_ref, f32[64,128]{1,0:T(8,128)S(1)} %get-tuple-element.9.own_ref, f32[64,128]{1,0:T(8,128)S(1)} %collective-permute-done.5.near_ref, f32[64,128]{1,0:T(8,128)S(1)} %collective-permute-done.6.far_ref, f32[64,128]{1,0:T(8,128)S(1)} %bitcast.9), custom_call_target="tpu_custom_call" | custom-call | tf_op jit(solution)/shard_map/pallas_call | solution.py:222
Async XLA Ops:
  2.3 7.3 %copy-start = (f32[2,8,4,128]{3,2,1,0:T(4,128)S(1)}, f32[2,8,4,128]{3,2,1,0:T(4,128)}, u32[]{:S(2)}) copy-start(f32[2,8,4,128]{3,2,1,0:T(4,128)} %param.7) | copy-start | bytes 98308
  2.3 20.7 %all-to-all-start = ((bf16[32,16,128]{2,1,0:T(8,128)(2,1)}), bf16[32,16,128]{2,1,0:T(8,128)(2,1)S(1)}, u32[]{:S(2)}, u32[]{:S(2)}) async-start(bf16[32,16,128]{2,1,0:T(8,128)(2,1)} %shard_map.77), calls=%async_computation | async-start | bytes 262144 | tf_op jit(solution)/shard_map/all_to_all | solution.py:194
  9.6 13.4 %copy-start.1 = (f32[8,2,4,128]{3,2,1,0:T(4,128)S(1)}, f32[8,2,4,128]{3,2,1,0:T(4,128)}, u32[]{:S(2)}) copy-start(f32[8,2,4,128]{3,2,1,0:T(4,128)} %param.9) | copy-start | bytes 98308
  9.6 13.3 %copy-start.2 = (f32[8,2,4,128]{3,2,1,0:T(4,128)S(1)}, f32[8,2,4,128]{3,2,1,0:T(4,128)}, u32[]{:S(2)}) copy-start(f32[8,2,4,128]{3,2,1,0:T(4,128)} %param.8) | copy-start | bytes 98308
  9.6 2.0 %collective-permute-start = (f32[64,128]{1,0:T(8,128)S(1)}, f32[64,128]{1,0:T(8,128)S(1)}, u32[]{:S(2)}, u32[]{:S(2)}) collective-permute-start(f32[64,128]{1,0:T(8,128)S(1)} %bitcast.6), channel_id=1, source_target_pairs={{0,1},{1,0},{2,3},{3,2},{4,5},{5,4},{6,7},{7,6},{8,9},{9,8},{10,11... | collective-permute-start | bytes 98312 | tf_op jit(solution)/shard_map/ppermute | solution.py:175
  9.9 4.1 %collective-permute-start.1 = (f32[64,128]{1,0:T(8,128)S(1)}, f32[64,128]{1,0:T(8,128)S(1)}, u32[]{:S(2)}, u32[]{:S(2)}) collective-permute-start(f32[64,128]{1,0:T(8,128)S(1)} %bitcast.7), channel_id=1, source_target_pairs={{0,8},{1,2},{2,1},{3,4},{4,3},{5,6},{6,5},{7,15},{8,0},{9,10},{10,... | collective-permute-start | bytes 98312 | tf_op jit(solution)/shard_map/ppermute | solution.py:176
  15.0 4.0 %collective-permute-start.2 = (f32[64,128]{1,0:T(8,128)S(1)}, f32[64,128]{1,0:T(8,128)S(1)}, u32[]{:S(2)}, u32[]{:S(2)}) collective-permute-start(f32[64,128]{1,0:T(8,128)S(1)} %get-tuple-element.6.refs_0_), channel_id=1, source_target_pairs={{0,8},{8,0},{16,24},{24,16},{1,9},{9,1},{17,25},{25,17},{2,10},{10... | collective-permute-start | bytes 98312 | tf_op jit(solution)/shard_map/ppermute | solution.py:205
  16.6 3.9 %collective-permute-start.3 = (f32[64,128]{1,0:T(8,128)S(1)}, f32[64,128]{1,0:T(8,128)S(1)}, u32[]{:S(2)}, u32[]{:S(2)}) collective-permute-start(f32[64,128]{1,0:T(8,128)S(1)} %get-tuple-element.6.refs_0_), channel_id=1, source_target_pairs={{0,16},{8,24},{16,0},{24,8},{1,17},{9,25},{17,1},{25,9},{2,18},{10... | collective-permute-start | bytes 98312 | tf_op jit(solution)/shard_map/ppermute | solution.py:205
  18.1 4.8 %collective-permute-start.4 = (f32[64,128]{1,0:T(8,128)S(1)}, f32[64,128]{1,0:T(8,128)S(1)}, u32[]{:S(2)}, u32[]{:S(2)}) collective-permute-start(f32[64,128]{1,0:T(8,128)S(1)} %get-tuple-element.6.refs_0_), channel_id=1, source_target_pairs={{0,24},{8,16},{16,8},{24,0},{1,25},{9,17},{17,9},{25,1},{2,26},{10... | collective-permute-start | bytes 98312 | tf_op jit(solution)/shard_map/ppermute | solution.py:205
  23.7 1.2 %collective-permute-start.5 = (f32[64,128]{1,0:T(8,128)S(1)}, f32[64,128]{1,0:T(8,128)S(1)}, u32[]{:S(2)}, u32[]{:S(2)}) collective-permute-start(f32[64,128]{1,0:T(8,128)S(1)} %get-tuple-element.9.own_ref), channel_id=1, source_target_pairs={{0,1},{1,0},{2,3},{3,2},{4,5},{5,4},{6,7},{7,6},{8,9},{9,8},{10,11... | collective-permute-start | bytes 98312 | tf_op jit(solution)/shard_map/ppermute | solution.py:175
  23.7 3.9 %collective-permute-start.6 = (f32[64,128]{1,0:T(8,128)S(1)}, f32[64,128]{1,0:T(8,128)S(1)}, u32[]{:S(2)}, u32[]{:S(2)}) collective-permute-start(f32[64,128]{1,0:T(8,128)S(1)} %get-tuple-element.9.own_ref), channel_id=1, source_target_pairs={{0,8},{1,2},{2,1},{3,4},{4,3},{5,6},{6,5},{7,15},{8,0},{9,10},{10,... | collective-permute-start | bytes 98312 | tf_op jit(solution)/shard_map/ppermute | solution.py:176

commit v2 on v1

--- a/solution.py
+++ b/solution.py
@@ -17,7 +17,15 @@
     return pltpu.with_memory_space_constraint(x, pltpu.VMEM)
 
 
-def pack_kernel(doms, rows, groups, pert_ref, out_ref):
+def pack_kernel(doms, rows, groups, rate_ref, count_ref, pert_ref, out_ref, rates_ref):
+    shape = rates_ref.shape[1:]
+    level_of = lax.broadcasted_iota(jnp.int32, shape, 0)
+    rate, count = jnp.zeros(shape, jnp.float32), jnp.zeros(shape, jnp.int32)
+    for l in range(shape[0]):
+        rate = jnp.where(level_of == l, rate_ref[l], rate)
+        count = jnp.where(level_of == l, count_ref[l], count)
+    for step in range(NSTEP):
+        rates_ref[step] = jnp.where(step < count, rate, 0.0)
     pairs, variables, cells = pert_ref.shape
     lons = cells // (doms * rows)
     pert = pert_ref[...].astype(jnp.float32)
@@ -79,19 +87,11 @@
     return below + own + above
 
 
-def localize_kernel(members, tile, rate_ref, count_ref, own_ref, near_ref, far_ref, out_ref, rates_ref):
-    levels = rate_ref.shape[0]
-    shape = (levels, own_ref.shape[1])
+def localize_kernel(members, tile, rates_ref, own_ref, near_ref, far_ref, out_ref):
+    levels = rates_ref.shape[1]
     odd, low, high = edges()
     low_on, high_on = low.astype(jnp.float32), high.astype(jnp.float32)
-    level_of = lax.broadcasted_iota(jnp.int32, shape, 0)
-    rate, count = jnp.zeros(shape, jnp.float32), jnp.zeros(shape, jnp.int32)
-    for l in range(levels):
-        rate = jnp.where(level_of == l, rate_ref[l], rate)
-        count = jnp.where(level_of == l, count_ref[l], count)
-    rates = [jnp.where(step < count, rate, 0.0) for step in range(NSTEP)]
-    for step in range(NSTEP):
-        rates_ref[step] = rates[step]
+    rates = [rates_ref[step] for step in range(NSTEP)]
     for m in range(members):
         own, near, far = (
             [ref[pl.ds(m * levels * tile + r, levels, stride=tile), :] for r in range(tile)]
@@ -185,22 +185,23 @@
     fields = members * levels * variables * tile
     flat = control.reshape(-1, lons)
     near, far = beside(flat, groups, doms)
-    tiles = pl.pallas_call(
+    tiles, rates = pl.pallas_call(
         functools.partial(pack_kernel, doms, tile, groups),
-        out_shape=pltpu.VMEM((groups * doms, lons // doms, fields), jnp.bfloat16),
-        in_specs=[VMEM],
-        out_specs=VMEM,
-    )(pert_fcst.reshape(members * levels, variables, -1))
-    tiles = lax.all_to_all(tiles, ("grp", "dom"), split_axis=0, concat_axis=0, tiled=True)
-    local, rates = pl.pallas_call(
-        functools.partial(localize_kernel, members, tile),
         out_shape=[
-            pltpu.VMEM(flat.shape, jnp.float32),
+            pltpu.VMEM((groups * doms, lons // doms, fields), jnp.bfloat16),
             pltpu.VMEM((NSTEP, levels, lons), jnp.float32),
         ],
-        in_specs=[SMEM, SMEM, VMEM, VMEM, VMEM],
+        in_specs=[SMEM, SMEM, VMEM],
         out_specs=[VMEM, VMEM],
-    )(diff_rate, step_counts, in_vmem(flat), in_vmem(near), in_vmem(far))
+    )(diff_rate, step_counts, in_vmem(pert_fcst.reshape(members * levels, variables, -1)))
+    tiles, near, far = lax.optimization_barrier((tiles, near, far))
+    tiles = lax.all_to_all(tiles, ("grp", "dom"), split_axis=0, concat_axis=0, tiled=True)
+    local = pl.pallas_call(
+        functools.partial(localize_kernel, members, tile),
+        out_shape=pltpu.VMEM(flat.shape, jnp.float32),
+        in_specs=[VMEM] * 4,
+        out_specs=VMEM,
+    )(in_vmem(rates), in_vmem(flat), in_vmem(near), in_vmem(far))
     locals_ = [local] + [
         lax.ppermute(local, "grp", [(i, i ^ j) for i in range(groups)]) for j in range(1, groups)
     ]

time: 28.8 us -> 25.6 us (0.89)
  waiting for transfers between devices: 10 us -> 7.16 us
  Pallas kernels: 4.3 us -> 3.54 us
  local copies, waits for them, and re-layouts: 0.02 us -> 0.77 us
  starting transfers between devices: 13.5 us -> 13.2 us
    ppermute x2, waiting for transfers between devices: 5.15 us -> 2.91 us  [beside(): far = lax.ppermute(x, ('grp', 'dom'), far_pairs(groups, doms))]
    all_to_all x1, starting transfers between devices: 7.3 us -> 5.4 us  [small_device(): lax.all_to_all(tiles, ('grp', 'dom'), split_axis=0, concat_axis=0, tiled=...]
    ppermute x2, starting transfers between devices: 2.33 us -> 3.83 us  [beside(): far = lax.ppermute(x, ('grp', 'dom'), far_pairs(groups, doms))]
    unnamed x6 -> x8, local copies, waits for them, and re-layouts: 0.02 us -> 0.77 us
    pallas_call x1, Pallas kernels: 1 us -> 0.33 us  [small_device(): pl.pallas_call(functools.partial(localize_kernel, members, tile), out_sha...]
    ppermute x3, waiting for transfers between devices: 4.33 us -> 3.71 us  [small_device(): lax.ppermute(local, 'grp', [(i, i ^ j) for i in range(groups)])]
    ppermute x2, waiting for transfers between devices: 0.55 us -> 0.01 us  [beside(): near = lax.ppermute(x, 'dom', near_pairs(doms))]
    all_to_all x1, waiting for transfers between devices: 0.01 us -> 0.54 us  [small_device(): lax.all_to_all(tiles, ('grp', 'dom'), split_axis=0, concat_axis=0, tiled=...]
  transfers between devices with their start and end apart: 8 -> 8, of which waited for: 6 -> 5; matrix products, arithmetic and copies ran while one was open for 0% -> 0% of each run, Pallas kernels for 3% -> 7%
where the time goes in v2:
time: 25.6 us; the launch traced here: 25.3 us
  starting transfers between devices  13.2 us (52%)
  waiting for transfers between devices  7.16 us (28%)
  Pallas kernels  3.54 us (14%)
  local copies, waits for them, and re-layouts  0.77 us (3%)
  between operations  0.69 us (3%)
    all_to_all x1, starting transfers between devices, small_device(): lax.all_to_all(tiles, ('grp', 'dom'), split_axis=0, concat_axis=0, tiled=...  5.4 us
    ppermute x2, starting transfers between devices, beside(): far = lax.ppermute(x, ('grp', 'dom'), far_pairs(groups, doms))  3.83 us
    ppermute x3, waiting for transfers between devices, small_device(): lax.ppermute(local, 'grp', [(i, i ^ j) for i in range(groups)])  3.71 us
    ppermute x3, starting transfers between devices, small_device(): lax.ppermute(local, 'grp', [(i, i ^ j) for i in range(groups)])  3.55 us
    ppermute x2, waiting for transfers between devices, beside(): far = lax.ppermute(x, ('grp', 'dom'), far_pairs(groups, doms))  2.91 us
    pallas_call x1, Pallas kernels, small_device(): pl.pallas_call(functools.partial(pack_kernel, doms, tile, groups), out_sh...  1.54 us
    pallas_call x1, Pallas kernels, small_device(): pl.pallas_call(functools.partial(gradient_kernel, members, tile), out_sha...  0.94 us
    unnamed x8, local copies, waits for them, and re-layouts  0.77 us
  transfers between devices with their start and end apart: 8, of which 5 were waited for; matrix products, arithmetic and copies ran while one was open for 0% of the time, Pallas kernels for 7%

profile of v2, /device:TPU:0, one launch (start us, length us, event | category | flops | bytes accessed | tf_op | source)
XLA Modules:
  0.0 25.3 jit_solution(2732664900254582154)
XLA Ops:
  0.6 3.0 %collective-permute-start.1 = (f32[64,128]{1,0:T(8,128)}, f32[64,128]{1,0:T(8,128)S(1)}, u32[]{:S(2)}, u32[]{:S(2)}) collective-permute-start(f32[64,128]{1,0:T(8,128)} %bitcast.6), channel_id=1, source_target_pairs={{0,8},{1,2},{2,1},{3,4},{4,3},{5,6},{6,5},{7,15},{8,0},{9,10},{10,... | collective-permute-start | bytes 98312 | tf_op jit(solution)/shard_map/ppermute | solution.py:176
  3.6 0.2 collective-permute-start
  3.8 0.0 copy-start.3
  3.8 0.8 %copy-done.3 = bf16[2,8,2,1,512]{4,2,3,1,0:T(2,128)(2,1)S(1)} copy-done((bf16[2,8,2,1,512]{4,2,3,1,0:T(2,128)(2,1)S(1)}, bf16[2,8,2,1,512]{4,2,3,1,0:T(2,128)(2,1)}, u32[]{:S(2)}) %copy-start.3) | copy-done | bytes 32792
  4.6 1.5 %shard_map.77 = (bf16[32,16,128]{2,1,0:T(8,128)(2,1)}, f32[4,8,128]{2,1,0:T(8,128)S(1)}) custom-call(f32[8]{0:T(128)} %rate_ref.1, s32[8]{0:T(128)} %count_ref.1, bf16[16,2,512]{2,1,0:T(2,128)(2,1)S(1)} %bitcast.12), custom_call_target="tpu_custom_call" | custom-call | tf_op jit(solution)/shard_map/pallas_call | solution.py:188
  6.1 0.0 collective-permute-done.1.far_ref
  6.1 0.0 collective-permute-done.near_ref
  6.1 0.0 copy-start
  6.1 5.4 %all-to-all-start = ((bf16[32,16,128]{2,1,0:T(8,128)(2,1)}), bf16[32,16,128]{2,1,0:T(8,128)(2,1)S(1)}, u32[]{:S(2)}, u32[]{:S(2)}) async-start(bf16[32,16,128]{2,1,0:T(8,128)(2,1)} %get-tuple-element.10), calls=%async_computation | async-start | bytes 262144 | tf_op jit(solution)/shard_map/all_to_all | solution.py:198
  11.6 0.0 copy-done
  11.6 0.0 copy-start.1
  11.6 0.0 copy-start.2
  11.6 0.3 %shard_map.78.refs_0_ = f32[64,128]{1,0:T(8,128)S(1)} custom-call(f32[4,8,128]{2,1,0:T(8,128)S(1)} %get-tuple-element.11.rates_ref, f32[64,128]{1,0:T(8,128)S(1)} %bitcast.8, f32[64,128]{1,0:T(8,128)S(1)} %collective-permute-done.near_ref, f32[64,128]{1,0:T(8,128)S(1)} %collective-permute-done.1.far_ref), custom_call_target="tpu_custom_call" | custom-call | tf_op jit(solution)/shard_map/pallas_call | solution.py:199
  11.9 2.7 %collective-permute-start.4 = (f32[64,128]{1,0:T(8,128)S(1)}, f32[64,128]{1,0:T(8,128)S(1)}, u32[]{:S(2)}, u32[]{:S(2)}) collective-permute-start(f32[64,128]{1,0:T(8,128)S(1)} %shard_map.78.refs_0_), channel_id=1, source_target_pairs={{0,24},{8,16},{16,8},{24,0},{1,25},{9,17},{17,9},{25,1},{2,26},{10... | collective-permute-start | bytes 98312 | tf_op jit(solution)/shard_map/ppermute | solution.py:206
  14.7 0.6 %collective-permute-start.3 = (f32[64,128]{1,0:T(8,128)S(1)}, f32[64,128]{1,0:T(8,128)S(1)}, u32[]{:S(2)}, u32[]{:S(2)}) collective-permute-start(f32[64,128]{1,0:T(8,128)S(1)} %shard_map.78.refs_0_), channel_id=1, source_target_pairs={{0,16},{8,24},{16,0},{24,8},{1,17},{9,25},{17,1},{25,9},{2,18},{10... | collective-permute-start | bytes 98312 | tf_op jit(solution)/shard_map/ppermute | solution.py:206
  15.2 0.3 %collective-permute-start.2 = (f32[64,128]{1,0:T(8,128)S(1)}, f32[64,128]{1,0:T(8,128)S(1)}, u32[]{:S(2)}, u32[]{:S(2)}) collective-permute-start(f32[64,128]{1,0:T(8,128)S(1)} %shard_map.78.refs_0_), channel_id=1, source_target_pairs={{0,8},{8,0},{16,24},{24,16},{1,9},{9,1},{17,25},{25,17},{2,10},{10... | collective-permute-start | bytes 98312 | tf_op jit(solution)/shard_map/ppermute | solution.py:206
  15.5 1.5 %collective-permute-done.4.refs_3_ = f32[64,128]{1,0:T(8,128)S(1)} collective-permute-done((f32[64,128]{1,0:T(8,128)S(1)}, f32[64,128]{1,0:T(8,128)S(1)}, u32[]{:S(2)}, u32[]{:S(2)}) %collective-permute-start.4) | collective-permute-done | bytes 32800 | tf_op jit(solution)/shard_map/ppermute | solution.py:206
  17.0 1.7 %collective-permute-done.3.refs_2_ = f32[64,128]{1,0:T(8,128)S(1)} collective-permute-done((f32[64,128]{1,0:T(8,128)S(1)}, f32[64,128]{1,0:T(8,128)S(1)}, u32[]{:S(2)}, u32[]{:S(2)}) %collective-permute-start.3) | collective-permute-done | bytes 32800 | tf_op jit(solution)/shard_map/ppermute | solution.py:206
  18.7 0.5 %collective-permute-done.2.refs_1_ = f32[64,128]{1,0:T(8,128)S(1)} collective-permute-done((f32[64,128]{1,0:T(8,128)S(1)}, f32[64,128]{1,0:T(8,128)S(1)}, u32[]{:S(2)}, u32[]{:S(2)}) %collective-permute-start.2) | collective-permute-done | bytes 32800 | tf_op jit(solution)/shard_map/ppermute | solution.py:206
  19.2 0.5 %all-to-all-done.tiles_ref = bf16[32,16,128]{2,1,0:T(8,128)(2,1)S(1)} async-done(((bf16[32,16,128]{2,1,0:T(8,128)(2,1)}), bf16[32,16,128]{2,1,0:T(8,128)(2,1)S(1)}, u32[]{:S(2)}, u32[]{:S(2)}) %all-to-all-start) | async-done | bytes 131104 | tf_op jit(solution)/shard_map/all_to_all | solution.py:198
  19.7 0.0 copy-done.1
  19.7 0.0 copy-done.2
  19.7 0.7 %shard_map.79 = (f32[64,128]{1,0:T(8,128)}, f32[64,128]{1,0:T(8,128)S(1)}) custom-call(bf16[32,16,128]{2,1,0:T(8,128)(2,1)S(1)} %all-to-all-done.tiles_ref, f32[64,128]{1,0:T(8,128)S(1)} %shard_map.78.refs_0_, f32[64,128]{1,0:T(8,128)S(1)} %collective-permute-done.2.refs_1_, f32[64,128]{1,0:T(8,128)S(1)} %collective-permute-done.3.refs_2_, ...), custom_call_target="tpu_custom_call" | custom-call | tf_op jit(solution)/shard_map/pallas_call | solution.py:208
  20.5 0.8 %collective-permute-start.6 = (f32[64,128]{1,0:T(8,128)S(1)}, f32[64,128]{1,0:T(8,128)S(1)}, u32[]{:S(2)}, u32[]{:S(2)}) collective-permute-start(f32[64,128]{1,0:T(8,128)S(1)} %get-tuple-element.15.own_ref), channel_id=1, source_target_pairs={{0,8},{1,2},{2,1},{3,4},{4,3},{5,6},{6,5},{7,15},{8,0},{9,10},{10,... | collective-permute-start | bytes 98312 | tf_op jit(solution)/shard_map/ppermute | solution.py:176
  21.3 0.2 collective-permute-start.5
  21.5 2.9 %collective-permute-done.6.far_ref = f32[64,128]{1,0:T(8,128)S(1)} collective-permute-done((f32[64,128]{1,0:T(8,128)S(1)}, f32[64,128]{1,0:T(8,128)S(1)}, u32[]{:S(2)}, u32[]{:S(2)}) %collective-permute-start.6) | collective-permute-done | bytes 32800 | tf_op jit(solution)/shard_map/ppermute | solution.py:176
  24.4 0.0 collective-permute-done.5.near_ref
  24.4 0.9 %shard_map.80 = f32[64,128]{1,0:T(8,128)} custom-call(f32[4,8,128]{2,1,0:T(8,128)S(1)} %get-tuple-element.11.rates_ref, f32[64,128]{1,0:T(8,128)S(1)} %get-tuple-element.15.own_ref, f32[64,128]{1,0:T(8,128)S(1)} %collective-permute-done.5.near_ref, f32[64,128]{1,0:T(8,128)S(1)} %collective-permute-done.6.far_ref, f32[64,128]{1,0:T(8,128)S(1)} %bitcast.9), custom_call_target="tpu_custom_call" | custom-call | tf_op jit(solution)/shard_map/pallas_call | solution.py:223
Async XLA Ops:
  0.6 5.5 %collective-permute-start.1 = (f32[64,128]{1,0:T(8,128)}, f32[64,128]{1,0:T(8,128)S(1)}, u32[]{:S(2)}, u32[]{:S(2)}) collective-permute-start(f32[64,128]{1,0:T(8,128)} %bitcast.6), channel_id=1, source_target_pairs={{0,8},{1,2},{2,1},{3,4},{4,3},{5,6},{6,5},{7,15},{8,0},{9,10},{10,... | collective-permute-start | bytes 98312 | tf_op jit(solution)/shard_map/ppermute | solution.py:176
  3.6 2.5 %collective-permute-start = (f32[64,128]{1,0:T(8,128)}, f32[64,128]{1,0:T(8,128)S(1)}, u32[]{:S(2)}, u32[]{:S(2)}) collective-permute-start(f32[64,128]{1,0:T(8,128)} %bitcast.7), channel_id=1, source_target_pairs={{0,1},{1,0},{2,3},{3,2},{4,5},{5,4},{6,7},{7,6},{8,9},{9,8},{10,11... | collective-permute-start | bytes 98312 | tf_op jit(solution)/shard_map/ppermute | solution.py:175
  3.8 0.8 %copy-start.3 = (bf16[2,8,2,1,512]{4,2,3,1,0:T(2,128)(2,1)S(1)}, bf16[2,8,2,1,512]{4,2,3,1,0:T(2,128)(2,1)}, u32[]{:S(2)}) copy-start(bf16[2,8,2,1,512]{4,2,3,1,0:T(2,128)(2,1)} %param.6) | copy-start | bytes 98308
  6.1 5.4 %copy-start = (f32[2,8,4,128]{3,2,1,0:T(4,128)S(1)}, f32[2,8,4,128]{3,2,1,0:T(4,128)}, u32[]{:S(2)}) copy-start(f32[2,8,4,128]{3,2,1,0:T(4,128)} %param.7) | copy-start | bytes 98308
  6.1 13.6 %all-to-all-start = ((bf16[32,16,128]{2,1,0:T(8,128)(2,1)}), bf16[32,16,128]{2,1,0:T(8,128)(2,1)S(1)}, u32[]{:S(2)}, u32[]{:S(2)}) async-start(bf16[32,16,128]{2,1,0:T(8,128)(2,1)} %get-tuple-element.10), calls=%async_computation | async-start | bytes 262144 | tf_op jit(solution)/shard_map/all_to_all | solution.py:198
  11.6 8.2 %copy-start.1 = (f32[8,2,4,128]{3,2,1,0:T(4,128)S(1)}, f32[8,2,4,128]{3,2,1,0:T(4,128)}, u32[]{:S(2)}) copy-start(f32[8,2,4,128]{3,2,1,0:T(4,128)} %param.9) | copy-start | bytes 98308
  11.6 8.2 %copy-start.2 = (f32[8,2,4,128]{3,2,1,0:T(4,128)S(1)}, f32[8,2,4,128]{3,2,1,0:T(4,128)}, u32[]{:S(2)}) copy-start(f32[8,2,4,128]{3,2,1,0:T(4,128)} %param.8) | copy-start | bytes 98308
  11.9 5.1 %collective-permute-start.4 = (f32[64,128]{1,0:T(8,128)S(1)}, f32[64,128]{1,0:T(8,128)S(1)}, u32[]{:S(2)}, u32[]{:S(2)}) collective-permute-start(f32[64,128]{1,0:T(8,128)S(1)} %shard_map.78.refs_0_), channel_id=1, source_target_pairs={{0,24},{8,16},{16,8},{24,0},{1,25},{9,17},{17,9},{25,1},{2,26},{10... | collective-permute-start | bytes 98312 | tf_op jit(solution)/shard_map/ppermute | solution.py:206
  14.7 4.0 %collective-permute-start.3 = (f32[64,128]{1,0:T(8,128)S(1)}, f32[64,128]{1,0:T(8,128)S(1)}, u32[]{:S(2)}, u32[]{:S(2)}) collective-permute-start(f32[64,128]{1,0:T(8,128)S(1)} %shard_map.78.refs_0_), channel_id=1, source_target_pairs={{0,16},{8,24},{16,0},{24,8},{1,17},{9,25},{17,1},{25,9},{2,18},{10... | collective-permute-start | bytes 98312 | tf_op jit(solution)/shard_map/ppermute | solution.py:206
  15.2 4.0 %collective-permute-start.2 = (f32[64,128]{1,0:T(8,128)S(1)}, f32[64,128]{1,0:T(8,128)S(1)}, u32[]{:S(2)}, u32[]{:S(2)}) collective-permute-start(f32[64,128]{1,0:T(8,128)S(1)} %shard_map.78.refs_0_), channel_id=1, source_target_pairs={{0,8},{8,0},{16,24},{24,16},{1,9},{9,1},{17,25},{25,17},{2,10},{10... | collective-permute-start | bytes 98312 | tf_op jit(solution)/shard_map/ppermute | solution.py:206
  20.5 3.9 %collective-permute-start.6 = (f32[64,128]{1,0:T(8,128)S(1)}, f32[64,128]{1,0:T(8,128)S(1)}, u32[]{:S(2)}, u32[]{:S(2)}) collective-permute-start(f32[64,128]{1,0:T(8,128)S(1)} %get-tuple-element.15.own_ref), channel_id=1, source_target_pairs={{0,8},{1,2},{2,1},{3,4},{4,3},{5,6},{6,5},{7,15},{8,0},{9,10},{10,... | collective-permute-start | bytes 98312 | tf_op jit(solution)/shard_map/ppermute | solution.py:176
  21.3 3.1 %collective-permute-start.5 = (f32[64,128]{1,0:T(8,128)S(1)}, f32[64,128]{1,0:T(8,128)S(1)}, u32[]{:S(2)}, u32[]{:S(2)}) collective-permute-start(f32[64,128]{1,0:T(8,128)S(1)} %get-tuple-element.15.own_ref), channel_id=1, source_target_pairs={{0,1},{1,0},{2,3},{3,2},{4,5},{5,4},{6,7},{7,6},{8,9},{9,8},{10,11... | collective-permute-start | bytes 98312 | tf_op jit(solution)/shard_map/ppermute | solution.py:175

commit v3 on v1

--- a/solution.py
+++ b/solution.py
@@ -10,7 +10,6 @@
 
 NSTEP = 4
 VMEM = pl.BlockSpec(memory_space=pltpu.VMEM)
-SMEM = pl.BlockSpec(memory_space=pltpu.SMEM)
 
 
 def in_vmem(x):
@@ -22,7 +21,7 @@
     lons = cells // (doms * rows)
     pert = pert_ref[...].astype(jnp.float32)
     fields = jnp.concatenate([pert[:, v, :] for v in range(variables)], axis=0)
-    row_of = lax.rem(lax.broadcasted_iota(jnp.int32, fields.shape, 1) // lons, rows)
+    row_of = (lax.broadcasted_iota(jnp.int32, fields.shape, 1) // lons) % rows
     spread = jnp.concatenate(
         [jnp.where(row_of == r, fields, 0.0) for r in range(rows)], axis=0
     ).astype(jnp.bfloat16)
@@ -79,19 +78,22 @@
     return below + own + above
 
 
-def localize_kernel(members, tile, rate_ref, count_ref, own_ref, near_ref, far_ref, out_ref, rates_ref):
-    levels = rate_ref.shape[0]
-    shape = (levels, own_ref.shape[1])
+def down_rows(x, lons):
+    wide = jnp.broadcast_to(x.astype(jnp.float32), (x.shape[1], x.shape[1]))
+    on = lax.broadcasted_iota(jnp.int32, wide.shape, 0) == lax.broadcasted_iota(jnp.int32, wide.shape, 1)
+    return jnp.broadcast_to(jnp.sum(jnp.where(on, wide, 0.0), axis=1, keepdims=True), (x.shape[1], lons))
+
+
+def sweep_rates(rate_ref, count_ref, lons):
+    rate, count = down_rows(rate_ref[...], lons), down_rows(count_ref[...], lons)
+    return [jnp.where(step < count, rate, 0.0) for step in range(NSTEP)]
+
+
+def localize_kernel(members, tile, rate_ref, count_ref, own_ref, near_ref, far_ref, out_ref):
+    levels = rate_ref.shape[1]
     odd, low, high = edges()
     low_on, high_on = low.astype(jnp.float32), high.astype(jnp.float32)
-    level_of = lax.broadcasted_iota(jnp.int32, shape, 0)
-    rate, count = jnp.zeros(shape, jnp.float32), jnp.zeros(shape, jnp.int32)
-    for l in range(levels):
-        rate = jnp.where(level_of == l, rate_ref[l], rate)
-        count = jnp.where(level_of == l, count_ref[l], count)
-    rates = [jnp.where(step < count, rate, 0.0) for step in range(NSTEP)]
-    for step in range(NSTEP):
-        rates_ref[step] = rates[step]
+    rates = sweep_rates(rate_ref, count_ref, own_ref.shape[1])
     for m in range(members):
         own, near, far = (
             [ref[pl.ds(m * levels * tile + r, levels, stride=tile), :] for r in range(tile)]
@@ -140,11 +142,11 @@
             adj_ref[pl.ds((m * tile + r) * levels, levels), :] = total * factor
 
 
-def gradient_kernel(members, tile, rates_ref, own_ref, near_ref, far_ref, control_ref, out_ref):
-    levels = rates_ref.shape[1]
+def gradient_kernel(members, tile, rate_ref, count_ref, own_ref, near_ref, far_ref, control_ref, out_ref):
+    levels = rate_ref.shape[1]
     odd, low, high = edges()
     low_on, high_on = low.astype(jnp.float32), high.astype(jnp.float32)
-    rates = [rates_ref[step] for step in range(NSTEP)]
+    rates = sweep_rates(rate_ref, count_ref, own_ref.shape[1])
     for m in range(members):
         own, near, far = (
             [ref[pl.ds((m * tile + r) * levels, levels), :] for r in range(tile)]
@@ -184,30 +186,30 @@
     factor = 1.0 / math.sqrt(members * groups - 1)
     fields = members * levels * variables * tile
     flat = control.reshape(-1, lons)
-    near, far = beside(flat, groups, doms)
+    level_args = [in_vmem(diff_rate.reshape(1, -1)), in_vmem(step_counts.reshape(1, -1))]
     tiles = pl.pallas_call(
         functools.partial(pack_kernel, doms, tile, groups),
         out_shape=pltpu.VMEM((groups * doms, lons // doms, fields), jnp.bfloat16),
         in_specs=[VMEM],
         out_specs=VMEM,
-    )(pert_fcst.reshape(members * levels, variables, -1))
+    )(in_vmem(pert_fcst.reshape(members * levels, variables, -1)))
+    tiles, flat = lax.optimization_barrier((tiles, flat))
+    near, far = beside(flat, groups, doms)
     tiles = lax.all_to_all(tiles, ("grp", "dom"), split_axis=0, concat_axis=0, tiled=True)
-    local, rates = pl.pallas_call(
+    local = pl.pallas_call(
         functools.partial(localize_kernel, members, tile),
-        out_shape=[
-            pltpu.VMEM(flat.shape, jnp.float32),
-            pltpu.VMEM((NSTEP, levels, lons), jnp.float32),
-        ],
-        in_specs=[SMEM, SMEM, VMEM, VMEM, VMEM],
-        out_specs=[VMEM, VMEM],
-    )(diff_rate, step_counts, in_vmem(flat), in_vmem(near), in_vmem(far))
+        out_shape=pltpu.VMEM(flat.shape, jnp.float32),
+        in_specs=[VMEM] * 5,
+        out_specs=VMEM,
+        cost_estimate=pl.CostEstimate(flops=10**10, bytes_accessed=0, transcendentals=0),
+    )(*level_args, in_vmem(flat), in_vmem(near), in_vmem(far))
     locals_ = [local] + [
         lax.ppermute(local, "grp", [(i, i ^ j) for i in range(groups)]) for j in range(1, groups)
     ]
     increment, adjoint = pl.pallas_call(
         functools.partial(adjoint_kernel, members, levels, variables, tile, groups, factor),
         out_shape=[
-            jax.ShapeDtypeStruct((levels * variables * tile, lons), jnp.float32),
+            pltpu.VMEM((levels * variables * tile, lons), jnp.float32),
             pltpu.VMEM(flat.shape, jnp.float32),
         ],
         in_specs=[VMEM] * (groups + 3),
@@ -222,9 +224,9 @@
     gradient = pl.pallas_call(
         functools.partial(gradient_kernel, members, tile),
         out_shape=jax.ShapeDtypeStruct(flat.shape, jnp.float32),
-        in_specs=[VMEM] * 5,
+        in_specs=[VMEM] * 6,
         out_specs=VMEM,
-    )(in_vmem(rates), in_vmem(adjoint), in_vmem(near), in_vmem(far), in_vmem(flat))
+    )(*level_args, in_vmem(adjoint), in_vmem(near), in_vmem(far), in_vmem(flat))
     return increment.reshape(departures.shape), gradient.reshape(control.shape)
 
 

time: 28.8 us -> 23.8 us (0.83)
  waiting for transfers between devices: 10 us -> 5.38 us
  Pallas kernels: 4.3 us -> 2.29 us
  local copies, waits for them, and re-layouts: 0.02 us -> 2.03 us
  starting transfers between devices: 13.5 us -> 13.2 us
    ppermute x2, waiting for transfers between devices: 5.15 us -> 1.72 us  [beside(): far = lax.ppermute(x, ('grp', 'dom'), far_pairs(groups, doms))]
    all_to_all x1, starting transfers between devices: 7.3 us -> 4.84 us  [small_device(): lax.all_to_all(tiles, ('grp', 'dom'), split_axis=0, concat_axis=0, tiled=...]
    unnamed x6 -> x13, local copies, waits for them, and re-layouts: 0.02 us -> 2.03 us
    ppermute x2, starting transfers between devices: 2.33 us -> 3.73 us  [beside(): far = lax.ppermute(x, ('grp', 'dom'), far_pairs(groups, doms))]
    pallas_call x1, Pallas kernels: 1.62 us -> 0.87 us  [small_device(): pl.pallas_call(functools.partial(pack_kernel, doms, tile, groups), out_sh...]
    ppermute x2, starting transfers between devices: 0.32 us -> 1.06 us  [beside(): near = lax.ppermute(x, 'dom', near_pairs(doms))]
    ppermute x3, waiting for transfers between devices: 4.33 us -> 3.65 us  [small_device(): lax.ppermute(local, 'grp', [(i, i ^ j) for i in range(groups)])]
    pallas_call x1, Pallas kernels: 1 us -> 0.33 us  [small_device(): pl.pallas_call(functools.partial(localize_kernel, members, tile), out_sha...]
  transfers between devices with their start and end apart: 8 -> 8, of which waited for: 6 -> 4; matrix products, arithmetic and copies ran while one was open for 0% -> 3% of each run, Pallas kernels for 3% -> 1%
where the time goes in v3:
time: 23.8 us; the launch traced here: 23.6 us
  starting transfers between devices  13.2 us (55%)
  waiting for transfers between devices  5.38 us (23%)
  Pallas kernels  2.29 us (10%)
  local copies, waits for them, and re-layouts  2.03 us (9%)
  between operations  0.7 us (3%)
    all_to_all x1, starting transfers between devices, small_device(): lax.all_to_all(tiles, ('grp', 'dom'), split_axis=0, concat_axis=0, tiled=...  4.84 us
    ppermute x2, starting transfers between devices, beside(): far = lax.ppermute(x, ('grp', 'dom'), far_pairs(groups, doms))  3.73 us
    ppermute x3, waiting for transfers between devices, small_device(): lax.ppermute(local, 'grp', [(i, i ^ j) for i in range(groups)])  3.65 us
    ppermute x3, starting transfers between devices, small_device(): lax.ppermute(local, 'grp', [(i, i ^ j) for i in range(groups)])  3.55 us
    unnamed x13, local copies, waits for them, and re-layouts  2.03 us
    ppermute x2, waiting for transfers between devices, beside(): far = lax.ppermute(x, ('grp', 'dom'), far_pairs(groups, doms))  1.72 us
    ppermute x2, starting transfers between devices, beside(): near = lax.ppermute(x, 'dom', near_pairs(doms))  1.06 us
    pallas_call x1, Pallas kernels, small_device(): pl.pallas_call(functools.partial(gradient_kernel, members, tile), out_sha...  0.96 us
  transfers between devices with their start and end apart: 8, of which 4 were waited for; matrix products, arithmetic and copies ran while one was open for 3% of the time, Pallas kernels for 1%

profile of v3, /device:TPU:0, one launch (start us, length us, event | category | flops | bytes accessed | tf_op | source)
XLA Modules:
  0.0 23.6 jit_solution(9083177240385623157)
XLA Ops:
  0.6 0.0 copy-start
  0.6 0.7 %copy-done = bf16[2,8,2,1,512]{4,2,3,1,0:T(2,128)(2,1)S(1)} copy-done((bf16[2,8,2,1,512]{4,2,3,1,0:T(2,128)(2,1)S(1)}, bf16[2,8,2,1,512]{4,2,3,1,0:T(2,128)(2,1)}, u32[]{:S(2)}) %copy-start) | copy-done | bytes 32792
  1.4 0.0 copy-start.3
  1.4 0.9 %shard_map.77 = bf16[32,16,128]{2,1,0:T(8,128)(2,1)} custom-call(bf16[16,2,512]{2,1,0:T(2,128)(2,1)S(1)} %bitcast.9), custom_call_target="tpu_custom_call" | custom-call | tf_op jit(solution)/shard_map/pallas_call | solution.py:190
  2.3 0.0 copy-done.3
  2.3 2.9 %collective-permute-start.1 = (f32[64,128]{1,0:T(8,128)S(1)}, f32[64,128]{1,0:T(8,128)S(1)}, u32[]{:S(2)}, u32[]{:S(2)}) collective-permute-start(f32[64,128]{1,0:T(8,128)S(1)} %bitcast.12), channel_id=1, source_target_pairs={{0,8},{1,2},{2,1},{3,4},{4,3},{5,6},{6,5},{7,15},{8,0},{9,10},{10,... | collective-permute-start | bytes 98312 | tf_op jit(solution)/shard_map/ppermute | solution.py:178
  5.2 0.2 collective-permute-start
  5.4 4.8 %all-to-all-start = ((bf16[32,16,128]{2,1,0:T(8,128)(2,1)}), bf16[32,16,128]{2,1,0:T(8,128)(2,1)S(1)}, u32[]{:S(2)}, u32[]{:S(2)}) async-start(bf16[32,16,128]{2,1,0:T(8,128)(2,1)} %shard_map.77), calls=%async_computation | async-start | bytes 262144 | tf_op jit(solution)/shard_map/all_to_all | solution.py:198
  10.3 0.0 collective-permute-done.1.far_ref
  10.3 0.0 collective-permute-done.near_ref
  10.3 0.0 copy-start.4
  10.3 0.0 copy-start.5
  10.3 0.6 %copy-done.4 = f32[8]{0:T(128)S(1)} copy-done((f32[8]{0:T(128)S(1)}, f32[8]{0:T(128)}, u32[]{:S(2)}) %copy-start.4) | copy-done | bytes 56
  10.9 0.0 copy-done.5
  10.9 0.0 copy-start.1
  11.0 0.3 %shard_map.78.refs_0_ = f32[64,128]{1,0:T(8,128)S(1)} custom-call(f32[1,8]{1,0:T(1,128)S(1)} %bitcast.16, s32[1,8]{1,0:T(1,128)S(1)} %bitcast.18, f32[64,128]{1,0:T(8,128)S(1)} %bitcast.14, f32[64,128]{1,0:T(8,128)S(1)} %collective-permute-done.near_ref, f32[64,128]{1,0:T(8,128)S(1)} %collective-permute-done.1.far_ref), custom_call_target="tpu_custom_call" | custom-call | flops 10000000000 | tf_op jit(solution)/shard_map/pallas_call | solution.py:199
  11.3 2.7 %collective-permute-start.4 = (f32[64,128]{1,0:T(8,128)S(1)}, f32[64,128]{1,0:T(8,128)S(1)}, u32[]{:S(2)}, u32[]{:S(2)}) collective-permute-start(f32[64,128]{1,0:T(8,128)S(1)} %shard_map.78.refs_0_), channel_id=1, source_target_pairs={{0,24},{8,16},{16,8},{24,0},{1,25},{9,17},{17,9},{25,1},{2,26},{10... | collective-permute-start | bytes 98312 | tf_op jit(solution)/shard_map/ppermute | solution.py:207
  14.0 0.6 %collective-permute-start.3 = (f32[64,128]{1,0:T(8,128)S(1)}, f32[64,128]{1,0:T(8,128)S(1)}, u32[]{:S(2)}, u32[]{:S(2)}) collective-permute-start(f32[64,128]{1,0:T(8,128)S(1)} %shard_map.78.refs_0_), channel_id=1, source_target_pairs={{0,16},{8,24},{16,0},{24,8},{1,17},{9,25},{17,1},{25,9},{2,18},{10... | collective-permute-start | bytes 98312 | tf_op jit(solution)/shard_map/ppermute | solution.py:207
  14.6 0.3 %collective-permute-start.2 = (f32[64,128]{1,0:T(8,128)S(1)}, f32[64,128]{1,0:T(8,128)S(1)}, u32[]{:S(2)}, u32[]{:S(2)}) collective-permute-start(f32[64,128]{1,0:T(8,128)S(1)} %shard_map.78.refs_0_), channel_id=1, source_target_pairs={{0,8},{8,0},{16,24},{24,16},{1,9},{9,1},{17,25},{25,17},{2,10},{10... | collective-permute-start | bytes 98312 | tf_op jit(solution)/shard_map/ppermute | solution.py:207
  14.8 1.5 %collective-permute-done.4.refs_3_ = f32[64,128]{1,0:T(8,128)S(1)} collective-permute-done((f32[64,128]{1,0:T(8,128)S(1)}, f32[64,128]{1,0:T(8,128)S(1)}, u32[]{:S(2)}, u32[]{:S(2)}) %collective-permute-start.4) | collective-permute-done | bytes 32800 | tf_op jit(solution)/shard_map/ppermute | solution.py:207
  16.3 1.8 %collective-permute-done.3.refs_2_ = f32[64,128]{1,0:T(8,128)S(1)} collective-permute-done((f32[64,128]{1,0:T(8,128)S(1)}, f32[64,128]{1,0:T(8,128)S(1)}, u32[]{:S(2)}, u32[]{:S(2)}) %collective-permute-start.3) | collective-permute-done | bytes 32800 | tf_op jit(solution)/shard_map/ppermute | solution.py:207
  18.1 0.4 %collective-permute-done.2.refs_1_ = f32[64,128]{1,0:T(8,128)S(1)} collective-permute-done((f32[64,128]{1,0:T(8,128)S(1)}, f32[64,128]{1,0:T(8,128)S(1)}, u32[]{:S(2)}, u32[]{:S(2)}) %collective-permute-start.2) | collective-permute-done | bytes 32800 | tf_op jit(solution)/shard_map/ppermute | solution.py:207
  18.5 0.0 all-to-all-done.tiles_ref
  18.5 0.0 copy-done.1
  18.5 0.0 copy-done.2
  18.5 0.1 shard_map.79
  18.6 0.8 %collective-permute-start.6 = (f32[64,128]{1,0:T(8,128)S(1)}, f32[64,128]{1,0:T(8,128)S(1)}, u32[]{:S(2)}, u32[]{:S(2)}) collective-permute-start(f32[64,128]{1,0:T(8,128)S(1)} %get-tuple-element.9.own_ref), channel_id=1, source_target_pairs={{0,8},{1,2},{2,1},{3,4},{4,3},{5,6},{6,5},{7,15},{8,0},{9,10},{10,... | collective-permute-start | bytes 98312 | tf_op jit(solution)/shard_map/ppermute | solution.py:178
  19.4 0.9 %collective-permute-start.5 = (f32[64,128]{1,0:T(8,128)S(1)}, f32[64,128]{1,0:T(8,128)S(1)}, u32[]{:S(2)}, u32[]{:S(2)}) collective-permute-start(f32[64,128]{1,0:T(8,128)S(1)} %get-tuple-element.9.own_ref), channel_id=1, source_target_pairs={{0,1},{1,0},{2,3},{3,2},{4,5},{5,4},{6,7},{7,6},{8,9},{9,8},{10,11... | collective-permute-start | bytes 98312 | tf_op jit(solution)/shard_map/ppermute | solution.py:177
  20.3 0.6 %copy.8 = f32[8,2,4,128]{3,2,1,0:T(4,128)} copy(f32[8,2,4,128]{3,2,1,0:T(4,128)S(1)} %bitcast.8) | data formatting | bytes 65536
  20.9 1.7 %collective-permute-done.6.far_ref = f32[64,128]{1,0:T(8,128)S(1)} collective-permute-done((f32[64,128]{1,0:T(8,128)S(1)}, f32[64,128]{1,0:T(8,128)S(1)}, u32[]{:S(2)}, u32[]{:S(2)}) %collective-permute-start.6) | collective-permute-done | bytes 32800 | tf_op jit(solution)/shard_map/ppermute | solution.py:178
  22.6 0.0 collective-permute-done.5.near_ref
  22.6 1.0 %shard_map.80 = f32[64,128]{1,0:T(8,128)} custom-call(f32[1,8]{1,0:T(1,128)S(1)} %bitcast.17, s32[1,8]{1,0:T(1,128)S(1)} %bitcast.19, f32[64,128]{1,0:T(8,128)S(1)} %get-tuple-element.9.own_ref, f32[64,128]{1,0:T(8,128)S(1)} %collective-permute-done.5.near_ref, f32[64,128]{1,0:T(8,128)S(1)} %collective-permute-done.6.far_ref, f32[64,128]{1,0:T(8,128)S(1)} %bitcast.15), custom_call_target="tpu_custom_call" | custom-call | tf_op jit(solution)/shard_map/pallas_call | solution.py:224
  (1 shorter events, 0.0 us)
Async XLA Ops:
  0.6 0.8 %copy-start = (bf16[2,8,2,1,512]{4,2,3,1,0:T(2,128)(2,1)S(1)}, bf16[2,8,2,1,512]{4,2,3,1,0:T(2,128)(2,1)}, u32[]{:S(2)}) copy-start(bf16[2,8,2,1,512]{4,2,3,1,0:T(2,128)(2,1)} %param.6) | copy-start | bytes 98308
  1.4 0.9 %copy-start.3 = (f32[2,8,4,128]{3,2,1,0:T(4,128)S(1)}, f32[2,8,4,128]{3,2,1,0:T(4,128)}, u32[]{:S(2)}) copy-start(f32[2,8,4,128]{3,2,1,0:T(4,128)} %param.7) | copy-start | bytes 98308
  2.3 8.0 %collective-permute-start.1 = (f32[64,128]{1,0:T(8,128)S(1)}, f32[64,128]{1,0:T(8,128)S(1)}, u32[]{:S(2)}, u32[]{:S(2)}) collective-permute-start(f32[64,128]{1,0:T(8,128)S(1)} %bitcast.12), channel_id=1, source_target_pairs={{0,8},{1,2},{2,1},{3,4},{4,3},{5,6},{6,5},{7,15},{8,0},{9,10},{10,... | collective-permute-start | bytes 98312 | tf_op jit(solution)/shard_map/ppermute | solution.py:178
  5.2 5.1 %collective-permute-start = (f32[64,128]{1,0:T(8,128)S(1)}, f32[64,128]{1,0:T(8,128)S(1)}, u32[]{:S(2)}, u32[]{:S(2)}) collective-permute-start(f32[64,128]{1,0:T(8,128)S(1)} %bitcast.13), channel_id=1, source_target_pairs={{0,1},{1,0},{2,3},{3,2},{4,5},{5,4},{6,7},{7,6},{8,9},{9,8},{10,11... | collective-permute-start | bytes 98312 | tf_op jit(solution)/shard_map/ppermute | solution.py:177
  5.4 13.1 %all-to-all-start = ((bf16[32,16,128]{2,1,0:T(8,128)(2,1)}), bf16[32,16,128]{2,1,0:T(8,128)(2,1)S(1)}, u32[]{:S(2)}, u32[]{:S(2)}) async-start(bf16[32,16,128]{2,1,0:T(8,128)(2,1)} %shard_map.77), calls=%async_computation | async-start | bytes 262144 | tf_op jit(solution)/shard_map/all_to_all | solution.py:198
  10.3 0.7 %copy-start.4 = (f32[8]{0:T(128)S(1)}, f32[8]{0:T(128)}, u32[]{:S(2)}) copy-start(f32[8]{0:T(128)} %param.10) | copy-start | bytes 100
  10.3 0.7 %copy-start.5 = (s32[8]{0:T(128)S(1)}, s32[8]{0:T(128)}, u32[]{:S(2)}) copy-start(s32[8]{0:T(128)} %param.11) | copy-start | bytes 100
  10.9 7.6 %copy-start.1 = (f32[8,2,4,128]{3,2,1,0:T(4,128)S(1)}, f32[8,2,4,128]{3,2,1,0:T(4,128)}, u32[]{:S(2)}) copy-start(f32[8,2,4,128]{3,2,1,0:T(4,128)} %param.9) | copy-start | bytes 98308
  10.9 7.6 %copy-start.2 = (f32[8,2,4,128]{3,2,1,0:T(4,128)S(1)}, f32[8,2,4,128]{3,2,1,0:T(4,128)}, u32[]{:S(2)}) copy-start(f32[8,2,4,128]{3,2,1,0:T(4,128)} %param.8) | copy-start | bytes 98308
  11.3 5.0 %collective-permute-start.4 = (f32[64,128]{1,0:T(8,128)S(1)}, f32[64,128]{1,0:T(8,128)S(1)}, u32[]{:S(2)}, u32[]{:S(2)}) collective-permute-start(f32[64,128]{1,0:T(8,128)S(1)} %shard_map.78.refs_0_), channel_id=1, source_target_pairs={{0,24},{8,16},{16,8},{24,0},{1,25},{9,17},{17,9},{25,1},{2,26},{10... | collective-permute-start | bytes 98312 | tf_op jit(solution)/shard_map/ppermute | solution.py:207
  14.0 4.0 %collective-permute-start.3 = (f32[64,128]{1,0:T(8,128)S(1)}, f32[64,128]{1,0:T(8,128)S(1)}, u32[]{:S(2)}, u32[]{:S(2)}) collective-permute-start(f32[64,128]{1,0:T(8,128)S(1)} %shard_map.78.refs_0_), channel_id=1, source_target_pairs={{0,16},{8,24},{16,0},{24,8},{1,17},{9,25},{17,1},{25,9},{2,18},{10... | collective-permute-start | bytes 98312 | tf_op jit(solution)/shard_map/ppermute | solution.py:207
  14.6 3.9 %collective-permute-start.2 = (f32[64,128]{1,0:T(8,128)S(1)}, f32[64,128]{1,0:T(8,128)S(1)}, u32[]{:S(2)}, u32[]{:S(2)}) collective-permute-start(f32[64,128]{1,0:T(8,128)S(1)} %shard_map.78.refs_0_), channel_id=1, source_target_pairs={{0,8},{8,0},{16,24},{24,16},{1,9},{9,1},{17,25},{25,17},{2,10},{10... | collective-permute-start | bytes 98312 | tf_op jit(solution)/shard_map/ppermute | solution.py:207
  18.6 4.0 %collective-permute-start.6 = (f32[64,128]{1,0:T(8,128)S(1)}, f32[64,128]{1,0:T(8,128)S(1)}, u32[]{:S(2)}, u32[]{:S(2)}) collective-permute-start(f32[64,128]{1,0:T(8,128)S(1)} %get-tuple-element.9.own_ref), channel_id=1, source_target_pairs={{0,8},{1,2},{2,1},{3,4},{4,3},{5,6},{6,5},{7,15},{8,0},{9,10},{10,... | collective-permute-start | bytes 98312 | tf_op jit(solution)/shard_map/ppermute | solution.py:178
  19.4 3.2 %collective-permute-start.5 = (f32[64,128]{1,0:T(8,128)S(1)}, f32[64,128]{1,0:T(8,128)S(1)}, u32[]{:S(2)}, u32[]{:S(2)}) collective-permute-start(f32[64,128]{1,0:T(8,128)S(1)} %get-tuple-element.9.own_ref), channel_id=1, source_target_pairs={{0,1},{1,0},{2,3},{3,2},{4,5},{5,4},{6,7},{7,6},{8,9},{9,8},{10,11... | collective-permute-start | bytes 98312 | tf_op jit(solution)/shard_map/ppermute | solution.py:177

commit v4 on v2

--- a/solution.py
+++ b/solution.py
@@ -10,44 +10,62 @@
 
 NSTEP = 4
 VMEM = pl.BlockSpec(memory_space=pltpu.VMEM)
-SMEM = pl.BlockSpec(memory_space=pltpu.SMEM)
+ANY = pl.BlockSpec(memory_space=pl.ANY)
 
 
 def in_vmem(x):
     return pltpu.with_memory_space_constraint(x, pltpu.VMEM)
 
 
-def pack_kernel(doms, rows, groups, rate_ref, count_ref, pert_ref, out_ref, rates_ref):
-    shape = rates_ref.shape[1:]
-    level_of = lax.broadcasted_iota(jnp.int32, shape, 0)
-    rate, count = jnp.zeros(shape, jnp.float32), jnp.zeros(shape, jnp.int32)
-    for l in range(shape[0]):
-        rate = jnp.where(level_of == l, rate_ref[l], rate)
-        count = jnp.where(level_of == l, count_ref[l], count)
-    for step in range(NSTEP):
-        rates_ref[step] = jnp.where(step < count, rate, 0.0)
-    pairs, variables, cells = pert_ref.shape
+def down_rows(x, lons):
+    wide = jnp.broadcast_to(x.astype(jnp.float32), (x.shape[1], x.shape[1]))
+    on = lax.broadcasted_iota(jnp.int32, wide.shape, 0) == lax.broadcasted_iota(jnp.int32, wide.shape, 1)
+    return jnp.broadcast_to(jnp.sum(jnp.where(on, wide, 0.0), axis=1, keepdims=True), (x.shape[1], lons))
+
+
+def choice_kernel(rows, lons, out_ref):
+    target = lax.broadcasted_iota(jnp.int32, out_ref.shape, 0)
+    source = lax.broadcasted_iota(jnp.int32, out_ref.shape, 1)
+    chosen = (target // lons == source // (rows * lons)) & (
+        lax.rem(target, lons) == lax.rem(source, lons)
+    )
+    out_ref[...] = chosen.astype(jnp.float32).astype(jnp.bfloat16)
+
+
+def pack_kernel(
+    doms, rows, groups, chosen_ref, pert_ref, rate_ref, count_ref, out_ref, rates_ref, tiles_ref, rate_here, count_here, sems
+):
+    fetches = [
+        pltpu.make_async_copy(rate_ref, rate_here, sems.at[groups]),
+        pltpu.make_async_copy(count_ref, count_here, sems.at[groups + 1]),
+    ]
+    for copy in fetches:
+        copy.start()
+    _, variables, cells = pert_ref.shape
     lons = cells // (doms * rows)
     pert = pert_ref[...].astype(jnp.float32)
     fields = jnp.concatenate([pert[:, v, :] for v in range(variables)], axis=0)
-    row_of = lax.rem(lax.broadcasted_iota(jnp.int32, fields.shape, 1) // lons, rows)
+    row_of = (lax.broadcasted_iota(jnp.int32, fields.shape, 1) // lons) % rows
     spread = jnp.concatenate(
         [jnp.where(row_of == r, fields, 0.0) for r in range(rows)], axis=0
     ).astype(jnp.bfloat16)
-    target = lax.broadcasted_iota(jnp.int32, (doms * lons, cells), 0)
-    source = lax.broadcasted_iota(jnp.int32, (doms * lons, cells), 1)
-    chosen = (target // lons == source // (rows * lons)) & (
-        lax.rem(target, lons) == lax.rem(source, lons)
-    )
     tiles = lax.dot_general(
-        chosen.astype(jnp.float32).astype(jnp.bfloat16),
-        spread,
-        (((1,), (1,)), ((), ())),
-        preferred_element_type=jnp.float32,
-    )
-    tiles = tiles.astype(jnp.bfloat16).reshape(doms, lons, spread.shape[0])
-    for g in range(groups):
-        out_ref[pl.ds(g * doms, doms)] = tiles
+        chosen_ref[...], spread, (((1,), (1,)), ((), ())), preferred_element_type=jnp.float32
+    )
+    tiles_ref[...] = tiles.astype(jnp.bfloat16).reshape(tiles_ref.shape)
+    stores = [
+        pltpu.make_async_copy(tiles_ref, out_ref.at[pl.ds(g * doms, doms)], sems.at[g])
+        for g in range(groups)
+    ]
+    for copy in stores:
+        copy.start()
+    for copy in fetches:
+        copy.wait()
+    rate, count = (down_rows(ref[...], rates_ref.shape[2]) for ref in (rate_here, count_here))
+    for step in range(NSTEP):
+        rates_ref[step] = jnp.where(step < count, rate, 0.0)
+    for copy in stores:
+        copy.wait()
 
 
 def sweeps(extended, rates, low_on, high_on, tile):
@@ -184,23 +202,41 @@
     factor = 1.0 / math.sqrt(members * groups - 1)
     fields = members * levels * variables * tile
     flat = control.reshape(-1, lons)
-    near, far = beside(flat, groups, doms)
+    cells = pert_fcst.shape[-1]
+    chosen = pl.pallas_call(
+        functools.partial(choice_kernel, tile, lons // doms),
+        out_shape=pltpu.VMEM((lons, cells), jnp.bfloat16),
+        out_specs=VMEM,
+        cost_estimate=pl.CostEstimate(flops=10**10, bytes_accessed=0, transcendentals=0),
+    )()
     tiles, rates = pl.pallas_call(
         functools.partial(pack_kernel, doms, tile, groups),
         out_shape=[
-            pltpu.VMEM((groups * doms, lons // doms, fields), jnp.bfloat16),
+            jax.ShapeDtypeStruct((groups * doms, lons // doms, fields), jnp.bfloat16),
             pltpu.VMEM((NSTEP, levels, lons), jnp.float32),
         ],
-        in_specs=[SMEM, SMEM, VMEM],
-        out_specs=[VMEM, VMEM],
-    )(diff_rate, step_counts, in_vmem(pert_fcst.reshape(members * levels, variables, -1)))
-    tiles, near, far = lax.optimization_barrier((tiles, near, far))
+        in_specs=[VMEM, VMEM, ANY, ANY],
+        out_specs=[ANY, VMEM],
+        scratch_shapes=[
+            pltpu.VMEM((doms, lons // doms, fields), jnp.bfloat16),
+            pltpu.VMEM((1, levels), jnp.float32),
+            pltpu.VMEM((1, levels), jnp.int32),
+            pltpu.SemaphoreType.DMA((groups + 2,)),
+        ],
+    )(
+        in_vmem(chosen),
+        in_vmem(pert_fcst.reshape(members * levels, variables, -1)),
+        diff_rate.reshape(1, -1),
+        step_counts.reshape(1, -1),
+    )
+    near, far = beside(flat, groups, doms)
     tiles = lax.all_to_all(tiles, ("grp", "dom"), split_axis=0, concat_axis=0, tiled=True)
     local = pl.pallas_call(
         functools.partial(localize_kernel, members, tile),
         out_shape=pltpu.VMEM(flat.shape, jnp.float32),
         in_specs=[VMEM] * 4,
         out_specs=VMEM,
+        cost_estimate=pl.CostEstimate(flops=10**10, bytes_accessed=0, transcendentals=0),
     )(in_vmem(rates), in_vmem(flat), in_vmem(near), in_vmem(far))
     locals_ = [local] + [
         lax.ppermute(local, "grp", [(i, i ^ j) for i in range(groups)]) for j in range(1, groups)
@@ -208,7 +244,7 @@
     increment, adjoint = pl.pallas_call(
         functools.partial(adjoint_kernel, members, levels, variables, tile, groups, factor),
         out_shape=[
-            jax.ShapeDtypeStruct((levels * variables * tile, lons), jnp.float32),
+            pltpu.VMEM((levels * variables * tile, lons), jnp.float32),
             pltpu.VMEM(flat.shape, jnp.float32),
         ],
         in_specs=[VMEM] * (groups + 3),

time: 25.6 us -> 23.2 us (0.906)
  Pallas kernels: 3.54 us -> 2.34 us
  waiting for transfers between devices: 7.16 us -> 6.51 us
  starting transfers between devices: 13.2 us -> 12.7 us
    ppermute x2, waiting for transfers between devices: 2.91 us -> 2.27 us  [beside(): far = lax.ppermute(x, ('grp', 'dom'), far_pairs(groups, doms))]
    pallas_call x1, Pallas kernels: 1.54 us -> 0.92 us  [small_device(): pl.pallas_call(functools.partial(pack_kernel, doms, tile, groups), out_sh...]
    pallas_call x1, Pallas kernels: 0.73 us -> 0.12 us  [small_device(): pl.pallas_call(functools.partial(adjoint_kernel, members, levels, variabl...]
    all_to_all x1, starting transfers between devices: 5.4 us -> 4.84 us  [small_device(): lax.all_to_all(tiles, ('grp', 'dom'), split_axis=0, concat_axis=0, tiled=...]
    unnamed x8 -> x9, local copies, waits for them, and re-layouts: 0.77 us -> 0.64 us
  transfers between devices with their start and end apart: 8 -> 8, of which waited for: 5 -> 5; matrix products, arithmetic and copies ran while one was open for 0% -> 3% of each run, Pallas kernels for 7% -> 6%
where the time goes in v4:
time: 23.2 us; the launch traced here: 22.9 us
  starting transfers between devices  12.7 us (55%)
  waiting for transfers between devices  6.51 us (28%)
  Pallas kernels  2.34 us (10%)
  between operations  0.73 us (3%)
  local copies, waits for them, and re-layouts  0.64 us (3%)
    all_to_all x1, starting transfers between devices, small_device(): lax.all_to_all(tiles, ('grp', 'dom'), split_axis=0, concat_axis=0, tiled=...  4.84 us
    ppermute x2, starting transfers between devices, beside(): far = lax.ppermute(x, ('grp', 'dom'), far_pairs(groups, doms))  3.89 us
    ppermute x3, waiting for transfers between devices, small_device(): lax.ppermute(local, 'grp', [(i, i ^ j) for i in range(groups)])  3.7 us
    ppermute x3, starting transfers between devices, small_device(): lax.ppermute(local, 'grp', [(i, i ^ j) for i in range(groups)])  3.55 us
    ppermute x2, waiting for transfers between devices, beside(): far = lax.ppermute(x, ('grp', 'dom'), far_pairs(groups, doms))  2.27 us
    pallas_call x1, Pallas kernels, small_device(): pl.pallas_call(functools.partial(gradient_kernel, members, tile), out_sha...  0.94 us
    pallas_call x1, Pallas kernels, small_device(): pl.pallas_call(functools.partial(pack_kernel, doms, tile, groups), out_sh...  0.92 us
    unnamed x9, local copies, waits for them, and re-layouts  0.64 us
  transfers between devices with their start and end apart: 8, of which 5 were waited for; matrix products, arithmetic and copies ran while one was open for 3% of the time, Pallas kernels for 6%

profile of v4, /device:TPU:0, one launch (start us, length us, event | category | flops | bytes accessed | tf_op | source)
XLA Modules:
  0.0 22.9 jit_solution(14599338016005528202)
XLA Ops:
  0.6 0.0 copy-start
  0.6 3.0 %collective-permute-start.1 = (f32[64,128]{1,0:T(8,128)}, f32[64,128]{1,0:T(8,128)S(1)}, u32[]{:S(2)}, u32[]{:S(2)}) collective-permute-start(f32[64,128]{1,0:T(8,128)} %bitcast.12), channel_id=1, source_target_pairs={{0,8},{1,2},{2,1},{3,4},{4,3},{5,6},{6,5},{7,15},{8,0},{9,10},{10,... | collective-permute-start | bytes 98312 | tf_op jit(solution)/shard_map/ppermute | solution.py:194
  3.6 0.2 collective-permute-start
  3.9 0.0 copy-done
  3.9 0.9 %shard_map.78 = (bf16[32,16,128]{2,1,0:T(8,128)(2,1)}, f32[4,8,128]{2,1,0:T(8,128)S(1)}) custom-call(bf16[128,512]{1,0:T(8,128)(2,1)S(1)} %shard_map.77.chosen_ref, bf16[16,2,512]{2,1,0:T(2,128)(2,1)S(1)} %bitcast.9, f32[1,8]{1,0:T(1,128)} %bitcast.17, s32[1,8]{1,0:T(1,128)} %bitcast.18), custom_call_target="tpu_custom_call" | custom-call | tf_op jit(solution)/shard_map/pallas_call | solution.py:212
  4.8 0.0 copy-start.3
  4.8 4.8 %all-to-all-start = ((bf16[32,16,128]{2,1,0:T(8,128)(2,1)}), bf16[32,16,128]{2,1,0:T(8,128)(2,1)S(1)}, u32[]{:S(2)}, u32[]{:S(2)}) async-start(bf16[32,16,128]{2,1,0:T(8,128)(2,1)} %get-tuple-element.6), calls=%async_computation | async-start | bytes 262144 | tf_op jit(solution)/shard_map/all_to_all | solution.py:233
  9.7 0.0 collective-permute-done.1.far_ref
  9.7 0.0 collective-permute-done.near_ref
  9.7 0.0 copy-done.3
  9.7 0.0 copy-start.1
  9.7 0.0 copy-start.2
  9.7 0.3 %shard_map.79.refs_0_ = f32[64,128]{1,0:T(8,128)S(1)} custom-call(f32[4,8,128]{2,1,0:T(8,128)S(1)} %get-tuple-element.7.rates_ref, f32[64,128]{1,0:T(8,128)S(1)} %bitcast.14, f32[64,128]{1,0:T(8,128)S(1)} %collective-permute-done.near_ref, f32[64,128]{1,0:T(8,128)S(1)} %collective-permute-done.1.far_ref), custom_call_target="tpu_custom_call" | custom-call | flops 10000000000 | tf_op jit(solution)/shard_map/pallas_call | solution.py:234
  10.1 2.7 %collective-permute-start.4 = (f32[64,128]{1,0:T(8,128)S(1)}, f32[64,128]{1,0:T(8,128)S(1)}, u32[]{:S(2)}, u32[]{:S(2)}) collective-permute-start(f32[64,128]{1,0:T(8,128)S(1)} %shard_map.79.refs_0_), channel_id=1, source_target_pairs={{0,24},{8,16},{16,8},{24,0},{1,25},{9,17},{17,9},{25,1},{2,26},{10... | collective-permute-start | bytes 98312 | tf_op jit(solution)/shard_map/ppermute | solution.py:242
  12.8 0.6 %collective-permute-start.3 = (f32[64,128]{1,0:T(8,128)S(1)}, f32[64,128]{1,0:T(8,128)S(1)}, u32[]{:S(2)}, u32[]{:S(2)}) collective-permute-start(f32[64,128]{1,0:T(8,128)S(1)} %shard_map.79.refs_0_), channel_id=1, source_target_pairs={{0,16},{8,24},{16,0},{24,8},{1,17},{9,25},{17,1},{25,9},{2,18},{10... | collective-permute-start | bytes 98312 | tf_op jit(solution)/shard_map/ppermute | solution.py:242
  13.4 0.3 %collective-permute-start.2 = (f32[64,128]{1,0:T(8,128)S(1)}, f32[64,128]{1,0:T(8,128)S(1)}, u32[]{:S(2)}, u32[]{:S(2)}) collective-permute-start(f32[64,128]{1,0:T(8,128)S(1)} %shard_map.79.refs_0_), channel_id=1, source_target_pairs={{0,8},{8,0},{16,24},{24,16},{1,9},{9,1},{17,25},{25,17},{2,10},{10... | collective-permute-start | bytes 98312 | tf_op jit(solution)/shard_map/ppermute | solution.py:242
  13.6 1.5 %collective-permute-done.4.refs_3_ = f32[64,128]{1,0:T(8,128)S(1)} collective-permute-done((f32[64,128]{1,0:T(8,128)S(1)}, f32[64,128]{1,0:T(8,128)S(1)}, u32[]{:S(2)}, u32[]{:S(2)}) %collective-permute-start.4) | collective-permute-done | bytes 32800 | tf_op jit(solution)/shard_map/ppermute | solution.py:242
  15.1 1.7 %collective-permute-done.3.refs_2_ = f32[64,128]{1,0:T(8,128)S(1)} collective-permute-done((f32[64,128]{1,0:T(8,128)S(1)}, f32[64,128]{1,0:T(8,128)S(1)}, u32[]{:S(2)}, u32[]{:S(2)}) %collective-permute-start.3) | collective-permute-done | bytes 32800 | tf_op jit(solution)/shard_map/ppermute | solution.py:242
  16.8 0.5 %collective-permute-done.2.refs_1_ = f32[64,128]{1,0:T(8,128)S(1)} collective-permute-done((f32[64,128]{1,0:T(8,128)S(1)}, f32[64,128]{1,0:T(8,128)S(1)}, u32[]{:S(2)}, u32[]{:S(2)}) %collective-permute-start.2) | collective-permute-done | bytes 32800 | tf_op jit(solution)/shard_map/ppermute | solution.py:242
  17.3 0.5 %all-to-all-done.tiles_ref = bf16[32,16,128]{2,1,0:T(8,128)(2,1)S(1)} async-done(((bf16[32,16,128]{2,1,0:T(8,128)(2,1)}), bf16[32,16,128]{2,1,0:T(8,128)(2,1)S(1)}, u32[]{:S(2)}, u32[]{:S(2)}) %all-to-all-start) | async-done | bytes 131104 | tf_op jit(solution)/shard_map/all_to_all | solution.py:233
  17.9 0.0 copy-done.1
  17.9 0.0 copy-done.2
  17.9 0.1 shard_map.80
  18.0 0.9 %collective-permute-start.6 = (f32[64,128]{1,0:T(8,128)S(1)}, f32[64,128]{1,0:T(8,128)S(1)}, u32[]{:S(2)}, u32[]{:S(2)}) collective-permute-start(f32[64,128]{1,0:T(8,128)S(1)} %get-tuple-element.9.own_ref), channel_id=1, source_target_pairs={{0,8},{1,2},{2,1},{3,4},{4,3},{5,6},{6,5},{7,15},{8,0},{9,10},{10,... | collective-permute-start | bytes 98312 | tf_op jit(solution)/shard_map/ppermute | solution.py:194
  18.9 0.2 collective-permute-start.5
  19.1 0.6 %copy.8 = f32[8,2,4,128]{3,2,1,0:T(4,128)} copy(f32[8,2,4,128]{3,2,1,0:T(4,128)S(1)} %bitcast.8) | data formatting | bytes 65536
  19.7 2.3 %collective-permute-done.6.far_ref = f32[64,128]{1,0:T(8,128)S(1)} collective-permute-done((f32[64,128]{1,0:T(8,128)S(1)}, f32[64,128]{1,0:T(8,128)S(1)}, u32[]{:S(2)}, u32[]{:S(2)}) %collective-permute-start.6) | collective-permute-done | bytes 32800 | tf_op jit(solution)/shard_map/ppermute | solution.py:194
  22.0 0.0 collective-permute-done.5.near_ref
  22.0 0.9 %shard_map.81 = f32[64,128]{1,0:T(8,128)} custom-call(f32[4,8,128]{2,1,0:T(8,128)S(1)} %get-tuple-element.7.rates_ref, f32[64,128]{1,0:T(8,128)S(1)} %get-tuple-element.9.own_ref, f32[64,128]{1,0:T(8,128)S(1)} %collective-permute-done.5.near_ref, f32[64,128]{1,0:T(8,128)S(1)} %collective-permute-done.6.far_ref, f32[64,128]{1,0:T(8,128)S(1)} %bitcast.15), custom_call_target="tpu_custom_call" | custom-call | tf_op jit(solution)/shard_map/pallas_call | solution.py:259
  (1 shorter events, 0.0 us)
Async XLA Ops:
  0.6 3.3 %copy-start = (bf16[2,8,2,1,512]{4,2,3,1,0:T(2,128)(2,1)S(1)}, bf16[2,8,2,1,512]{4,2,3,1,0:T(2,128)(2,1)}, u32[]{:S(2)}) copy-start(bf16[2,8,2,1,512]{4,2,3,1,0:T(2,128)(2,1)} %param.6) | copy-start | bytes 98308
  0.6 9.0 %collective-permute-start.1 = (f32[64,128]{1,0:T(8,128)}, f32[64,128]{1,0:T(8,128)S(1)}, u32[]{:S(2)}, u32[]{:S(2)}) collective-permute-start(f32[64,128]{1,0:T(8,128)} %bitcast.12), channel_id=1, source_target_pairs={{0,8},{1,2},{2,1},{3,4},{4,3},{5,6},{6,5},{7,15},{8,0},{9,10},{10,... | collective-permute-start | bytes 98312 | tf_op jit(solution)/shard_map/ppermute | solution.py:194
  3.6 6.1 %collective-permute-start = (f32[64,128]{1,0:T(8,128)}, f32[64,128]{1,0:T(8,128)S(1)}, u32[]{:S(2)}, u32[]{:S(2)}) collective-permute-start(f32[64,128]{1,0:T(8,128)} %bitcast.13), channel_id=1, source_target_pairs={{0,1},{1,0},{2,3},{3,2},{4,5},{5,4},{6,7},{7,6},{8,9},{9,8},{10,11... | collective-permute-start | bytes 98312 | tf_op jit(solution)/shard_map/ppermute | solution.py:193
  4.8 4.9 %copy-start.3 = (f32[2,8,4,128]{3,2,1,0:T(4,128)S(1)}, f32[2,8,4,128]{3,2,1,0:T(4,128)}, u32[]{:S(2)}) copy-start(f32[2,8,4,128]{3,2,1,0:T(4,128)} %param.7) | copy-start | bytes 98308
  4.8 13.0 %all-to-all-start = ((bf16[32,16,128]{2,1,0:T(8,128)(2,1)}), bf16[32,16,128]{2,1,0:T(8,128)(2,1)S(1)}, u32[]{:S(2)}, u32[]{:S(2)}) async-start(bf16[32,16,128]{2,1,0:T(8,128)(2,1)} %get-tuple-element.6), calls=%async_computation | async-start | bytes 262144 | tf_op jit(solution)/shard_map/all_to_all | solution.py:233
  9.7 8.1 %copy-start.1 = (f32[8,2,4,128]{3,2,1,0:T(4,128)S(1)}, f32[8,2,4,128]{3,2,1,0:T(4,128)}, u32[]{:S(2)}) copy-start(f32[8,2,4,128]{3,2,1,0:T(4,128)} %param.9) | copy-start | bytes 98308
  9.7 8.1 %copy-start.2 = (f32[8,2,4,128]{3,2,1,0:T(4,128)S(1)}, f32[8,2,4,128]{3,2,1,0:T(4,128)}, u32[]{:S(2)}) copy-start(f32[8,2,4,128]{3,2,1,0:T(4,128)} %param.8) | copy-start | bytes 98308
  10.1 5.1 %collective-permute-start.4 = (f32[64,128]{1,0:T(8,128)S(1)}, f32[64,128]{1,0:T(8,128)S(1)}, u32[]{:S(2)}, u32[]{:S(2)}) collective-permute-start(f32[64,128]{1,0:T(8,128)S(1)} %shard_map.79.refs_0_), channel_id=1, source_target_pairs={{0,24},{8,16},{16,8},{24,0},{1,25},{9,17},{17,9},{25,1},{2,26},{10... | collective-permute-start | bytes 98312 | tf_op jit(solution)/shard_map/ppermute | solution.py:242
  12.8 4.0 %collective-permute-start.3 = (f32[64,128]{1,0:T(8,128)S(1)}, f32[64,128]{1,0:T(8,128)S(1)}, u32[]{:S(2)}, u32[]{:S(2)}) collective-permute-start(f32[64,128]{1,0:T(8,128)S(1)} %shard_map.79.refs_0_), channel_id=1, source_target_pairs={{0,16},{8,24},{16,0},{24,8},{1,17},{9,25},{17,1},{25,9},{2,18},{10... | collective-permute-start | bytes 98312 | tf_op jit(solution)/shard_map/ppermute | solution.py:242
  13.4 4.0 %collective-permute-start.2 = (f32[64,128]{1,0:T(8,128)S(1)}, f32[64,128]{1,0:T(8,128)S(1)}, u32[]{:S(2)}, u32[]{:S(2)}) collective-permute-start(f32[64,128]{1,0:T(8,128)S(1)} %shard_map.79.refs_0_), channel_id=1, source_target_pairs={{0,8},{8,0},{16,24},{24,16},{1,9},{9,1},{17,25},{25,17},{2,10},{10... | collective-permute-start | bytes 98312 | tf_op jit(solution)/shard_map/ppermute | solution.py:242
  18.0 4.0 %collective-permute-start.6 = (f32[64,128]{1,0:T(8,128)S(1)}, f32[64,128]{1,0:T(8,128)S(1)}, u32[]{:S(2)}, u32[]{:S(2)}) collective-permute-start(f32[64,128]{1,0:T(8,128)S(1)} %get-tuple-element.9.own_ref), channel_id=1, source_target_pairs={{0,8},{1,2},{2,1},{3,4},{4,3},{5,6},{6,5},{7,15},{8,0},{9,10},{10,... | collective-permute-start | bytes 98312 | tf_op jit(solution)/shard_map/ppermute | solution.py:194
  18.9 3.1 %collective-permute-start.5 = (f32[64,128]{1,0:T(8,128)S(1)}, f32[64,128]{1,0:T(8,128)S(1)}, u32[]{:S(2)}, u32[]{:S(2)}) collective-permute-start(f32[64,128]{1,0:T(8,128)S(1)} %get-tuple-element.9.own_ref), channel_id=1, source_target_pairs={{0,1},{1,0},{2,3},{3,2},{4,5},{5,4},{6,7},{7,6},{8,9},{9,8},{10,11... | collective-permute-start | bytes 98312 | tf_op jit(solution)/shard_map/ppermute | solution.py:193

commit v5 on v4

--- a/solution.py
+++ b/solution.py
@@ -49,14 +49,17 @@
     spread = jnp.concatenate(
         [jnp.where(row_of == r, fields, 0.0) for r in range(rows)], axis=0
     ).astype(jnp.bfloat16)
-    tiles = lax.dot_general(
-        chosen_ref[...], spread, (((1,), (1,)), ((), ())), preferred_element_type=jnp.float32
-    )
-    tiles_ref[...] = tiles.astype(jnp.bfloat16).reshape(tiles_ref.shape)
-    stores = [
-        pltpu.make_async_copy(tiles_ref, out_ref.at[pl.ds(g * doms, doms)], sems.at[g])
-        for g in range(groups)
-    ]
+    chosen, pair = chosen_ref[...], chosen_ref.shape[1]
+    for chip in range(doms // 2):
+        both = lax.dot_general(
+            chosen,
+            spread[:, chip * pair : (chip + 1) * pair],
+            (((1,), (1,)), ((), ())),
+            preferred_element_type=jnp.float32,
+        ).astype(jnp.bfloat16)
+        for core in range(2):
+            tiles_ref[core, chip] = both[core * lons : (core + 1) * lons]
+    stores = [pltpu.make_async_copy(tiles_ref, out_ref.at[:, g], sems.at[g]) for g in range(groups)]
     for copy in stores:
         copy.start()
     for copy in fetches:
@@ -69,28 +72,38 @@
 
 
 def sweeps(extended, rates, low_on, high_on, tile):
-    rows = list(extended)
-    lons = rows[0].shape[1]
+    lons = extended[0].shape[1]
+    count = len(extended)
+    powers = [list(extended)] + [[None] * count for _ in range(NSTEP)]
+    for i in range(1, count - 1):
+        deep = min(i, count - 1 - i, NSTEP)
+        row = extended[i]
+        pair = {
+            k: pltpu.roll(row, k, 1) + pltpu.roll(row, lons - k, 1) for k in range(1, deep + 1)
+        }
+        pair[0] = row
+        for n in range(1, deep + 1):
+            total = pair[n]
+            for k in range(1, (n + 1) // 2):
+                total = total + float(math.comb(n, k)) * pair[n - 2 * k]
+            if n % 2 == 0:
+                total = total + float(math.comb(n, n // 2)) * row
+            powers[n][i] = total
     for step in range(NSTEP):
-        new = list(rows)
-        for i in range(step + 1, len(rows) - 1 - step):
-            if i < NSTEP:
-                rate = rates[step] * low_on
-            elif i >= NSTEP + tile:
-                rate = rates[step] * high_on
-            else:
-                rate = rates[step]
-            mid = rows[i]
-            laplace = (
-                rows[i + 1]
-                + rows[i - 1]
-                + pltpu.roll(mid, 1, 1)
-                + pltpu.roll(mid, lons - 1, 1)
-                - 4.0 * mid
-            )
-            new[i] = mid + rate * laplace
-        rows = new
-    return rows[NSTEP : NSTEP + tile]
+        new = [[None] * count for _ in range(NSTEP - step)]
+        for n in range(NSTEP - step):
+            for i in range(step + 1 + n, count - 1 - step - n):
+                if i < NSTEP:
+                    rate = rates[step] * low_on
+                elif i >= NSTEP + tile:
+                    rate = rates[step] * high_on
+                else:
+                    rate = rates[step]
+                mid = powers[n][i]
+                laplace = powers[n][i + 1] + powers[n][i - 1] + powers[n + 1][i] - 4.0 * mid
+                new[n][i] = mid + rate * laplace
+        powers = new
+    return powers[0][NSTEP : NSTEP + tile]
 
 
 def edges():
@@ -124,13 +137,13 @@
     members, levels, variables, tile, groups, factor, tiles_ref, *refs
 ):
     local_refs, (weight_ref, depart_ref, inc_ref, adj_ref) = refs[:groups], refs[groups:]
-    doms = tiles_ref.shape[0] // groups
-    lons = inc_ref.shape[1]
+    chips = tiles_ref.shape[2]
     mine = lax.axis_index("grp")
     sums, first = {}, None
     for j in range(groups):
-        block = tiles_ref[pl.ds(jnp.bitwise_xor(mine, j) * doms, doms)]
-        fields = block.reshape(lons, -1).astype(jnp.float32).T
+        group = jnp.bitwise_xor(mine, j)
+        blocks = [tiles_ref[core, group, chip] for chip in range(chips) for core in range(2)]
+        fields = jnp.concatenate(blocks, axis=0).astype(jnp.float32).T
         if j == 0:
             first = fields
         for r in range(tile):
@@ -189,6 +202,10 @@
     return pairs
 
 
+def core_order(groups, doms):
+    return [[g * doms + d for core in range(2) for g in range(groups) for d in range(core, doms, 2)]]
+
+
 def beside(x, groups, doms):
     near = lax.ppermute(x, "dom", near_pairs(doms))
     far = lax.ppermute(x, ("grp", "dom"), far_pairs(groups, doms))
@@ -205,20 +222,20 @@
     cells = pert_fcst.shape[-1]
     chosen = pl.pallas_call(
         functools.partial(choice_kernel, tile, lons // doms),
-        out_shape=pltpu.VMEM((lons, cells), jnp.bfloat16),
+        out_shape=pltpu.VMEM((2 * lons // doms, 2 * cells // doms), jnp.bfloat16),
         out_specs=VMEM,
         cost_estimate=pl.CostEstimate(flops=10**10, bytes_accessed=0, transcendentals=0),
     )()
     tiles, rates = pl.pallas_call(
         functools.partial(pack_kernel, doms, tile, groups),
         out_shape=[
-            jax.ShapeDtypeStruct((groups * doms, lons // doms, fields), jnp.bfloat16),
+            jax.ShapeDtypeStruct((2, groups, doms // 2, lons // doms, fields), jnp.bfloat16),
             pltpu.VMEM((NSTEP, levels, lons), jnp.float32),
         ],
         in_specs=[VMEM, VMEM, ANY, ANY],
         out_specs=[ANY, VMEM],
         scratch_shapes=[
-            pltpu.VMEM((doms, lons // doms, fields), jnp.bfloat16),
+            pltpu.VMEM((2, doms // 2, lons // doms, fields), jnp.bfloat16),
             pltpu.VMEM((1, levels), jnp.float32),
             pltpu.VMEM((1, levels), jnp.int32),
             pltpu.SemaphoreType.DMA((groups + 2,)),
@@ -230,7 +247,15 @@
         step_counts.reshape(1, -1),
     )
     near, far = beside(flat, groups, doms)
-    tiles = lax.all_to_all(tiles, ("grp", "dom"), split_axis=0, concat_axis=0, tiled=True)
+    received = lax.all_to_all(
+        tiles.reshape(-1, *tiles.shape[3:]),
+        ("grp", "dom"),
+        split_axis=0,
+        concat_axis=0,
+        tiled=True,
+        axis_index_groups=core_order(groups, doms),
+    )
+    tiles = received.reshape(tiles.shape)
     local = pl.pallas_call(
         functools.partial(localize_kernel, members, tile),
         out_shape=pltpu.VMEM(flat.shape, jnp.float32),

time: 23.2 us -> 22.7 us (0.978)
  waiting for transfers between devices: 6.51 us -> 6.1 us
  Pallas kernels: 2.34 us -> 2.08 us
    ppermute x2, starting transfers between devices: 3.89 us -> 4.34 us  [beside(): far = lax.ppermute(x, ('grp', 'dom'), far_pairs(groups, doms))]
    ppermute x2, waiting for transfers between devices: 2.27 us -> 2.02 us  [beside(): far = lax.ppermute(x, ('grp', 'dom'), far_pairs(groups, doms))]
  transfers between devices with their start and end apart: 8 -> 8, of which waited for: 5 -> 5; matrix products, arithmetic and copies ran while one was open for 3% -> 3% of each run, Pallas kernels for 6% -> 5%
where the time goes in v5:
time: 22.7 us; the launch traced here: 22.5 us
  starting transfers between devices  12.9 us (57%)
  waiting for transfers between devices  6.1 us (27%)
  Pallas kernels  2.08 us (9%)
  between operations  0.73 us (3%)
  local copies, waits for them, and re-layouts  0.64 us (3%)
    all_to_all x1, starting transfers between devices, small_device(): lax.all_to_all(tiles.reshape(-1, *tiles.shape[3:]), ('grp', 'dom'), split...  4.84 us
    ppermute x2, starting transfers between devices, beside(): far = lax.ppermute(x, ('grp', 'dom'), far_pairs(groups, doms))  4.34 us
    ppermute x3, waiting for transfers between devices, small_device(): lax.ppermute(local, 'grp', [(i, i ^ j) for i in range(groups)])  3.66 us
    ppermute x3, starting transfers between devices, small_device(): lax.ppermute(local, 'grp', [(i, i ^ j) for i in range(groups)])  3.55 us
    ppermute x2, waiting for transfers between devices, beside(): far = lax.ppermute(x, ('grp', 'dom'), far_pairs(groups, doms))  2.02 us
    pallas_call x1, Pallas kernels, small_device(): pl.pallas_call(functools.partial(pack_kernel, doms, tile, groups), out_sh...  0.9 us
    pallas_call x1, Pallas kernels, small_device(): pl.pallas_call(functools.partial(gradient_kernel, members, tile), out_sha...  0.83 us
    unnamed x9, local copies, waits for them, and re-layouts  0.64 us
  transfers between devices with their start and end apart: 8, of which 5 were waited for; matrix products, arithmetic and copies ran while one was open for 3% of the time, Pallas kernels for 5%

profile of v5, /device:TPU:0, one launch (start us, length us, event | category | flops | bytes accessed | tf_op | source)
XLA Modules:
  0.0 22.5 jit_solution(3208861847763851387)
XLA Ops:
  0.6 0.0 copy-start.2
  0.6 3.0 %collective-permute-start.1 = (f32[64,128]{1,0:T(8,128)}, f32[64,128]{1,0:T(8,128)S(1)}, u32[]{:S(2)}, u32[]{:S(2)}) collective-permute-start(f32[64,128]{1,0:T(8,128)} %bitcast.15), channel_id=1, source_target_pairs={{0,8},{1,2},{2,1},{3,4},{4,3},{5,6},{6,5},{7,15},{8,0},{9,10},{10,... | collective-permute-start | bytes 98312 | tf_op jit(solution)/shard_map/ppermute | solution.py:211
  3.6 0.2 collective-permute-start
  3.9 0.0 copy-done.2
  3.9 0.9 %shard_map.78 = (bf16[2,4,4,16,128]{4,3,2,1,0:T(8,128)(2,1)}, f32[4,8,128]{2,1,0:T(8,128)S(1)}) custom-call(bf16[32,128]{1,0:T(8,128)(2,1)S(1)} %shard_map.77.chosen_ref, bf16[16,2,512]{2,1,0:T(2,128)(2,1)S(1)} %bitcast.14, f32[1,8]{1,0:T(1,128)} %bitcast.21, s32[1,8]{1,0:T(1,128)} %bitcast.22), custom_call_target="tpu_custom_call" | custom-call | tf_op jit(solution)/shard_map/pallas_call | solution.py:229
  4.8 0.0 copy-start.3
  4.8 4.8 %all-to-all-start = ((bf16[32,16,128]{2,1,0:T(8,128)(2,1)}), bf16[32,16,128]{2,1,0:T(8,128)(2,1)S(1)}, u32[]{:S(2)}, u32[]{:S(2)}) async-start(bf16[32,16,128]{2,1,0:T(8,128)(2,1)} %bitcast.19), calls=%async_computation | async-start | bytes 262144 | tf_op jit(solution)/shard_map/all_to_all | solution.py:250
  9.6 0.0 collective-permute-done.1.far_ref
  9.6 0.0 collective-permute-done.near_ref
  9.7 0.0 copy-done.3
  9.7 0.0 copy-start
  9.7 0.0 copy-start.1
  9.7 0.2 shard_map.79.refs_0_
  9.9 2.7 %collective-permute-start.4 = (f32[64,128]{1,0:T(8,128)S(1)}, f32[64,128]{1,0:T(8,128)S(1)}, u32[]{:S(2)}, u32[]{:S(2)}) collective-permute-start(f32[64,128]{1,0:T(8,128)S(1)} %shard_map.79.refs_0_), channel_id=1, source_target_pairs={{0,24},{8,16},{16,8},{24,0},{1,25},{9,17},{17,9},{25,1},{2,26},{10... | collective-permute-start | bytes 98312 | tf_op jit(solution)/shard_map/ppermute | solution.py:267
  12.6 0.6 %collective-permute-start.3 = (f32[64,128]{1,0:T(8,128)S(1)}, f32[64,128]{1,0:T(8,128)S(1)}, u32[]{:S(2)}, u32[]{:S(2)}) collective-permute-start(f32[64,128]{1,0:T(8,128)S(1)} %shard_map.79.refs_0_), channel_id=1, source_target_pairs={{0,16},{8,24},{16,0},{24,8},{1,17},{9,25},{17,1},{25,9},{2,18},{10... | collective-permute-start | bytes 98312 | tf_op jit(solution)/shard_map/ppermute | solution.py:267
  13.2 0.3 %collective-permute-start.2 = (f32[64,128]{1,0:T(8,128)S(1)}, f32[64,128]{1,0:T(8,128)S(1)}, u32[]{:S(2)}, u32[]{:S(2)}) collective-permute-start(f32[64,128]{1,0:T(8,128)S(1)} %shard_map.79.refs_0_), channel_id=1, source_target_pairs={{0,8},{8,0},{16,24},{24,16},{1,9},{9,1},{17,25},{25,17},{2,10},{10... | collective-permute-start | bytes 98312 | tf_op jit(solution)/shard_map/ppermute | solution.py:267
  13.5 1.4 %collective-permute-done.4.refs_3_ = f32[64,128]{1,0:T(8,128)S(1)} collective-permute-done((f32[64,128]{1,0:T(8,128)S(1)}, f32[64,128]{1,0:T(8,128)S(1)}, u32[]{:S(2)}, u32[]{:S(2)}) %collective-permute-start.4) | collective-permute-done | bytes 32800 | tf_op jit(solution)/shard_map/ppermute | solution.py:267
  14.9 1.9 %collective-permute-done.3.refs_2_ = f32[64,128]{1,0:T(8,128)S(1)} collective-permute-done((f32[64,128]{1,0:T(8,128)S(1)}, f32[64,128]{1,0:T(8,128)S(1)}, u32[]{:S(2)}, u32[]{:S(2)}) %collective-permute-start.3) | collective-permute-done | bytes 32800 | tf_op jit(solution)/shard_map/ppermute | solution.py:267
  16.7 0.4 %collective-permute-done.2.refs_1_ = f32[64,128]{1,0:T(8,128)S(1)} collective-permute-done((f32[64,128]{1,0:T(8,128)S(1)}, f32[64,128]{1,0:T(8,128)S(1)}, u32[]{:S(2)}, u32[]{:S(2)}) %collective-permute-start.2) | collective-permute-done | bytes 32800 | tf_op jit(solution)/shard_map/ppermute | solution.py:267
  17.1 0.4 %all-to-all-done = bf16[32,16,128]{2,1,0:T(8,128)(2,1)S(1)} async-done(((bf16[32,16,128]{2,1,0:T(8,128)(2,1)}), bf16[32,16,128]{2,1,0:T(8,128)(2,1)S(1)}, u32[]{:S(2)}, u32[]{:S(2)}) %all-to-all-start) | async-done | bytes 131104 | tf_op jit(solution)/shard_map/all_to_all | solution.py:250
  17.5 0.0 copy-done
  17.5 0.0 copy-done.1
  17.6 0.1 shard_map.80
  17.7 1.3 %collective-permute-start.6 = (f32[64,128]{1,0:T(8,128)S(1)}, f32[64,128]{1,0:T(8,128)S(1)}, u32[]{:S(2)}, u32[]{:S(2)}) collective-permute-start(f32[64,128]{1,0:T(8,128)S(1)} %get-tuple-element.9.own_ref), channel_id=1, source_target_pairs={{0,8},{1,2},{2,1},{3,4},{4,3},{5,6},{6,5},{7,15},{8,0},{9,10},{10,... | collective-permute-start | bytes 98312 | tf_op jit(solution)/shard_map/ppermute | solution.py:211
  19.0 0.0 collective-permute-start.5
  19.0 0.6 %copy.8 = f32[8,2,4,128]{3,2,1,0:T(4,128)} copy(f32[8,2,4,128]{3,2,1,0:T(4,128)S(1)} %bitcast.10) | data formatting | bytes 65536
  19.6 2.0 %collective-permute-done.6.far_ref = f32[64,128]{1,0:T(8,128)S(1)} collective-permute-done((f32[64,128]{1,0:T(8,128)S(1)}, f32[64,128]{1,0:T(8,128)S(1)}, u32[]{:S(2)}, u32[]{:S(2)}) %collective-permute-start.6) | collective-permute-done | bytes 32800 | tf_op jit(solution)/shard_map/ppermute | solution.py:211
  21.6 0.0 collective-permute-done.5.near_ref
  21.7 0.8 %shard_map.81 = f32[64,128]{1,0:T(8,128)} custom-call(f32[4,8,128]{2,1,0:T(8,128)S(1)} %get-tuple-element.7.rates_ref, f32[64,128]{1,0:T(8,128)S(1)} %get-tuple-element.9.own_ref, f32[64,128]{1,0:T(8,128)S(1)} %collective-permute-done.5.near_ref, f32[64,128]{1,0:T(8,128)S(1)} %collective-permute-done.6.far_ref, f32[64,128]{1,0:T(8,128)S(1)} %bitcast.18), custom_call_target="tpu_custom_call" | custom-call | tf_op jit(solution)/shard_map/pallas_call | solution.py:284
  (1 shorter events, 0.0 us)
Async XLA Ops:
  0.6 3.2 %copy-start.2 = (bf16[2,8,2,1,512]{4,2,3,1,0:T(2,128)(2,1)S(1)}, bf16[2,8,2,1,512]{4,2,3,1,0:T(2,128)(2,1)}, u32[]{:S(2)}) copy-start(bf16[2,8,2,1,512]{4,2,3,1,0:T(2,128)(2,1)} %param.6) | copy-start | bytes 98308
  0.6 9.0 %collective-permute-start.1 = (f32[64,128]{1,0:T(8,128)}, f32[64,128]{1,0:T(8,128)S(1)}, u32[]{:S(2)}, u32[]{:S(2)}) collective-permute-start(f32[64,128]{1,0:T(8,128)} %bitcast.15), channel_id=1, source_target_pairs={{0,8},{1,2},{2,1},{3,4},{4,3},{5,6},{6,5},{7,15},{8,0},{9,10},{10,... | collective-permute-start | bytes 98312 | tf_op jit(solution)/shard_map/ppermute | solution.py:211
  3.6 6.0 %collective-permute-start = (f32[64,128]{1,0:T(8,128)}, f32[64,128]{1,0:T(8,128)S(1)}, u32[]{:S(2)}, u32[]{:S(2)}) collective-permute-start(f32[64,128]{1,0:T(8,128)} %bitcast.16), channel_id=1, source_target_pairs={{0,1},{1,0},{2,3},{3,2},{4,5},{5,4},{6,7},{7,6},{8,9},{9,8},{10,11... | collective-permute-start | bytes 98312 | tf_op jit(solution)/shard_map/ppermute | solution.py:210
  4.8 4.9 %copy-start.3 = (f32[2,8,4,128]{3,2,1,0:T(4,128)S(1)}, f32[2,8,4,128]{3,2,1,0:T(4,128)}, u32[]{:S(2)}) copy-start(f32[2,8,4,128]{3,2,1,0:T(4,128)} %param.7) | copy-start | bytes 98308
  4.8 12.8 %all-to-all-start = ((bf16[32,16,128]{2,1,0:T(8,128)(2,1)}), bf16[32,16,128]{2,1,0:T(8,128)(2,1)S(1)}, u32[]{:S(2)}, u32[]{:S(2)}) async-start(bf16[32,16,128]{2,1,0:T(8,128)(2,1)} %bitcast.19), calls=%async_computation | async-start | bytes 262144 | tf_op jit(solution)/shard_map/all_to_all | solution.py:250
  9.7 7.9 %copy-start = (f32[8,2,4,128]{3,2,1,0:T(4,128)S(1)}, f32[8,2,4,128]{3,2,1,0:T(4,128)}, u32[]{:S(2)}) copy-start(f32[8,2,4,128]{3,2,1,0:T(4,128)} %param.9) | copy-start | bytes 98308
  9.7 7.9 %copy-start.1 = (f32[8,2,4,128]{3,2,1,0:T(4,128)S(1)}, f32[8,2,4,128]{3,2,1,0:T(4,128)}, u32[]{:S(2)}) copy-start(f32[8,2,4,128]{3,2,1,0:T(4,128)} %param.8) | copy-start | bytes 98308
  9.9 5.0 %collective-permute-start.4 = (f32[64,128]{1,0:T(8,128)S(1)}, f32[64,128]{1,0:T(8,128)S(1)}, u32[]{:S(2)}, u32[]{:S(2)}) collective-permute-start(f32[64,128]{1,0:T(8,128)S(1)} %shard_map.79.refs_0_), channel_id=1, source_target_pairs={{0,24},{8,16},{16,8},{24,0},{1,25},{9,17},{17,9},{25,1},{2,26},{10... | collective-permute-start | bytes 98312 | tf_op jit(solution)/shard_map/ppermute | solution.py:267
  12.6 4.1 %collective-permute-start.3 = (f32[64,128]{1,0:T(8,128)S(1)}, f32[64,128]{1,0:T(8,128)S(1)}, u32[]{:S(2)}, u32[]{:S(2)}) collective-permute-start(f32[64,128]{1,0:T(8,128)S(1)} %shard_map.79.refs_0_), channel_id=1, source_target_pairs={{0,16},{8,24},{16,0},{24,8},{1,17},{9,25},{17,1},{25,9},{2,18},{10... | collective-permute-start | bytes 98312 | tf_op jit(solution)/shard_map/ppermute | solution.py:267
  13.2 3.9 %collective-permute-start.2 = (f32[64,128]{1,0:T(8,128)S(1)}, f32[64,128]{1,0:T(8,128)S(1)}, u32[]{:S(2)}, u32[]{:S(2)}) collective-permute-start(f32[64,128]{1,0:T(8,128)S(1)} %shard_map.79.refs_0_), channel_id=1, source_target_pairs={{0,8},{8,0},{16,24},{24,16},{1,9},{9,1},{17,25},{25,17},{2,10},{10... | collective-permute-start | bytes 98312 | tf_op jit(solution)/shard_map/ppermute | solution.py:267
  17.7 4.0 %collective-permute-start.6 = (f32[64,128]{1,0:T(8,128)S(1)}, f32[64,128]{1,0:T(8,128)S(1)}, u32[]{:S(2)}, u32[]{:S(2)}) collective-permute-start(f32[64,128]{1,0:T(8,128)S(1)} %get-tuple-element.9.own_ref), channel_id=1, source_target_pairs={{0,8},{1,2},{2,1},{3,4},{4,3},{5,6},{6,5},{7,15},{8,0},{9,10},{10,... | collective-permute-start | bytes 98312 | tf_op jit(solution)/shard_map/ppermute | solution.py:211
  19.0 2.6 %collective-permute-start.5 = (f32[64,128]{1,0:T(8,128)S(1)}, f32[64,128]{1,0:T(8,128)S(1)}, u32[]{:S(2)}, u32[]{:S(2)}) collective-permute-start(f32[64,128]{1,0:T(8,128)S(1)} %get-tuple-element.9.own_ref), channel_id=1, source_target_pairs={{0,1},{1,0},{2,3},{3,2},{4,5},{5,4},{6,7},{7,6},{8,9},{9,8},{10,11... | collective-permute-start | bytes 98312 | tf_op jit(solution)/shard_map/ppermute | solution.py:210

commit v6 on v5

--- a/solution.py
+++ b/solution.py
@@ -136,7 +136,7 @@
 def adjoint_kernel(
     members, levels, variables, tile, groups, factor, tiles_ref, *refs
 ):
-    local_refs, (weight_ref, depart_ref, inc_ref, adj_ref) = refs[:groups], refs[groups:]
+    local_refs, (weight_ref, depart_ref, inc_ref, adj_ref, far_ref) = refs[:groups], refs[groups:]
     chips = tiles_ref.shape[2]
     mine = lax.axis_index("grp")
     sums, first = {}, None
@@ -169,9 +169,11 @@
                 term = first[at : at + levels] * residual[v]
                 total = term if total is None else total + term
             adj_ref[pl.ds((m * tile + r) * levels, levels), :] = total * factor
-
-
-def gradient_kernel(members, tile, rates_ref, own_ref, near_ref, far_ref, control_ref, out_ref):
+            far_ref[pl.ds((m * tile + r) * levels, levels), :] = total * factor
+    far_ref[pl.ds(members * tile * levels, levels), :] = jnp.zeros((levels, inc_ref.shape[1]), jnp.float32)
+
+
+def gradient_rows(members, tile, rates_ref, own_ref, near_ref, far_ref, control_ref, out_ref):
     levels = rates_ref.shape[1]
     odd, low, high = edges()
     low_on, high_on = low.astype(jnp.float32), high.astype(jnp.float32)
@@ -179,12 +181,38 @@
     for m in range(members):
         own, near, far = (
             [ref[pl.ds((m * tile + r) * levels, levels), :] for r in range(tile)]
-            for ref in (own_ref, near_ref, far_ref)
+            for ref in (own_ref, near_ref, near_ref if far_ref is None else far_ref)
         )
         done = sweeps(with_halo(own, near, far, odd, low, high), rates, low_on, high_on, tile)
         for r in range(tile):
             rows = pl.ds(m * levels * tile + r, levels, stride=tile)
             out_ref[rows, :] = control_ref[rows, :] + done[r]
+
+
+def end_kernel(members, tile, rates_ref, own_ref, near_ref, control_ref, out_ref, rows_ref, sem):
+    _, low, high = edges()
+
+    @pl.when(jnp.logical_not(low & high))
+    def _():
+        gradient_rows(members, tile, rates_ref, own_ref, near_ref, None, control_ref, rows_ref)
+        copy = pltpu.make_async_copy(rows_ref, out_ref, sem)
+        copy.start()
+        copy.wait()
+
+
+def inner_kernel(
+    members, tile, rates_ref, own_ref, near_ref, far_ref, control_ref, _, out_ref, rows_ref, sem
+):
+    _, low, high = edges()
+
+    @pl.when(low & high)
+    def _():
+        gradient_rows(
+            members, tile, rates_ref, own_ref, near_ref, far_ref, control_ref, rows_ref
+        )
+        copy = pltpu.make_async_copy(rows_ref, out_ref, sem)
+        copy.start()
+        copy.wait()
 
 
 def near_pairs(doms):
@@ -266,27 +294,39 @@
     locals_ = [local] + [
         lax.ppermute(local, "grp", [(i, i ^ j) for i in range(groups)]) for j in range(1, groups)
     ]
-    increment, adjoint = pl.pallas_call(
+    increment, adjoint, for_far = pl.pallas_call(
         functools.partial(adjoint_kernel, members, levels, variables, tile, groups, factor),
         out_shape=[
             pltpu.VMEM((levels * variables * tile, lons), jnp.float32),
             pltpu.VMEM(flat.shape, jnp.float32),
+            pltpu.VMEM((flat.shape[0] + levels, lons), jnp.float32),
         ],
         in_specs=[VMEM] * (groups + 3),
-        out_specs=[VMEM, VMEM],
+        out_specs=[VMEM, VMEM, VMEM],
     )(
         in_vmem(tiles),
         *[in_vmem(x) for x in locals_],
         in_vmem(obs_weight.reshape(-1, lons)),
         in_vmem(departures.reshape(-1, lons)),
     )
-    near, far = beside(adjoint, groups, doms)
+    near = lax.ppermute(adjoint, "dom", near_pairs(doms))
+    far = lax.ppermute(for_far, ("grp", "dom"), far_pairs(groups, doms))
+    at_ends = pl.pallas_call(
+        functools.partial(end_kernel, members, tile),
+        out_shape=jax.ShapeDtypeStruct(flat.shape, jnp.float32),
+        in_specs=[VMEM] * 4,
+        out_specs=ANY,
+        scratch_shapes=[pltpu.VMEM(flat.shape, jnp.float32), pltpu.SemaphoreType.DMA],
+        cost_estimate=pl.CostEstimate(flops=0, bytes_accessed=0, transcendentals=0),
+    )(in_vmem(rates), in_vmem(adjoint), in_vmem(near), in_vmem(flat))
     gradient = pl.pallas_call(
-        functools.partial(gradient_kernel, members, tile),
+        functools.partial(inner_kernel, members, tile),
         out_shape=jax.ShapeDtypeStruct(flat.shape, jnp.float32),
-        in_specs=[VMEM] * 5,
-        out_specs=VMEM,
-    )(in_vmem(rates), in_vmem(adjoint), in_vmem(near), in_vmem(far), in_vmem(flat))
+        in_specs=[VMEM] * 5 + [ANY],
+        out_specs=ANY,
+        scratch_shapes=[pltpu.VMEM(flat.shape, jnp.float32), pltpu.SemaphoreType.DMA],
+        input_output_aliases={5: 0},
+    )(in_vmem(rates), in_vmem(adjoint), in_vmem(near), in_vmem(far), in_vmem(flat), at_ends)
     return increment.reshape(departures.shape), gradient.reshape(control.shape)
 
 

time: 22.7 us -> 22 us (0.969)
  waiting for transfers between devices: 6.1 us -> 5.3 us
    ppermute x2 -> x1, waiting for transfers between devices: 2.02 us -> 0.01 us  [beside(): far = lax.ppermute(x, ('grp', 'dom'), far_pairs(groups, doms))]
    ppermute x0 -> x2, starting transfers between devices: none -> 1.34 us  [the longest x1 1.34 us: small_device(): far = lax.ppermute(for_far, ('grp', 'dom'), far_pairs(groups, doms))]
    ppermute x2 -> x1, starting transfers between devices: 4.34 us -> 3 us  [beside(): far = lax.ppermute(x, ('grp', 'dom'), far_pairs(groups, doms))]
    ppermute x0 -> x2, waiting for transfers between devices: none -> 1.22 us  [the longest x1 0.63 us: small_device(): far = lax.ppermute(for_far, ('grp', 'dom'), far_pairs(groups, doms))]
    pallas_call x1 -> x2, Pallas kernels: 0.83 us -> 0.84 us  [the longest x1 0.83 us: small_device(): pl.pallas_call(functools.partial(end_kernel, members, tile), out_shape=ja...]
  transfers between devices with their start and end apart: 8 -> 8, of which waited for: 5 -> 6; matrix products, arithmetic and copies ran while one was open for 3% -> 3% of each run, Pallas kernels for 5% -> 9%
where the time goes in v6:
time: 22 us; the launch traced here: 21.7 us
  starting transfers between devices  12.9 us (59%)
  waiting for transfers between devices  5.3 us (24%)
  Pallas kernels  2.09 us (10%)
  between operations  0.73 us (3%)
  local copies, waits for them, and re-layouts  0.64 us (3%)
    all_to_all x1, starting transfers between devices, small_device(): lax.all_to_all(tiles.reshape(-1, *tiles.shape[3:]), ('grp', 'dom'), split...  4.84 us
    ppermute x3, waiting for transfers between devices, small_device(): lax.ppermute(local, 'grp', [(i, i ^ j) for i in range(groups)])  3.66 us
    ppermute x3, starting transfers between devices, small_device(): lax.ppermute(local, 'grp', [(i, i ^ j) for i in range(groups)])  3.55 us
    ppermute x1, starting transfers between devices, beside(): far = lax.ppermute(x, ('grp', 'dom'), far_pairs(groups, doms))  3 us
    ppermute x1, starting transfers between devices, small_device(): far = lax.ppermute(for_far, ('grp', 'dom'), far_pairs(groups, doms))  1.34 us
    pallas_call x1, Pallas kernels, small_device(): pl.pallas_call(functools.partial(pack_kernel, doms, tile, groups), out_sh...  0.9 us
    pallas_call x1, Pallas kernels, small_device(): pl.pallas_call(functools.partial(end_kernel, members, tile), out_shape=ja...  0.83 us
    unnamed x9, local copies, waits for them, and re-layouts  0.64 us
  transfers between devices with their start and end apart: 8, of which 6 were waited for; matrix products, arithmetic and copies ran while one was open for 3% of the time, Pallas kernels for 9%

profile of v6, /device:TPU:0, one launch (start us, length us, event | category | flops | bytes accessed | tf_op | source)
XLA Modules:
  0.0 21.7 jit_solution(15637312584226179954)
XLA Ops:
  0.6 0.0 copy-start.3
  0.6 3.0 %collective-permute-start.1 = (f32[64,128]{1,0:T(8,128)}, f32[64,128]{1,0:T(8,128)S(1)}, u32[]{:S(2)}, u32[]{:S(2)}) collective-permute-start(f32[64,128]{1,0:T(8,128)} %bitcast.12), channel_id=1, source_target_pairs={{0,8},{1,2},{2,1},{3,4},{4,3},{5,6},{6,5},{7,15},{8,0},{9,10},{10,... | collective-permute-start | bytes 98312 | tf_op jit(solution)/shard_map/ppermute | solution.py:239
  3.6 0.2 collective-permute-start
  3.9 0.0 copy-done.3
  3.9 0.9 %shard_map.78 = (bf16[2,4,4,16,128]{4,3,2,1,0:T(8,128)(2,1)}, f32[4,8,128]{2,1,0:T(8,128)S(1)}) custom-call(bf16[32,128]{1,0:T(8,128)(2,1)S(1)} %shard_map.77.chosen_ref, bf16[16,2,512]{2,1,0:T(2,128)(2,1)S(1)} %bitcast.19, f32[1,8]{1,0:T(1,128)} %bitcast.22, s32[1,8]{1,0:T(1,128)} %bitcast.23), custom_call_target="tpu_custom_call" | custom-call | tf_op jit(solution)/shard_map/pallas_call | solution.py:257
  4.8 0.0 copy-start
  4.8 4.8 %all-to-all-start = ((bf16[32,16,128]{2,1,0:T(8,128)(2,1)}), bf16[32,16,128]{2,1,0:T(8,128)(2,1)S(1)}, u32[]{:S(2)}, u32[]{:S(2)}) async-start(bf16[32,16,128]{2,1,0:T(8,128)(2,1)} %bitcast.20), calls=%async_computation | async-start | bytes 262144 | tf_op jit(solution)/shard_map/all_to_all | solution.py:278
  9.6 0.0 collective-permute-done.1.far_ref
  9.6 0.0 collective-permute-done.near_ref
  9.7 0.0 copy-done
  9.7 0.0 copy-start.1
  9.7 0.0 copy-start.2
  9.7 0.2 %shard_map.79.refs_0_ = f32[64,128]{1,0:T(8,128)S(1)} custom-call(f32[4,8,128]{2,1,0:T(8,128)S(1)} %get-tuple-element.8.rates_ref, f32[64,128]{1,0:T(8,128)S(1)} %bitcast.14, f32[64,128]{1,0:T(8,128)S(1)} %collective-permute-done.near_ref, f32[64,128]{1,0:T(8,128)S(1)} %collective-permute-done.1.far_ref), custom_call_target="tpu_custom_call" | custom-call | flops 10000000000 | tf_op jit(solution)/shard_map/pallas_call | solution.py:287
  9.9 2.7 %collective-permute-start.4 = (f32[64,128]{1,0:T(8,128)S(1)}, f32[64,128]{1,0:T(8,128)S(1)}, u32[]{:S(2)}, u32[]{:S(2)}) collective-permute-start(f32[64,128]{1,0:T(8,128)S(1)} %shard_map.79.refs_0_), channel_id=1, source_target_pairs={{0,24},{8,16},{16,8},{24,0},{1,25},{9,17},{17,9},{25,1},{2,26},{10... | collective-permute-start | bytes 98312 | tf_op jit(solution)/shard_map/ppermute | solution.py:295
  12.6 0.6 %collective-permute-start.3 = (f32[64,128]{1,0:T(8,128)S(1)}, f32[64,128]{1,0:T(8,128)S(1)}, u32[]{:S(2)}, u32[]{:S(2)}) collective-permute-start(f32[64,128]{1,0:T(8,128)S(1)} %shard_map.79.refs_0_), channel_id=1, source_target_pairs={{0,16},{8,24},{16,0},{24,8},{1,17},{9,25},{17,1},{25,9},{2,18},{10... | collective-permute-start | bytes 98312 | tf_op jit(solution)/shard_map/ppermute | solution.py:295
  13.2 0.3 %collective-permute-start.2 = (f32[64,128]{1,0:T(8,128)S(1)}, f32[64,128]{1,0:T(8,128)S(1)}, u32[]{:S(2)}, u32[]{:S(2)}) collective-permute-start(f32[64,128]{1,0:T(8,128)S(1)} %shard_map.79.refs_0_), channel_id=1, source_target_pairs={{0,8},{8,0},{16,24},{24,16},{1,9},{9,1},{17,25},{25,17},{2,10},{10... | collective-permute-start | bytes 98312 | tf_op jit(solution)/shard_map/ppermute | solution.py:295
  13.5 1.4 %collective-permute-done.4.refs_3_ = f32[64,128]{1,0:T(8,128)S(1)} collective-permute-done((f32[64,128]{1,0:T(8,128)S(1)}, f32[64,128]{1,0:T(8,128)S(1)}, u32[]{:S(2)}, u32[]{:S(2)}) %collective-permute-start.4) | collective-permute-done | bytes 32800 | tf_op jit(solution)/shard_map/ppermute | solution.py:295
  14.9 1.9 %collective-permute-done.3.refs_2_ = f32[64,128]{1,0:T(8,128)S(1)} collective-permute-done((f32[64,128]{1,0:T(8,128)S(1)}, f32[64,128]{1,0:T(8,128)S(1)}, u32[]{:S(2)}, u32[]{:S(2)}) %collective-permute-start.3) | collective-permute-done | bytes 32800 | tf_op jit(solution)/shard_map/ppermute | solution.py:295
  16.7 0.4 %collective-permute-done.2.refs_1_ = f32[64,128]{1,0:T(8,128)S(1)} collective-permute-done((f32[64,128]{1,0:T(8,128)S(1)}, f32[64,128]{1,0:T(8,128)S(1)}, u32[]{:S(2)}, u32[]{:S(2)}) %collective-permute-start.2) | collective-permute-done | bytes 32800 | tf_op jit(solution)/shard_map/ppermute | solution.py:295
  17.1 0.4 %all-to-all-done = bf16[32,16,128]{2,1,0:T(8,128)(2,1)S(1)} async-done(((bf16[32,16,128]{2,1,0:T(8,128)(2,1)}), bf16[32,16,128]{2,1,0:T(8,128)(2,1)S(1)}, u32[]{:S(2)}, u32[]{:S(2)}) %all-to-all-start) | async-done | bytes 131104 | tf_op jit(solution)/shard_map/all_to_all | solution.py:278
  17.5 0.0 copy-done.1
  17.5 0.0 copy-done.2
  17.6 0.1 shard_map.80
  17.7 1.3 %collective-permute-start.6 = (f32[72,128]{1,0:T(8,128)S(1)}, f32[72,128]{1,0:T(8,128)S(1)}, u32[]{:S(2)}, u32[]{:S(2)}) collective-permute-start(f32[72,128]{1,0:T(8,128)S(1)} %get-tuple-element.11), channel_id=1, source_target_pairs={{0,8},{1,2},{2,1},{3,4},{4,3},{5,6},{6,5},{7,15},{8,0},{9,10},{10,... | collective-permute-start | bytes 110600 | tf_op jit(solution)/shard_map/ppermute | solution.py:313
  19.0 0.0 collective-permute-start.5
  19.0 0.6 %copy.10 = f32[8,2,4,128]{3,2,1,0:T(4,128)} copy(f32[8,2,4,128]{3,2,1,0:T(4,128)S(1)} %bitcast.10) | data formatting | bytes 65536
  19.6 0.6 %collective-permute-done.5.near_ref = f32[64,128]{1,0:T(8,128)S(1)} collective-permute-done((f32[64,128]{1,0:T(8,128)S(1)}, f32[64,128]{1,0:T(8,128)S(1)}, u32[]{:S(2)}, u32[]{:S(2)}) %collective-permute-start.5) | collective-permute-done | bytes 32800 | tf_op jit(solution)/shard_map/ppermute | solution.py:312
  20.2 0.8 %shard_map.81._ = f32[64,128]{1,0:T(8,128)} custom-call(f32[4,8,128]{2,1,0:T(8,128)S(1)} %get-tuple-element.8.rates_ref, f32[64,128]{1,0:T(8,128)S(1)} %get-tuple-element.10.own_ref, f32[64,128]{1,0:T(8,128)S(1)} %collective-permute-done.5.near_ref, f32[64,128]{1,0:T(8,128)S(1)} %bitcast.15), custom_call_target="tpu_custom_call" | custom-call | tf_op jit(solution)/shard_map/pallas_call | solution.py:314
  21.1 0.6 %collective-permute-done.6.far_ref = f32[72,128]{1,0:T(8,128)S(1)} collective-permute-done((f32[72,128]{1,0:T(8,128)S(1)}, f32[72,128]{1,0:T(8,128)S(1)}, u32[]{:S(2)}, u32[]{:S(2)}) %collective-permute-start.6) | collective-permute-done | bytes 36896 | tf_op jit(solution)/shard_map/ppermute | solution.py:313
  (2 shorter events, 0.0 us)
Async XLA Ops:
  0.6 3.2 %copy-start.3 = (bf16[2,8,2,1,512]{4,2,3,1,0:T(2,128)(2,1)S(1)}, bf16[2,8,2,1,512]{4,2,3,1,0:T(2,128)(2,1)}, u32[]{:S(2)}) copy-start(bf16[2,8,2,1,512]{4,2,3,1,0:T(2,128)(2,1)} %param.6) | copy-start | bytes 98308
  0.6 9.0 %collective-permute-start.1 = (f32[64,128]{1,0:T(8,128)}, f32[64,128]{1,0:T(8,128)S(1)}, u32[]{:S(2)}, u32[]{:S(2)}) collective-permute-start(f32[64,128]{1,0:T(8,128)} %bitcast.12), channel_id=1, source_target_pairs={{0,8},{1,2},{2,1},{3,4},{4,3},{5,6},{6,5},{7,15},{8,0},{9,10},{10,... | collective-permute-start | bytes 98312 | tf_op jit(solution)/shard_map/ppermute | solution.py:239
  3.6 6.0 %collective-permute-start = (f32[64,128]{1,0:T(8,128)}, f32[64,128]{1,0:T(8,128)S(1)}, u32[]{:S(2)}, u32[]{:S(2)}) collective-permute-start(f32[64,128]{1,0:T(8,128)} %bitcast.13), channel_id=1, source_target_pairs={{0,1},{1,0},{2,3},{3,2},{4,5},{5,4},{6,7},{7,6},{8,9},{9,8},{10,11... | collective-permute-start | bytes 98312 | tf_op jit(solution)/shard_map/ppermute | solution.py:238
  4.8 4.9 %copy-start = (f32[2,8,4,128]{3,2,1,0:T(4,128)S(1)}, f32[2,8,4,128]{3,2,1,0:T(4,128)}, u32[]{:S(2)}) copy-start(f32[2,8,4,128]{3,2,1,0:T(4,128)} %param.7) | copy-start | bytes 98308
  4.8 12.8 %all-to-all-start = ((bf16[32,16,128]{2,1,0:T(8,128)(2,1)}), bf16[32,16,128]{2,1,0:T(8,128)(2,1)S(1)}, u32[]{:S(2)}, u32[]{:S(2)}) async-start(bf16[32,16,128]{2,1,0:T(8,128)(2,1)} %bitcast.20), calls=%async_computation | async-start | bytes 262144 | tf_op jit(solution)/shard_map/all_to_all | solution.py:278
  9.7 7.9 %copy-start.1 = (f32[8,2,4,128]{3,2,1,0:T(4,128)S(1)}, f32[8,2,4,128]{3,2,1,0:T(4,128)}, u32[]{:S(2)}) copy-start(f32[8,2,4,128]{3,2,1,0:T(4,128)} %param.9) | copy-start | bytes 98308
  9.7 7.9 %copy-start.2 = (f32[8,2,4,128]{3,2,1,0:T(4,128)S(1)}, f32[8,2,4,128]{3,2,1,0:T(4,128)}, u32[]{:S(2)}) copy-start(f32[8,2,4,128]{3,2,1,0:T(4,128)} %param.8) | copy-start | bytes 98308
  9.9 5.0 %collective-permute-start.4 = (f32[64,128]{1,0:T(8,128)S(1)}, f32[64,128]{1,0:T(8,128)S(1)}, u32[]{:S(2)}, u32[]{:S(2)}) collective-permute-start(f32[64,128]{1,0:T(8,128)S(1)} %shard_map.79.refs_0_), channel_id=1, source_target_pairs={{0,24},{8,16},{16,8},{24,0},{1,25},{9,17},{17,9},{25,1},{2,26},{10... | collective-permute-start | bytes 98312 | tf_op jit(solution)/shard_map/ppermute | solution.py:295
  12.6 4.1 %collective-permute-start.3 = (f32[64,128]{1,0:T(8,128)S(1)}, f32[64,128]{1,0:T(8,128)S(1)}, u32[]{:S(2)}, u32[]{:S(2)}) collective-permute-start(f32[64,128]{1,0:T(8,128)S(1)} %shard_map.79.refs_0_), channel_id=1, source_target_pairs={{0,16},{8,24},{16,0},{24,8},{1,17},{9,25},{17,1},{25,9},{2,18},{10... | collective-permute-start | bytes 98312 | tf_op jit(solution)/shard_map/ppermute | solution.py:295
  13.2 3.9 %collective-permute-start.2 = (f32[64,128]{1,0:T(8,128)S(1)}, f32[64,128]{1,0:T(8,128)S(1)}, u32[]{:S(2)}, u32[]{:S(2)}) collective-permute-start(f32[64,128]{1,0:T(8,128)S(1)} %shard_map.79.refs_0_), channel_id=1, source_target_pairs={{0,8},{8,0},{16,24},{24,16},{1,9},{9,1},{17,25},{25,17},{2,10},{10... | collective-permute-start | bytes 98312 | tf_op jit(solution)/shard_map/ppermute | solution.py:295
  17.7 4.0 %collective-permute-start.6 = (f32[72,128]{1,0:T(8,128)S(1)}, f32[72,128]{1,0:T(8,128)S(1)}, u32[]{:S(2)}, u32[]{:S(2)}) collective-permute-start(f32[72,128]{1,0:T(8,128)S(1)} %get-tuple-element.11), channel_id=1, source_target_pairs={{0,8},{1,2},{2,1},{3,4},{4,3},{5,6},{6,5},{7,15},{8,0},{9,10},{10,... | collective-permute-start | bytes 110600 | tf_op jit(solution)/shard_map/ppermute | solution.py:313
  19.0 1.2 %collective-permute-start.5 = (f32[64,128]{1,0:T(8,128)S(1)}, f32[64,128]{1,0:T(8,128)S(1)}, u32[]{:S(2)}, u32[]{:S(2)}) collective-permute-start(f32[64,128]{1,0:T(8,128)S(1)} %get-tuple-element.10.own_ref), channel_id=1, source_target_pairs={{0,1},{1,0},{2,3},{3,2},{4,5},{5,4},{6,7},{7,6},{8,9},{9,8},{10,11... | collective-permute-start | bytes 98312 | tf_op jit(solution)/shard_map/ppermute | solution.py:312

commit v7 on v6

--- a/solution.py
+++ b/solution.py
@@ -9,6 +9,8 @@
 from jax.sharding import PartitionSpec as P
 
 NSTEP = 4
+CHIPS = (2, 3, 1, 0)
+GROUPS = (3, 0, 1, 2)
 VMEM = pl.BlockSpec(memory_space=pltpu.VMEM)
 ANY = pl.BlockSpec(memory_space=pl.ANY)
 
@@ -58,7 +60,7 @@
             preferred_element_type=jnp.float32,
         ).astype(jnp.bfloat16)
         for core in range(2):
-            tiles_ref[core, chip] = both[core * lons : (core + 1) * lons]
+            tiles_ref[core, CHIPS.index(chip)] = both[core * lons : (core + 1) * lons]
     stores = [pltpu.make_async_copy(tiles_ref, out_ref.at[:, g], sems.at[g]) for g in range(groups)]
     for copy in stores:
         copy.start()
@@ -137,12 +139,17 @@
     members, levels, variables, tile, groups, factor, tiles_ref, *refs
 ):
     local_refs, (weight_ref, depart_ref, inc_ref, adj_ref, far_ref) = refs[:groups], refs[groups:]
-    chips = tiles_ref.shape[2]
     mine = lax.axis_index("grp")
     sums, first = {}, None
     for j in range(groups):
-        group = jnp.bitwise_xor(mine, j)
-        blocks = [tiles_ref[core, group, chip] for chip in range(chips) for core in range(2)]
+        group = sum(
+            jnp.where(jnp.bitwise_xor(mine, j) == g, GROUPS.index(g), 0) for g in range(groups)
+        )
+        blocks = [
+            tiles_ref[core, group, CHIPS.index(chip)]
+            for chip in range(len(CHIPS))
+            for core in range(2)
+        ]
         fields = jnp.concatenate(blocks, axis=0).astype(jnp.float32).T
         if j == 0:
             first = fields
@@ -231,7 +238,14 @@
 
 
 def core_order(groups, doms):
-    return [[g * doms + d for core in range(2) for g in range(groups) for d in range(core, doms, 2)]]
+    return [
+        [
+            g * doms + 2 * chip + core
+            for core in range(2)
+            for g in GROUPS
+            for chip in CHIPS
+        ]
+    ]
 
 
 def beside(x, groups, doms):
@@ -388,9 +402,9 @@
         and levels == 8
         and tile == NSTEP
         and members * levels * variables * tile == 128
-        and doms % 2 == 0
+        and doms == 2 * len(CHIPS)
         and lons // doms == 16
-        and groups == 4
+        and groups == len(GROUPS)
     )
     run = small_device if small else any_device
     return run(pert_fcst, control, departures, obs_weight, diff_rate, step_counts)

time: 22 us -> 21.7 us (0.986)
  waiting for transfers between devices: 5.3 us -> 4.9 us
    all_to_all x1, waiting for transfers between devices: 0.41 us -> 0.17 us  [small_device(): lax.all_to_all(tiles.reshape(-1, *tiles.shape[3:]), ('grp', 'dom'), split...]
where the time goes in v7:
time: 21.7 us; the launch traced here: 21.5 us
  starting transfers between devices  13.1 us (60%)
  waiting for transfers between devices  4.9 us (23%)
  Pallas kernels  2.09 us (10%)
  between operations  0.73 us (3%)
  local copies, waits for them, and re-layouts  0.64 us (3%)
    all_to_all x1, starting transfers between devices, small_device(): lax.all_to_all(tiles.reshape(-1, *tiles.shape[3:]), ('grp', 'dom'), split...  4.84 us
    ppermute x3, waiting for transfers between devices, small_device(): lax.ppermute(local, 'grp', [(i, i ^ j) for i in range(groups)])  3.65 us
    ppermute x3, starting transfers between devices, small_device(): lax.ppermute(local, 'grp', [(i, i ^ j) for i in range(groups)])  3.55 us
    ppermute x1, starting transfers between devices, beside(): far = lax.ppermute(x, ('grp', 'dom'), far_pairs(groups, doms))  3 us
    ppermute x1, starting transfers between devices, small_device(): far = lax.ppermute(for_far, ('grp', 'dom'), far_pairs(groups, doms))  1.28 us
    pallas_call x1, Pallas kernels, small_device(): pl.pallas_call(functools.partial(pack_kernel, doms, tile, groups), out_sh...  0.9 us
    pallas_call x1, Pallas kernels, small_device(): pl.pallas_call(functools.partial(end_kernel, members, tile), out_shape=ja...  0.83 us
    ppermute x1, waiting for transfers between devices, small_device(): far = lax.ppermute(for_far, ('grp', 'dom'), far_pairs(groups, doms))  0.69 us
  transfers between devices with their start and end apart: 8, of which 6 were waited for; matrix products, arithmetic and copies ran while one was open for 3% of the time, Pallas kernels for 9%

profile of v7, /device:TPU:0, one launch (start us, length us, event | category | flops | bytes accessed | tf_op | source)
XLA Modules:
  0.0 21.5 jit_solution(12082208515837127296)
XLA Ops:
  0.6 0.0 copy-start.3
  0.6 3.0 %collective-permute-start.1 = (f32[64,128]{1,0:T(8,128)}, f32[64,128]{1,0:T(8,128)S(1)}, u32[]{:S(2)}, u32[]{:S(2)}) collective-permute-start(f32[64,128]{1,0:T(8,128)} %bitcast.12), channel_id=1, source_target_pairs={{0,8},{1,2},{2,1},{3,4},{4,3},{5,6},{6,5},{7,15},{8,0},{9,10},{10,... | collective-permute-start | bytes 98312 | tf_op jit(solution)/shard_map/ppermute | solution.py:253
  3.6 0.2 collective-permute-start
  3.9 0.0 copy-done.3
  3.9 0.9 %shard_map.78 = (bf16[2,4,4,16,128]{4,3,2,1,0:T(8,128)(2,1)}, f32[4,8,128]{2,1,0:T(8,128)S(1)}) custom-call(bf16[32,128]{1,0:T(8,128)(2,1)S(1)} %shard_map.77.chosen_ref, bf16[16,2,512]{2,1,0:T(2,128)(2,1)S(1)} %bitcast.19, f32[1,8]{1,0:T(1,128)} %bitcast.22, s32[1,8]{1,0:T(1,128)} %bitcast.23), custom_call_target="tpu_custom_call" | custom-call | tf_op jit(solution)/shard_map/pallas_call | solution.py:271
  4.8 0.0 copy-start
  4.8 4.8 %all-to-all-start = ((bf16[32,16,128]{2,1,0:T(8,128)(2,1)}), bf16[32,16,128]{2,1,0:T(8,128)(2,1)S(1)}, u32[]{:S(2)}, u32[]{:S(2)}) async-start(bf16[32,16,128]{2,1,0:T(8,128)(2,1)} %bitcast.20), calls=%async_computation | async-start | bytes 262144 | tf_op jit(solution)/shard_map/all_to_all | solution.py:292
  9.6 0.0 collective-permute-done.1.far_ref
  9.6 0.0 collective-permute-done.near_ref
  9.7 0.0 copy-done
  9.7 0.0 copy-start.1
  9.7 0.0 copy-start.2
  9.7 0.2 %shard_map.79.refs_0_ = f32[64,128]{1,0:T(8,128)S(1)} custom-call(f32[4,8,128]{2,1,0:T(8,128)S(1)} %get-tuple-element.8.rates_ref, f32[64,128]{1,0:T(8,128)S(1)} %bitcast.14, f32[64,128]{1,0:T(8,128)S(1)} %collective-permute-done.near_ref, f32[64,128]{1,0:T(8,128)S(1)} %collective-permute-done.1.far_ref), custom_call_target="tpu_custom_call" | custom-call | flops 10000000000 | tf_op jit(solution)/shard_map/pallas_call | solution.py:301
  9.9 2.7 %collective-permute-start.4 = (f32[64,128]{1,0:T(8,128)S(1)}, f32[64,128]{1,0:T(8,128)S(1)}, u32[]{:S(2)}, u32[]{:S(2)}) collective-permute-start(f32[64,128]{1,0:T(8,128)S(1)} %shard_map.79.refs_0_), channel_id=1, source_target_pairs={{0,24},{8,16},{16,8},{24,0},{1,25},{9,17},{17,9},{25,1},{2,26},{10... | collective-permute-start | bytes 98312 | tf_op jit(solution)/shard_map/ppermute | solution.py:309
  12.6 0.6 %collective-permute-start.3 = (f32[64,128]{1,0:T(8,128)S(1)}, f32[64,128]{1,0:T(8,128)S(1)}, u32[]{:S(2)}, u32[]{:S(2)}) collective-permute-start(f32[64,128]{1,0:T(8,128)S(1)} %shard_map.79.refs_0_), channel_id=1, source_target_pairs={{0,16},{8,24},{16,0},{24,8},{1,17},{9,25},{17,1},{25,9},{2,18},{10... | collective-permute-start | bytes 98312 | tf_op jit(solution)/shard_map/ppermute | solution.py:309
  13.2 0.3 %collective-permute-start.2 = (f32[64,128]{1,0:T(8,128)S(1)}, f32[64,128]{1,0:T(8,128)S(1)}, u32[]{:S(2)}, u32[]{:S(2)}) collective-permute-start(f32[64,128]{1,0:T(8,128)S(1)} %shard_map.79.refs_0_), channel_id=1, source_target_pairs={{0,8},{8,0},{16,24},{24,16},{1,9},{9,1},{17,25},{25,17},{2,10},{10... | collective-permute-start | bytes 98312 | tf_op jit(solution)/shard_map/ppermute | solution.py:309
  13.5 1.5 %collective-permute-done.4.refs_3_ = f32[64,128]{1,0:T(8,128)S(1)} collective-permute-done((f32[64,128]{1,0:T(8,128)S(1)}, f32[64,128]{1,0:T(8,128)S(1)}, u32[]{:S(2)}, u32[]{:S(2)}) %collective-permute-start.4) | collective-permute-done | bytes 32800 | tf_op jit(solution)/shard_map/ppermute | solution.py:309
  15.0 1.7 %collective-permute-done.3.refs_2_ = f32[64,128]{1,0:T(8,128)S(1)} collective-permute-done((f32[64,128]{1,0:T(8,128)S(1)}, f32[64,128]{1,0:T(8,128)S(1)}, u32[]{:S(2)}, u32[]{:S(2)}) %collective-permute-start.3) | collective-permute-done | bytes 32800 | tf_op jit(solution)/shard_map/ppermute | solution.py:309
  16.7 0.4 %collective-permute-done.2.refs_1_ = f32[64,128]{1,0:T(8,128)S(1)} collective-permute-done((f32[64,128]{1,0:T(8,128)S(1)}, f32[64,128]{1,0:T(8,128)S(1)}, u32[]{:S(2)}, u32[]{:S(2)}) %collective-permute-start.2) | collective-permute-done | bytes 32800 | tf_op jit(solution)/shard_map/ppermute | solution.py:309
  17.1 0.2 all-to-all-done
  17.3 0.0 copy-done.1
  17.3 0.0 copy-done.2
  17.3 0.1 shard_map.80
  17.4 1.3 %collective-permute-start.6 = (f32[72,128]{1,0:T(8,128)S(1)}, f32[72,128]{1,0:T(8,128)S(1)}, u32[]{:S(2)}, u32[]{:S(2)}) collective-permute-start(f32[72,128]{1,0:T(8,128)S(1)} %get-tuple-element.11), channel_id=1, source_target_pairs={{0,8},{1,2},{2,1},{3,4},{4,3},{5,6},{6,5},{7,15},{8,0},{9,10},{10,... | collective-permute-start | bytes 110600 | tf_op jit(solution)/shard_map/ppermute | solution.py:327
  18.7 0.2 collective-permute-start.5
  18.9 0.6 %copy.10 = f32[8,2,4,128]{3,2,1,0:T(4,128)} copy(f32[8,2,4,128]{3,2,1,0:T(4,128)S(1)} %bitcast.10) | data formatting | bytes 65536
  19.5 0.4 %collective-permute-done.5.near_ref = f32[64,128]{1,0:T(8,128)S(1)} collective-permute-done((f32[64,128]{1,0:T(8,128)S(1)}, f32[64,128]{1,0:T(8,128)S(1)}, u32[]{:S(2)}, u32[]{:S(2)}) %collective-permute-start.5) | collective-permute-done | bytes 32800 | tf_op jit(solution)/shard_map/ppermute | solution.py:326
  19.9 0.8 %shard_map.81._ = f32[64,128]{1,0:T(8,128)} custom-call(f32[4,8,128]{2,1,0:T(8,128)S(1)} %get-tuple-element.8.rates_ref, f32[64,128]{1,0:T(8,128)S(1)} %get-tuple-element.10.own_ref, f32[64,128]{1,0:T(8,128)S(1)} %collective-permute-done.5.near_ref, f32[64,128]{1,0:T(8,128)S(1)} %bitcast.15), custom_call_target="tpu_custom_call" | custom-call | tf_op jit(solution)/shard_map/pallas_call | solution.py:328
  20.8 0.7 %collective-permute-done.6.far_ref = f32[72,128]{1,0:T(8,128)S(1)} collective-permute-done((f32[72,128]{1,0:T(8,128)S(1)}, f32[72,128]{1,0:T(8,128)S(1)}, u32[]{:S(2)}, u32[]{:S(2)}) %collective-permute-start.6) | collective-permute-done | bytes 36896 | tf_op jit(solution)/shard_map/ppermute | solution.py:327
  (2 shorter events, 0.0 us)
Async XLA Ops:
  0.6 3.2 %copy-start.3 = (bf16[2,8,2,1,512]{4,2,3,1,0:T(2,128)(2,1)S(1)}, bf16[2,8,2,1,512]{4,2,3,1,0:T(2,128)(2,1)}, u32[]{:S(2)}) copy-start(bf16[2,8,2,1,512]{4,2,3,1,0:T(2,128)(2,1)} %param.6) | copy-start | bytes 98308
  0.6 9.0 %collective-permute-start.1 = (f32[64,128]{1,0:T(8,128)}, f32[64,128]{1,0:T(8,128)S(1)}, u32[]{:S(2)}, u32[]{:S(2)}) collective-permute-start(f32[64,128]{1,0:T(8,128)} %bitcast.12), channel_id=1, source_target_pairs={{0,8},{1,2},{2,1},{3,4},{4,3},{5,6},{6,5},{7,15},{8,0},{9,10},{10,... | collective-permute-start | bytes 98312 | tf_op jit(solution)/shard_map/ppermute | solution.py:253
  3.6 6.0 %collective-permute-start = (f32[64,128]{1,0:T(8,128)}, f32[64,128]{1,0:T(8,128)S(1)}, u32[]{:S(2)}, u32[]{:S(2)}) collective-permute-start(f32[64,128]{1,0:T(8,128)} %bitcast.13), channel_id=1, source_target_pairs={{0,1},{1,0},{2,3},{3,2},{4,5},{5,4},{6,7},{7,6},{8,9},{9,8},{10,11... | collective-permute-start | bytes 98312 | tf_op jit(solution)/shard_map/ppermute | solution.py:252
  4.8 4.9 %copy-start = (f32[2,8,4,128]{3,2,1,0:T(4,128)S(1)}, f32[2,8,4,128]{3,2,1,0:T(4,128)}, u32[]{:S(2)}) copy-start(f32[2,8,4,128]{3,2,1,0:T(4,128)} %param.7) | copy-start | bytes 98308
  4.8 12.5 %all-to-all-start = ((bf16[32,16,128]{2,1,0:T(8,128)(2,1)}), bf16[32,16,128]{2,1,0:T(8,128)(2,1)S(1)}, u32[]{:S(2)}, u32[]{:S(2)}) async-start(bf16[32,16,128]{2,1,0:T(8,128)(2,1)} %bitcast.20), calls=%async_computation | async-start | bytes 262144 | tf_op jit(solution)/shard_map/all_to_all | solution.py:292
  9.7 7.6 %copy-start.1 = (f32[8,2,4,128]{3,2,1,0:T(4,128)S(1)}, f32[8,2,4,128]{3,2,1,0:T(4,128)}, u32[]{:S(2)}) copy-start(f32[8,2,4,128]{3,2,1,0:T(4,128)} %param.9) | copy-start | bytes 98308
  9.7 7.6 %copy-start.2 = (f32[8,2,4,128]{3,2,1,0:T(4,128)S(1)}, f32[8,2,4,128]{3,2,1,0:T(4,128)}, u32[]{:S(2)}) copy-start(f32[8,2,4,128]{3,2,1,0:T(4,128)} %param.8) | copy-start | bytes 98308
  9.9 5.1 %collective-permute-start.4 = (f32[64,128]{1,0:T(8,128)S(1)}, f32[64,128]{1,0:T(8,128)S(1)}, u32[]{:S(2)}, u32[]{:S(2)}) collective-permute-start(f32[64,128]{1,0:T(8,128)S(1)} %shard_map.79.refs_0_), channel_id=1, source_target_pairs={{0,24},{8,16},{16,8},{24,0},{1,25},{9,17},{17,9},{25,1},{2,26},{10... | collective-permute-start | bytes 98312 | tf_op jit(solution)/shard_map/ppermute | solution.py:309
  12.6 4.1 %collective-permute-start.3 = (f32[64,128]{1,0:T(8,128)S(1)}, f32[64,128]{1,0:T(8,128)S(1)}, u32[]{:S(2)}, u32[]{:S(2)}) collective-permute-start(f32[64,128]{1,0:T(8,128)S(1)} %shard_map.79.refs_0_), channel_id=1, source_target_pairs={{0,16},{8,24},{16,0},{24,8},{1,17},{9,25},{17,1},{25,9},{2,18},{10... | collective-permute-start | bytes 98312 | tf_op jit(solution)/shard_map/ppermute | solution.py:309
  13.2 3.9 %collective-permute-start.2 = (f32[64,128]{1,0:T(8,128)S(1)}, f32[64,128]{1,0:T(8,128)S(1)}, u32[]{:S(2)}, u32[]{:S(2)}) collective-permute-start(f32[64,128]{1,0:T(8,128)S(1)} %shard_map.79.refs_0_), channel_id=1, source_target_pairs={{0,8},{8,0},{16,24},{24,16},{1,9},{9,1},{17,25},{25,17},{2,10},{10... | collective-permute-start | bytes 98312 | tf_op jit(solution)/shard_map/ppermute | solution.py:309
  17.4 4.0 %collective-permute-start.6 = (f32[72,128]{1,0:T(8,128)S(1)}, f32[72,128]{1,0:T(8,128)S(1)}, u32[]{:S(2)}, u32[]{:S(2)}) collective-permute-start(f32[72,128]{1,0:T(8,128)S(1)} %get-tuple-element.11), channel_id=1, source_target_pairs={{0,8},{1,2},{2,1},{3,4},{4,3},{5,6},{6,5},{7,15},{8,0},{9,10},{10,... | collective-permute-start | bytes 110600 | tf_op jit(solution)/shard_map/ppermute | solution.py:327
  18.7 1.2 %collective-permute-start.5 = (f32[64,128]{1,0:T(8,128)S(1)}, f32[64,128]{1,0:T(8,128)S(1)}, u32[]{:S(2)}, u32[]{:S(2)}) collective-permute-start(f32[64,128]{1,0:T(8,128)S(1)} %get-tuple-element.10.own_ref), channel_id=1, source_target_pairs={{0,1},{1,0},{2,3},{3,2},{4,5},{5,4},{6,7},{7,6},{8,9},{9,8},{10,11... | collective-permute-start | bytes 98312 | tf_op jit(solution)/shard_map/ppermute | solution.py:326

commit v8 on v7

--- a/solution.py
+++ b/solution.py
@@ -11,6 +11,7 @@
 NSTEP = 4
 CHIPS = (2, 3, 1, 0)
 GROUPS = (3, 0, 1, 2)
+PARTNERS = ((1, 2, 3), (2, 3, 1))
 VMEM = pl.BlockSpec(memory_space=pltpu.VMEM)
 ANY = pl.BlockSpec(memory_space=pl.ANY)
 
@@ -139,11 +140,13 @@
     members, levels, variables, tile, groups, factor, tiles_ref, *refs
 ):
     local_refs, (weight_ref, depart_ref, inc_ref, adj_ref, far_ref) = refs[:groups], refs[groups:]
-    mine = lax.axis_index("grp")
+    mine, odd = lax.axis_index("grp"), lax.rem(lax.axis_index("dom"), 2) == 1
     sums, first = {}, None
     for j in range(groups):
+        partner = jnp.where(odd, PARTNERS[1][j - 1], PARTNERS[0][j - 1]) if j else 0
         group = sum(
-            jnp.where(jnp.bitwise_xor(mine, j) == g, GROUPS.index(g), 0) for g in range(groups)
+            jnp.where(jnp.bitwise_xor(mine, partner) == g, GROUPS.index(g), 0)
+            for g in range(groups)
         )
         blocks = [
             tiles_ref[core, group, CHIPS.index(chip)]
@@ -248,6 +251,14 @@
     ]
 
 
+def group_pairs(groups, doms, k):
+    return [
+        (g * doms + d, (g ^ PARTNERS[d % 2][k]) * doms + d)
+        for g in range(groups)
+        for d in range(doms)
+    ]
+
+
 def beside(x, groups, doms):
     near = lax.ppermute(x, "dom", near_pairs(doms))
     far = lax.ppermute(x, ("grp", "dom"), far_pairs(groups, doms))
@@ -306,7 +317,7 @@
         cost_estimate=pl.CostEstimate(flops=10**10, bytes_accessed=0, transcendentals=0),
     )(in_vmem(rates), in_vmem(flat), in_vmem(near), in_vmem(far))
     locals_ = [local] + [
-        lax.ppermute(local, "grp", [(i, i ^ j) for i in range(groups)]) for j in range(1, groups)
+        lax.ppermute(local, ("grp", "dom"), group_pairs(groups, doms, k)) for k in range(groups - 1)
     ]
     increment, adjoint, for_far = pl.pallas_call(
         functools.partial(adjoint_kernel, members, levels, variables, tile, groups, factor),

time: 21.7 us -> 21.7 us (level)
  no operation moved by 1% of the time
where the time goes in v8:
time: 21.7 us; the launch traced here: 21.5 us
  starting transfers between devices  13.1 us (60%)
  waiting for transfers between devices  4.9 us (23%)
  Pallas kernels  2.1 us (10%)
  between operations  0.73 us (3%)
  local copies, waits for them, and re-layouts  0.64 us (3%)
    all_to_all x1, starting transfers between devices, small_device(): lax.all_to_all(tiles.reshape(-1, *tiles.shape[3:]), ('grp', 'dom'), split...  4.84 us
    ppermute x3, waiting for transfers between devices, small_device(): lax.ppermute(local, ('grp', 'dom'), group_pairs(groups, doms, k))  3.65 us
    ppermute x3, starting transfers between devices, small_device(): lax.ppermute(local, ('grp', 'dom'), group_pairs(groups, doms, k))  3.55 us
    ppermute x1, starting transfers between devices, beside(): far = lax.ppermute(x, ('grp', 'dom'), far_pairs(groups, doms))  3 us
    ppermute x1, starting transfers between devices, small_device(): far = lax.ppermute(for_far, ('grp', 'dom'), far_pairs(groups, doms))  1.28 us
    pallas_call x1, Pallas kernels, small_device(): pl.pallas_call(functools.partial(pack_kernel, doms, tile, groups), out_sh...  0.9 us
    pallas_call x1, Pallas kernels, small_device(): pl.pallas_call(functools.partial(end_kernel, members, tile), out_shape=ja...  0.83 us
    ppermute x1, waiting for transfers between devices, small_device(): far = lax.ppermute(for_far, ('grp', 'dom'), far_pairs(groups, doms))  0.69 us
  transfers between devices with their start and end apart: 8, of which 6 were waited for; matrix products, arithmetic and copies ran while one was open for 3% of the time, Pallas kernels for 9%

profile of v8, /device:TPU:0, one launch (start us, length us, event | category | flops | bytes accessed | tf_op | source)
XLA Modules:
  0.0 21.5 jit_solution(13053154986499895718)
XLA Ops:
  0.6 0.0 copy-start.3
  0.6 3.0 %collective-permute-start.1 = (f32[64,128]{1,0:T(8,128)}, f32[64,128]{1,0:T(8,128)S(1)}, u32[]{:S(2)}, u32[]{:S(2)}) collective-permute-start(f32[64,128]{1,0:T(8,128)} %bitcast.12), channel_id=1, source_target_pairs={{0,8},{1,2},{2,1},{3,4},{4,3},{5,6},{6,5},{7,15},{8,0},{9,10},{10,... | collective-permute-start | bytes 98312 | tf_op jit(solution)/shard_map/ppermute | solution.py:264
  3.6 0.2 collective-permute-start
  3.9 0.0 copy-done.3
  3.9 0.9 %shard_map.78 = (bf16[2,4,4,16,128]{4,3,2,1,0:T(8,128)(2,1)}, f32[4,8,128]{2,1,0:T(8,128)S(1)}) custom-call(bf16[32,128]{1,0:T(8,128)(2,1)S(1)} %shard_map.77.chosen_ref, bf16[16,2,512]{2,1,0:T(2,128)(2,1)S(1)} %bitcast.19, f32[1,8]{1,0:T(1,128)} %bitcast.22, s32[1,8]{1,0:T(1,128)} %bitcast.23), custom_call_target="tpu_custom_call" | custom-call | tf_op jit(solution)/shard_map/pallas_call | solution.py:282
  4.8 0.0 copy-start
  4.8 4.8 %all-to-all-start = ((bf16[32,16,128]{2,1,0:T(8,128)(2,1)}), bf16[32,16,128]{2,1,0:T(8,128)(2,1)S(1)}, u32[]{:S(2)}, u32[]{:S(2)}) async-start(bf16[32,16,128]{2,1,0:T(8,128)(2,1)} %bitcast.20), calls=%async_computation | async-start | bytes 262144 | tf_op jit(solution)/shard_map/all_to_all | solution.py:303
  9.6 0.0 collective-permute-done.1.far_ref
  9.6 0.0 collective-permute-done.near_ref
  9.7 0.0 copy-done
  9.7 0.0 copy-start.1
  9.7 0.0 copy-start.2
  9.7 0.2 %shard_map.79.refs_0_ = f32[64,128]{1,0:T(8,128)S(1)} custom-call(f32[4,8,128]{2,1,0:T(8,128)S(1)} %get-tuple-element.8.rates_ref, f32[64,128]{1,0:T(8,128)S(1)} %bitcast.14, f32[64,128]{1,0:T(8,128)S(1)} %collective-permute-done.near_ref, f32[64,128]{1,0:T(8,128)S(1)} %collective-permute-done.1.far_ref), custom_call_target="tpu_custom_call" | custom-call | flops 10000000000 | tf_op jit(solution)/shard_map/pallas_call | solution.py:312
  9.9 2.7 %collective-permute-start.4 = (f32[64,128]{1,0:T(8,128)S(1)}, f32[64,128]{1,0:T(8,128)S(1)}, u32[]{:S(2)}, u32[]{:S(2)}) collective-permute-start(f32[64,128]{1,0:T(8,128)S(1)} %shard_map.79.refs_0_), channel_id=1, source_target_pairs={{0,24},{1,9},{2,26},{3,11},{4,28},{5,13},{6,30},{7,15},{8,16},{9,1... | collective-permute-start | bytes 98312 | tf_op jit(solution)/shard_map/ppermute | solution.py:320
  12.6 0.6 %collective-permute-start.3 = (f32[64,128]{1,0:T(8,128)S(1)}, f32[64,128]{1,0:T(8,128)S(1)}, u32[]{:S(2)}, u32[]{:S(2)}) collective-permute-start(f32[64,128]{1,0:T(8,128)S(1)} %shard_map.79.refs_0_), channel_id=1, source_target_pairs={{0,16},{1,25},{2,18},{3,27},{4,20},{5,29},{6,22},{7,31},{8,24},{9,... | collective-permute-start | bytes 98312 | tf_op jit(solution)/shard_map/ppermute | solution.py:320
  13.2 0.3 %collective-permute-start.2 = (f32[64,128]{1,0:T(8,128)S(1)}, f32[64,128]{1,0:T(8,128)S(1)}, u32[]{:S(2)}, u32[]{:S(2)}) collective-permute-start(f32[64,128]{1,0:T(8,128)S(1)} %shard_map.79.refs_0_), channel_id=1, source_target_pairs={{0,8},{1,17},{2,10},{3,19},{4,12},{5,21},{6,14},{7,23},{8,0},{9,25... | collective-permute-start | bytes 98312 | tf_op jit(solution)/shard_map/ppermute | solution.py:320
  13.5 1.6 %collective-permute-done.4.refs_3_ = f32[64,128]{1,0:T(8,128)S(1)} collective-permute-done((f32[64,128]{1,0:T(8,128)S(1)}, f32[64,128]{1,0:T(8,128)S(1)}, u32[]{:S(2)}, u32[]{:S(2)}) %collective-permute-start.4) | collective-permute-done | bytes 32800 | tf_op jit(solution)/shard_map/ppermute | solution.py:320
  15.0 1.7 %collective-permute-done.3.refs_2_ = f32[64,128]{1,0:T(8,128)S(1)} collective-permute-done((f32[64,128]{1,0:T(8,128)S(1)}, f32[64,128]{1,0:T(8,128)S(1)}, u32[]{:S(2)}, u32[]{:S(2)}) %collective-permute-start.3) | collective-permute-done | bytes 32800 | tf_op jit(solution)/shard_map/ppermute | solution.py:320
  16.7 0.4 %collective-permute-done.2.refs_1_ = f32[64,128]{1,0:T(8,128)S(1)} collective-permute-done((f32[64,128]{1,0:T(8,128)S(1)}, f32[64,128]{1,0:T(8,128)S(1)}, u32[]{:S(2)}, u32[]{:S(2)}) %collective-permute-start.2) | collective-permute-done | bytes 32800 | tf_op jit(solution)/shard_map/ppermute | solution.py:320
  17.1 0.2 all-to-all-done
  17.3 0.0 copy-done.1
  17.3 0.0 copy-done.2
  17.3 0.1 shard_map.80
  17.4 1.3 %collective-permute-start.6 = (f32[72,128]{1,0:T(8,128)S(1)}, f32[72,128]{1,0:T(8,128)S(1)}, u32[]{:S(2)}, u32[]{:S(2)}) collective-permute-start(f32[72,128]{1,0:T(8,128)S(1)} %get-tuple-element.11), channel_id=1, source_target_pairs={{0,8},{1,2},{2,1},{3,4},{4,3},{5,6},{6,5},{7,15},{8,0},{9,10},{10,... | collective-permute-start | bytes 110600 | tf_op jit(solution)/shard_map/ppermute | solution.py:338
  18.7 0.2 %collective-permute-start.5 = (f32[64,128]{1,0:T(8,128)S(1)}, f32[64,128]{1,0:T(8,128)S(1)}, u32[]{:S(2)}, u32[]{:S(2)}) collective-permute-start(f32[64,128]{1,0:T(8,128)S(1)} %get-tuple-element.10.own_ref), channel_id=1, source_target_pairs={{0,1},{1,0},{2,3},{3,2},{4,5},{5,4},{6,7},{7,6},{8,9},{9,8},{10,11... | collective-permute-start | bytes 98312 | tf_op jit(solution)/shard_map/ppermute | solution.py:337
  18.9 0.6 %copy.10 = f32[8,2,4,128]{3,2,1,0:T(4,128)} copy(f32[8,2,4,128]{3,2,1,0:T(4,128)S(1)} %bitcast.10) | data formatting | bytes 65536
  19.5 0.4 %collective-permute-done.5.near_ref = f32[64,128]{1,0:T(8,128)S(1)} collective-permute-done((f32[64,128]{1,0:T(8,128)S(1)}, f32[64,128]{1,0:T(8,128)S(1)}, u32[]{:S(2)}, u32[]{:S(2)}) %collective-permute-start.5) | collective-permute-done | bytes 32800 | tf_op jit(solution)/shard_map/ppermute | solution.py:337
  19.9 0.8 %shard_map.81._ = f32[64,128]{1,0:T(8,128)} custom-call(f32[4,8,128]{2,1,0:T(8,128)S(1)} %get-tuple-element.8.rates_ref, f32[64,128]{1,0:T(8,128)S(1)} %get-tuple-element.10.own_ref, f32[64,128]{1,0:T(8,128)S(1)} %collective-permute-done.5.near_ref, f32[64,128]{1,0:T(8,128)S(1)} %bitcast.15), custom_call_target="tpu_custom_call" | custom-call | tf_op jit(solution)/shard_map/pallas_call | solution.py:339
  20.8 0.7 %collective-permute-done.6.far_ref = f32[72,128]{1,0:T(8,128)S(1)} collective-permute-done((f32[72,128]{1,0:T(8,128)S(1)}, f32[72,128]{1,0:T(8,128)S(1)}, u32[]{:S(2)}, u32[]{:S(2)}) %collective-permute-start.6) | collective-permute-done | bytes 36896 | tf_op jit(solution)/shard_map/ppermute | solution.py:338
  (2 shorter events, 0.0 us)
Async XLA Ops:
  0.6 3.2 %copy-start.3 = (bf16[2,8,2,1,512]{4,2,3,1,0:T(2,128)(2,1)S(1)}, bf16[2,8,2,1,512]{4,2,3,1,0:T(2,128)(2,1)}, u32[]{:S(2)}) copy-start(bf16[2,8,2,1,512]{4,2,3,1,0:T(2,128)(2,1)} %param.6) | copy-start | bytes 98308
  0.6 9.0 %collective-permute-start.1 = (f32[64,128]{1,0:T(8,128)}, f32[64,128]{1,0:T(8,128)S(1)}, u32[]{:S(2)}, u32[]{:S(2)}) collective-permute-start(f32[64,128]{1,0:T(8,128)} %bitcast.12), channel_id=1, source_target_pairs={{0,8},{1,2},{2,1},{3,4},{4,3},{5,6},{6,5},{7,15},{8,0},{9,10},{10,... | collective-permute-start | bytes 98312 | tf_op jit(solution)/shard_map/ppermute | solution.py:264
  3.6 6.0 %collective-permute-start = (f32[64,128]{1,0:T(8,128)}, f32[64,128]{1,0:T(8,128)S(1)}, u32[]{:S(2)}, u32[]{:S(2)}) collective-permute-start(f32[64,128]{1,0:T(8,128)} %bitcast.13), channel_id=1, source_target_pairs={{0,1},{1,0},{2,3},{3,2},{4,5},{5,4},{6,7},{7,6},{8,9},{9,8},{10,11... | collective-permute-start | bytes 98312 | tf_op jit(solution)/shard_map/ppermute | solution.py:263
  4.8 4.9 %copy-start = (f32[2,8,4,128]{3,2,1,0:T(4,128)S(1)}, f32[2,8,4,128]{3,2,1,0:T(4,128)}, u32[]{:S(2)}) copy-start(f32[2,8,4,128]{3,2,1,0:T(4,128)} %param.7) | copy-start | bytes 98308
  4.8 12.5 %all-to-all-start = ((bf16[32,16,128]{2,1,0:T(8,128)(2,1)}), bf16[32,16,128]{2,1,0:T(8,128)(2,1)S(1)}, u32[]{:S(2)}, u32[]{:S(2)}) async-start(bf16[32,16,128]{2,1,0:T(8,128)(2,1)} %bitcast.20), calls=%async_computation | async-start | bytes 262144 | tf_op jit(solution)/shard_map/all_to_all | solution.py:303
  9.7 7.6 %copy-start.1 = (f32[8,2,4,128]{3,2,1,0:T(4,128)S(1)}, f32[8,2,4,128]{3,2,1,0:T(4,128)}, u32[]{:S(2)}) copy-start(f32[8,2,4,128]{3,2,1,0:T(4,128)} %param.9) | copy-start | bytes 98308
  9.7 7.6 %copy-start.2 = (f32[8,2,4,128]{3,2,1,0:T(4,128)S(1)}, f32[8,2,4,128]{3,2,1,0:T(4,128)}, u32[]{:S(2)}) copy-start(f32[8,2,4,128]{3,2,1,0:T(4,128)} %param.8) | copy-start | bytes 98308
  9.9 5.1 %collective-permute-start.4 = (f32[64,128]{1,0:T(8,128)S(1)}, f32[64,128]{1,0:T(8,128)S(1)}, u32[]{:S(2)}, u32[]{:S(2)}) collective-permute-start(f32[64,128]{1,0:T(8,128)S(1)} %shard_map.79.refs_0_), channel_id=1, source_target_pairs={{0,24},{1,9},{2,26},{3,11},{4,28},{5,13},{6,30},{7,15},{8,16},{9,1... | collective-permute-start | bytes 98312 | tf_op jit(solution)/shard_map/ppermute | solution.py:320
  12.6 4.1 %collective-permute-start.3 = (f32[64,128]{1,0:T(8,128)S(1)}, f32[64,128]{1,0:T(8,128)S(1)}, u32[]{:S(2)}, u32[]{:S(2)}) collective-permute-start(f32[64,128]{1,0:T(8,128)S(1)} %shard_map.79.refs_0_), channel_id=1, source_target_pairs={{0,16},{1,25},{2,18},{3,27},{4,20},{5,29},{6,22},{7,31},{8,24},{9,... | collective-permute-start | bytes 98312 | tf_op jit(solution)/shard_map/ppermute | solution.py:320
  13.2 3.9 %collective-permute-start.2 = (f32[64,128]{1,0:T(8,128)S(1)}, f32[64,128]{1,0:T(8,128)S(1)}, u32[]{:S(2)}, u32[]{:S(2)}) collective-permute-start(f32[64,128]{1,0:T(8,128)S(1)} %shard_map.79.refs_0_), channel_id=1, source_target_pairs={{0,8},{1,17},{2,10},{3,19},{4,12},{5,21},{6,14},{7,23},{8,0},{9,25... | collective-permute-start | bytes 98312 | tf_op jit(solution)/shard_map/ppermute | solution.py:320
  17.4 4.0 %collective-permute-start.6 = (f32[72,128]{1,0:T(8,128)S(1)}, f32[72,128]{1,0:T(8,128)S(1)}, u32[]{:S(2)}, u32[]{:S(2)}) collective-permute-start(f32[72,128]{1,0:T(8,128)S(1)} %get-tuple-element.11), channel_id=1, source_target_pairs={{0,8},{1,2},{2,1},{3,4},{4,3},{5,6},{6,5},{7,15},{8,0},{9,10},{10,... | collective-permute-start | bytes 110600 | tf_op jit(solution)/shard_map/ppermute | solution.py:338
  18.7 1.2 %collective-permute-start.5 = (f32[64,128]{1,0:T(8,128)S(1)}, f32[64,128]{1,0:T(8,128)S(1)}, u32[]{:S(2)}, u32[]{:S(2)}) collective-permute-start(f32[64,128]{1,0:T(8,128)S(1)} %get-tuple-element.10.own_ref), channel_id=1, source_target_pairs={{0,1},{1,0},{2,3},{3,2},{4,5},{5,4},{6,7},{7,6},{8,9},{9,8},{10,11... | collective-permute-start | bytes 98312 | tf_op jit(solution)/shard_map/ppermute | solution.py:337

commit v9 on v7

--- a/solution.py
+++ b/solution.py
@@ -231,7 +231,7 @@
     for g in range(groups):
         for d in range(doms):
             if d in (0, doms - 1):
-                pairs.append((g * doms + d, (g ^ 1) * doms + d))
+                pairs.append((g * doms + d, (g ^ 2) * doms + d))
             else:
                 pairs.append((g * doms + d, g * doms + (d + 1 if d % 2 else d - 1)))
     return pairs

time: 21.7 us -> 21.7 us (level)
  no operation moved by 1% of the time
where the time goes in v9:
time: 21.7 us; the launch traced here: 21.5 us
  starting transfers between devices  13.1 us (60%)
  waiting for transfers between devices  4.9 us (23%)
  Pallas kernels  2.09 us (10%)
  between operations  0.73 us (3%)
  local copies, waits for them, and re-layouts  0.64 us (3%)
    all_to_all x1, starting transfers between devices, small_device(): lax.all_to_all(tiles.reshape(-1, *tiles.shape[3:]), ('grp', 'dom'), split...  4.84 us
    ppermute x3, waiting for transfers between devices, small_device(): lax.ppermute(local, 'grp', [(i, i ^ j) for i in range(groups)])  3.65 us
    ppermute x3, starting transfers between devices, small_device(): lax.ppermute(local, 'grp', [(i, i ^ j) for i in range(groups)])  3.55 us
    ppermute x1, starting transfers between devices, beside(): far = lax.ppermute(x, ('grp', 'dom'), far_pairs(groups, doms))  3.03 us
    ppermute x1, starting transfers between devices, small_device(): far = lax.ppermute(for_far, ('grp', 'dom'), far_pairs(groups, doms))  1.38 us
    pallas_call x1, Pallas kernels, small_device(): pl.pallas_call(functools.partial(pack_kernel, doms, tile, groups), out_sh...  0.9 us
    pallas_call x1, Pallas kernels, small_device(): pl.pallas_call(functools.partial(end_kernel, members, tile), out_shape=ja...  0.83 us
    unnamed x9, local copies, waits for them, and re-layouts  0.64 us
  transfers between devices with their start and end apart: 8, of which 6 were waited for; matrix products, arithmetic and copies ran while one was open for 3% of the time, Pallas kernels for 9%

profile of v9, /device:TPU:0, one launch (start us, length us, event | category | flops | bytes accessed | tf_op | source)
XLA Modules:
  0.0 21.5 jit_solution(11019774624710378947)
XLA Ops:
  0.6 0.0 copy-start.3
  0.6 3.0 %collective-permute-start.1 = (f32[64,128]{1,0:T(8,128)}, f32[64,128]{1,0:T(8,128)S(1)}, u32[]{:S(2)}, u32[]{:S(2)}) collective-permute-start(f32[64,128]{1,0:T(8,128)} %bitcast.12), channel_id=1, source_target_pairs={{0,16},{1,2},{2,1},{3,4},{4,3},{5,6},{6,5},{7,23},{8,24},{9,10},{1... | collective-permute-start | bytes 98312 | tf_op jit(solution)/shard_map/ppermute | solution.py:253
  3.7 0.2 collective-permute-start
  3.9 0.0 copy-done.3
  3.9 0.9 %shard_map.78 = (bf16[2,4,4,16,128]{4,3,2,1,0:T(8,128)(2,1)}, f32[4,8,128]{2,1,0:T(8,128)S(1)}) custom-call(bf16[32,128]{1,0:T(8,128)(2,1)S(1)} %shard_map.77.chosen_ref, bf16[16,2,512]{2,1,0:T(2,128)(2,1)S(1)} %bitcast.19, f32[1,8]{1,0:T(1,128)} %bitcast.22, s32[1,8]{1,0:T(1,128)} %bitcast.23), custom_call_target="tpu_custom_call" | custom-call | tf_op jit(solution)/shard_map/pallas_call | solution.py:271
  4.8 0.0 copy-start
  4.8 4.8 %all-to-all-start = ((bf16[32,16,128]{2,1,0:T(8,128)(2,1)}), bf16[32,16,128]{2,1,0:T(8,128)(2,1)S(1)}, u32[]{:S(2)}, u32[]{:S(2)}) async-start(bf16[32,16,128]{2,1,0:T(8,128)(2,1)} %bitcast.20), calls=%async_computation | async-start | bytes 262144 | tf_op jit(solution)/shard_map/all_to_all | solution.py:292
  9.6 0.0 collective-permute-done.1.far_ref
  9.6 0.0 collective-permute-done.near_ref
  9.7 0.0 copy-done
  9.7 0.0 copy-start.1
  9.7 0.0 copy-start.2
  9.7 0.2 %shard_map.79.refs_0_ = f32[64,128]{1,0:T(8,128)S(1)} custom-call(f32[4,8,128]{2,1,0:T(8,128)S(1)} %get-tuple-element.8.rates_ref, f32[64,128]{1,0:T(8,128)S(1)} %bitcast.14, f32[64,128]{1,0:T(8,128)S(1)} %collective-permute-done.near_ref, f32[64,128]{1,0:T(8,128)S(1)} %collective-permute-done.1.far_ref), custom_call_target="tpu_custom_call" | custom-call | flops 10000000000 | tf_op jit(solution)/shard_map/pallas_call | solution.py:301
  9.9 2.7 %collective-permute-start.4 = (f32[64,128]{1,0:T(8,128)S(1)}, f32[64,128]{1,0:T(8,128)S(1)}, u32[]{:S(2)}, u32[]{:S(2)}) collective-permute-start(f32[64,128]{1,0:T(8,128)S(1)} %shard_map.79.refs_0_), channel_id=1, source_target_pairs={{0,24},{8,16},{16,8},{24,0},{1,25},{9,17},{17,9},{25,1},{2,26},{10... | collective-permute-start | bytes 98312 | tf_op jit(solution)/shard_map/ppermute | solution.py:309
  12.6 0.6 %collective-permute-start.3 = (f32[64,128]{1,0:T(8,128)S(1)}, f32[64,128]{1,0:T(8,128)S(1)}, u32[]{:S(2)}, u32[]{:S(2)}) collective-permute-start(f32[64,128]{1,0:T(8,128)S(1)} %shard_map.79.refs_0_), channel_id=1, source_target_pairs={{0,16},{8,24},{16,0},{24,8},{1,17},{9,25},{17,1},{25,9},{2,18},{10... | collective-permute-start | bytes 98312 | tf_op jit(solution)/shard_map/ppermute | solution.py:309
  13.2 0.3 %collective-permute-start.2 = (f32[64,128]{1,0:T(8,128)S(1)}, f32[64,128]{1,0:T(8,128)S(1)}, u32[]{:S(2)}, u32[]{:S(2)}) collective-permute-start(f32[64,128]{1,0:T(8,128)S(1)} %shard_map.79.refs_0_), channel_id=1, source_target_pairs={{0,8},{8,0},{16,24},{24,16},{1,9},{9,1},{17,25},{25,17},{2,10},{10... | collective-permute-start | bytes 98312 | tf_op jit(solution)/shard_map/ppermute | solution.py:309
  13.5 1.5 %collective-permute-done.4.refs_3_ = f32[64,128]{1,0:T(8,128)S(1)} collective-permute-done((f32[64,128]{1,0:T(8,128)S(1)}, f32[64,128]{1,0:T(8,128)S(1)}, u32[]{:S(2)}, u32[]{:S(2)}) %collective-permute-start.4) | collective-permute-done | bytes 32800 | tf_op jit(solution)/shard_map/ppermute | solution.py:309
  15.0 1.7 %collective-permute-done.3.refs_2_ = f32[64,128]{1,0:T(8,128)S(1)} collective-permute-done((f32[64,128]{1,0:T(8,128)S(1)}, f32[64,128]{1,0:T(8,128)S(1)}, u32[]{:S(2)}, u32[]{:S(2)}) %collective-permute-start.3) | collective-permute-done | bytes 32800 | tf_op jit(solution)/shard_map/ppermute | solution.py:309
  16.7 0.4 %collective-permute-done.2.refs_1_ = f32[64,128]{1,0:T(8,128)S(1)} collective-permute-done((f32[64,128]{1,0:T(8,128)S(1)}, f32[64,128]{1,0:T(8,128)S(1)}, u32[]{:S(2)}, u32[]{:S(2)}) %collective-permute-start.2) | collective-permute-done | bytes 32800 | tf_op jit(solution)/shard_map/ppermute | solution.py:309
  17.1 0.2 all-to-all-done
  17.3 0.0 copy-done.1
  17.3 0.0 copy-done.2
  17.3 0.1 shard_map.80
  17.4 1.4 %collective-permute-start.6 = (f32[72,128]{1,0:T(8,128)S(1)}, f32[72,128]{1,0:T(8,128)S(1)}, u32[]{:S(2)}, u32[]{:S(2)}) collective-permute-start(f32[72,128]{1,0:T(8,128)S(1)} %get-tuple-element.11), channel_id=1, source_target_pairs={{0,16},{1,2},{2,1},{3,4},{4,3},{5,6},{6,5},{7,23},{8,24},{9,10},{1... | collective-permute-start | bytes 110600 | tf_op jit(solution)/shard_map/ppermute | solution.py:327
  18.8 0.1 collective-permute-start.5
  18.9 0.6 %copy.10 = f32[8,2,4,128]{3,2,1,0:T(4,128)} copy(f32[8,2,4,128]{3,2,1,0:T(4,128)S(1)} %bitcast.10) | data formatting | bytes 65536
  19.5 0.5 %collective-permute-done.5.near_ref = f32[64,128]{1,0:T(8,128)S(1)} collective-permute-done((f32[64,128]{1,0:T(8,128)S(1)}, f32[64,128]{1,0:T(8,128)S(1)}, u32[]{:S(2)}, u32[]{:S(2)}) %collective-permute-start.5) | collective-permute-done | bytes 32800 | tf_op jit(solution)/shard_map/ppermute | solution.py:326
  20.0 0.8 %shard_map.81._ = f32[64,128]{1,0:T(8,128)} custom-call(f32[4,8,128]{2,1,0:T(8,128)S(1)} %get-tuple-element.8.rates_ref, f32[64,128]{1,0:T(8,128)S(1)} %get-tuple-element.10.own_ref, f32[64,128]{1,0:T(8,128)S(1)} %collective-permute-done.5.near_ref, f32[64,128]{1,0:T(8,128)S(1)} %bitcast.15), custom_call_target="tpu_custom_call" | custom-call | tf_op jit(solution)/shard_map/pallas_call | solution.py:328
  20.9 0.6 %collective-permute-done.6.far_ref = f32[72,128]{1,0:T(8,128)S(1)} collective-permute-done((f32[72,128]{1,0:T(8,128)S(1)}, f32[72,128]{1,0:T(8,128)S(1)}, u32[]{:S(2)}, u32[]{:S(2)}) %collective-permute-start.6) | collective-permute-done | bytes 36896 | tf_op jit(solution)/shard_map/ppermute | solution.py:327
  (2 shorter events, 0.0 us)
Async XLA Ops:
  0.6 3.2 %copy-start.3 = (bf16[2,8,2,1,512]{4,2,3,1,0:T(2,128)(2,1)S(1)}, bf16[2,8,2,1,512]{4,2,3,1,0:T(2,128)(2,1)}, u32[]{:S(2)}) copy-start(bf16[2,8,2,1,512]{4,2,3,1,0:T(2,128)(2,1)} %param.6) | copy-start | bytes 98308
  0.6 9.0 %collective-permute-start.1 = (f32[64,128]{1,0:T(8,128)}, f32[64,128]{1,0:T(8,128)S(1)}, u32[]{:S(2)}, u32[]{:S(2)}) collective-permute-start(f32[64,128]{1,0:T(8,128)} %bitcast.12), channel_id=1, source_target_pairs={{0,16},{1,2},{2,1},{3,4},{4,3},{5,6},{6,5},{7,23},{8,24},{9,10},{1... | collective-permute-start | bytes 98312 | tf_op jit(solution)/shard_map/ppermute | solution.py:253
  3.7 6.0 %collective-permute-start = (f32[64,128]{1,0:T(8,128)}, f32[64,128]{1,0:T(8,128)S(1)}, u32[]{:S(2)}, u32[]{:S(2)}) collective-permute-start(f32[64,128]{1,0:T(8,128)} %bitcast.13), channel_id=1, source_target_pairs={{0,1},{1,0},{2,3},{3,2},{4,5},{5,4},{6,7},{7,6},{8,9},{9,8},{10,11... | collective-permute-start | bytes 98312 | tf_op jit(solution)/shard_map/ppermute | solution.py:252
  4.8 4.9 %copy-start = (f32[2,8,4,128]{3,2,1,0:T(4,128)S(1)}, f32[2,8,4,128]{3,2,1,0:T(4,128)}, u32[]{:S(2)}) copy-start(f32[2,8,4,128]{3,2,1,0:T(4,128)} %param.7) | copy-start | bytes 98308
  4.8 12.5 %all-to-all-start = ((bf16[32,16,128]{2,1,0:T(8,128)(2,1)}), bf16[32,16,128]{2,1,0:T(8,128)(2,1)S(1)}, u32[]{:S(2)}, u32[]{:S(2)}) async-start(bf16[32,16,128]{2,1,0:T(8,128)(2,1)} %bitcast.20), calls=%async_computation | async-start | bytes 262144 | tf_op jit(solution)/shard_map/all_to_all | solution.py:292
  9.7 7.6 %copy-start.1 = (f32[8,2,4,128]{3,2,1,0:T(4,128)S(1)}, f32[8,2,4,128]{3,2,1,0:T(4,128)}, u32[]{:S(2)}) copy-start(f32[8,2,4,128]{3,2,1,0:T(4,128)} %param.9) | copy-start | bytes 98308
  9.7 7.6 %copy-start.2 = (f32[8,2,4,128]{3,2,1,0:T(4,128)S(1)}, f32[8,2,4,128]{3,2,1,0:T(4,128)}, u32[]{:S(2)}) copy-start(f32[8,2,4,128]{3,2,1,0:T(4,128)} %param.8) | copy-start | bytes 98308
  9.9 5.1 %collective-permute-start.4 = (f32[64,128]{1,0:T(8,128)S(1)}, f32[64,128]{1,0:T(8,128)S(1)}, u32[]{:S(2)}, u32[]{:S(2)}) collective-permute-start(f32[64,128]{1,0:T(8,128)S(1)} %shard_map.79.refs_0_), channel_id=1, source_target_pairs={{0,24},{8,16},{16,8},{24,0},{1,25},{9,17},{17,9},{25,1},{2,26},{10... | collective-permute-start | bytes 98312 | tf_op jit(solution)/shard_map/ppermute | solution.py:309
  12.6 4.1 %collective-permute-start.3 = (f32[64,128]{1,0:T(8,128)S(1)}, f32[64,128]{1,0:T(8,128)S(1)}, u32[]{:S(2)}, u32[]{:S(2)}) collective-permute-start(f32[64,128]{1,0:T(8,128)S(1)} %shard_map.79.refs_0_), channel_id=1, source_target_pairs={{0,16},{8,24},{16,0},{24,8},{1,17},{9,25},{17,1},{25,9},{2,18},{10... | collective-permute-start | bytes 98312 | tf_op jit(solution)/shard_map/ppermute | solution.py:309
  13.2 3.9 %collective-permute-start.2 = (f32[64,128]{1,0:T(8,128)S(1)}, f32[64,128]{1,0:T(8,128)S(1)}, u32[]{:S(2)}, u32[]{:S(2)}) collective-permute-start(f32[64,128]{1,0:T(8,128)S(1)} %shard_map.79.refs_0_), channel_id=1, source_target_pairs={{0,8},{8,0},{16,24},{24,16},{1,9},{9,1},{17,25},{25,17},{2,10},{10... | collective-permute-start | bytes 98312 | tf_op jit(solution)/shard_map/ppermute | solution.py:309
  17.4 4.0 %collective-permute-start.6 = (f32[72,128]{1,0:T(8,128)S(1)}, f32[72,128]{1,0:T(8,128)S(1)}, u32[]{:S(2)}, u32[]{:S(2)}) collective-permute-start(f32[72,128]{1,0:T(8,128)S(1)} %get-tuple-element.11), channel_id=1, source_target_pairs={{0,16},{1,2},{2,1},{3,4},{4,3},{5,6},{6,5},{7,23},{8,24},{9,10},{1... | collective-permute-start | bytes 110600 | tf_op jit(solution)/shard_map/ppermute | solution.py:327
  18.8 1.2 %collective-permute-start.5 = (f32[64,128]{1,0:T(8,128)S(1)}, f32[64,128]{1,0:T(8,128)S(1)}, u32[]{:S(2)}, u32[]{:S(2)}) collective-permute-start(f32[64,128]{1,0:T(8,128)S(1)} %get-tuple-element.10.own_ref), channel_id=1, source_target_pairs={{0,1},{1,0},{2,3},{3,2},{4,5},{5,4},{6,7},{7,6},{8,9},{9,8},{10,11... | collective-permute-start | bytes 98312 | tf_op jit(solution)/shard_map/ppermute | solution.py:326

commit v10 on v7

--- a/solution.py
+++ b/solution.py
@@ -150,7 +150,7 @@
             for chip in range(len(CHIPS))
             for core in range(2)
         ]
-        fields = jnp.concatenate(blocks, axis=0).astype(jnp.float32).T
+        fields = jnp.concatenate(blocks, axis=0).T.astype(jnp.float32)
         if j == 0:
             first = fields
         for r in range(tile):

time: 21.7 us -> 21.7 us (level)
  no operation moved by 1% of the time
where the time goes in v10:
time: 21.7 us; the launch traced here: 21.5 us
  starting transfers between devices  13.1 us (60%)
  waiting for transfers between devices  4.91 us (23%)
  Pallas kernels  2.08 us (10%)
  between operations  0.74 us (3%)
  local copies, waits for them, and re-layouts  0.64 us (3%)
    all_to_all x1, starting transfers between devices, small_device(): lax.all_to_all(tiles.reshape(-1, *tiles.shape[3:]), ('grp', 'dom'), split...  4.84 us
    ppermute x3, waiting for transfers between devices, small_device(): lax.ppermute(local, 'grp', [(i, i ^ j) for i in range(groups)])  3.65 us
    ppermute x3, starting transfers between devices, small_device(): lax.ppermute(local, 'grp', [(i, i ^ j) for i in range(groups)])  3.55 us
    ppermute x1, starting transfers between devices, beside(): far = lax.ppermute(x, ('grp', 'dom'), far_pairs(groups, doms))  3 us
    ppermute x1, starting transfers between devices, small_device(): far = lax.ppermute(for_far, ('grp', 'dom'), far_pairs(groups, doms))  1.28 us
    pallas_call x1, Pallas kernels, small_device(): pl.pallas_call(functools.partial(pack_kernel, doms, tile, groups), out_sh...  0.9 us
    pallas_call x1, Pallas kernels, small_device(): pl.pallas_call(functools.partial(end_kernel, members, tile), out_shape=ja...  0.83 us
    ppermute x1, waiting for transfers between devices, small_device(): far = lax.ppermute(for_far, ('grp', 'dom'), far_pairs(groups, doms))  0.69 us
  transfers between devices with their start and end apart: 8, of which 6 were waited for; matrix products, arithmetic and copies ran while one was open for 3% of the time, Pallas kernels for 9%

profile of v10, /device:TPU:0, one launch (start us, length us, event | category | flops | bytes accessed | tf_op | source)
XLA Modules:
  0.0 21.5 jit_solution(17309792374564221387)
XLA Ops:
  0.6 0.0 copy-start.3
  0.6 3.0 %collective-permute-start.1 = (f32[64,128]{1,0:T(8,128)}, f32[64,128]{1,0:T(8,128)S(1)}, u32[]{:S(2)}, u32[]{:S(2)}) collective-permute-start(f32[64,128]{1,0:T(8,128)} %bitcast.12), channel_id=1, source_target_pairs={{0,8},{1,2},{2,1},{3,4},{4,3},{5,6},{6,5},{7,15},{8,0},{9,10},{10,... | collective-permute-start | bytes 98312 | tf_op jit(solution)/shard_map/ppermute | solution.py:253
  3.6 0.2 collective-permute-start
  3.9 0.0 copy-done.3
  3.9 0.9 %shard_map.78 = (bf16[2,4,4,16,128]{4,3,2,1,0:T(8,128)(2,1)}, f32[4,8,128]{2,1,0:T(8,128)S(1)}) custom-call(bf16[32,128]{1,0:T(8,128)(2,1)S(1)} %shard_map.77.chosen_ref, bf16[16,2,512]{2,1,0:T(2,128)(2,1)S(1)} %bitcast.19, f32[1,8]{1,0:T(1,128)} %bitcast.22, s32[1,8]{1,0:T(1,128)} %bitcast.23), custom_call_target="tpu_custom_call" | custom-call | tf_op jit(solution)/shard_map/pallas_call | solution.py:271
  4.8 0.0 copy-start
  4.8 4.8 %all-to-all-start = ((bf16[32,16,128]{2,1,0:T(8,128)(2,1)}), bf16[32,16,128]{2,1,0:T(8,128)(2,1)S(1)}, u32[]{:S(2)}, u32[]{:S(2)}) async-start(bf16[32,16,128]{2,1,0:T(8,128)(2,1)} %bitcast.20), calls=%async_computation | async-start | bytes 262144 | tf_op jit(solution)/shard_map/all_to_all | solution.py:292
  9.6 0.0 collective-permute-done.1.far_ref
  9.6 0.0 collective-permute-done.near_ref
  9.7 0.0 copy-done
  9.7 0.0 copy-start.1
  9.7 0.0 copy-start.2
  9.7 0.2 %shard_map.79.refs_0_ = f32[64,128]{1,0:T(8,128)S(1)} custom-call(f32[4,8,128]{2,1,0:T(8,128)S(1)} %get-tuple-element.8.rates_ref, f32[64,128]{1,0:T(8,128)S(1)} %bitcast.14, f32[64,128]{1,0:T(8,128)S(1)} %collective-permute-done.near_ref, f32[64,128]{1,0:T(8,128)S(1)} %collective-permute-done.1.far_ref), custom_call_target="tpu_custom_call" | custom-call | flops 10000000000 | tf_op jit(solution)/shard_map/pallas_call | solution.py:301
  9.9 2.7 %collective-permute-start.4 = (f32[64,128]{1,0:T(8,128)S(1)}, f32[64,128]{1,0:T(8,128)S(1)}, u32[]{:S(2)}, u32[]{:S(2)}) collective-permute-start(f32[64,128]{1,0:T(8,128)S(1)} %shard_map.79.refs_0_), channel_id=1, source_target_pairs={{0,24},{8,16},{16,8},{24,0},{1,25},{9,17},{17,9},{25,1},{2,26},{10... | collective-permute-start | bytes 98312 | tf_op jit(solution)/shard_map/ppermute | solution.py:309
  12.6 0.6 %collective-permute-start.3 = (f32[64,128]{1,0:T(8,128)S(1)}, f32[64,128]{1,0:T(8,128)S(1)}, u32[]{:S(2)}, u32[]{:S(2)}) collective-permute-start(f32[64,128]{1,0:T(8,128)S(1)} %shard_map.79.refs_0_), channel_id=1, source_target_pairs={{0,16},{8,24},{16,0},{24,8},{1,17},{9,25},{17,1},{25,9},{2,18},{10... | collective-permute-start | bytes 98312 | tf_op jit(solution)/shard_map/ppermute | solution.py:309
  13.2 0.3 %collective-permute-start.2 = (f32[64,128]{1,0:T(8,128)S(1)}, f32[64,128]{1,0:T(8,128)S(1)}, u32[]{:S(2)}, u32[]{:S(2)}) collective-permute-start(f32[64,128]{1,0:T(8,128)S(1)} %shard_map.79.refs_0_), channel_id=1, source_target_pairs={{0,8},{8,0},{16,24},{24,16},{1,9},{9,1},{17,25},{25,17},{2,10},{10... | collective-permute-start | bytes 98312 | tf_op jit(solution)/shard_map/ppermute | solution.py:309
  13.5 1.5 %collective-permute-done.4.refs_3_ = f32[64,128]{1,0:T(8,128)S(1)} collective-permute-done((f32[64,128]{1,0:T(8,128)S(1)}, f32[64,128]{1,0:T(8,128)S(1)}, u32[]{:S(2)}, u32[]{:S(2)}) %collective-permute-start.4) | collective-permute-done | bytes 32800 | tf_op jit(solution)/shard_map/ppermute | solution.py:309
  15.0 1.7 %collective-permute-done.3.refs_2_ = f32[64,128]{1,0:T(8,128)S(1)} collective-permute-done((f32[64,128]{1,0:T(8,128)S(1)}, f32[64,128]{1,0:T(8,128)S(1)}, u32[]{:S(2)}, u32[]{:S(2)}) %collective-permute-start.3) | collective-permute-done | bytes 32800 | tf_op jit(solution)/shard_map/ppermute | solution.py:309
  16.7 0.4 %collective-permute-done.2.refs_1_ = f32[64,128]{1,0:T(8,128)S(1)} collective-permute-done((f32[64,128]{1,0:T(8,128)S(1)}, f32[64,128]{1,0:T(8,128)S(1)}, u32[]{:S(2)}, u32[]{:S(2)}) %collective-permute-start.2) | collective-permute-done | bytes 32800 | tf_op jit(solution)/shard_map/ppermute | solution.py:309
  17.1 0.2 all-to-all-done
  17.3 0.0 copy-done.1
  17.3 0.0 copy-done.2
  17.3 0.1 shard_map.80
  17.4 1.3 %collective-permute-start.6 = (f32[72,128]{1,0:T(8,128)S(1)}, f32[72,128]{1,0:T(8,128)S(1)}, u32[]{:S(2)}, u32[]{:S(2)}) collective-permute-start(f32[72,128]{1,0:T(8,128)S(1)} %get-tuple-element.11), channel_id=1, source_target_pairs={{0,8},{1,2},{2,1},{3,4},{4,3},{5,6},{6,5},{7,15},{8,0},{9,10},{10,... | collective-permute-start | bytes 110600 | tf_op jit(solution)/shard_map/ppermute | solution.py:327
  18.7 0.2 collective-permute-start.5
  18.9 0.6 %copy.10 = f32[8,2,4,128]{3,2,1,0:T(4,128)} copy(f32[8,2,4,128]{3,2,1,0:T(4,128)S(1)} %bitcast.10) | data formatting | bytes 65536
  19.5 0.4 %collective-permute-done.5.near_ref = f32[64,128]{1,0:T(8,128)S(1)} collective-permute-done((f32[64,128]{1,0:T(8,128)S(1)}, f32[64,128]{1,0:T(8,128)S(1)}, u32[]{:S(2)}, u32[]{:S(2)}) %collective-permute-start.5) | collective-permute-done | bytes 32800 | tf_op jit(solution)/shard_map/ppermute | solution.py:326
  19.9 0.8 %shard_map.81._ = f32[64,128]{1,0:T(8,128)} custom-call(f32[4,8,128]{2,1,0:T(8,128)S(1)} %get-tuple-element.8.rates_ref, f32[64,128]{1,0:T(8,128)S(1)} %get-tuple-element.10.own_ref, f32[64,128]{1,0:T(8,128)S(1)} %collective-permute-done.5.near_ref, f32[64,128]{1,0:T(8,128)S(1)} %bitcast.15), custom_call_target="tpu_custom_call" | custom-call | tf_op jit(solution)/shard_map/pallas_call | solution.py:328
  20.8 0.7 %collective-permute-done.6.far_ref = f32[72,128]{1,0:T(8,128)S(1)} collective-permute-done((f32[72,128]{1,0:T(8,128)S(1)}, f32[72,128]{1,0:T(8,128)S(1)}, u32[]{:S(2)}, u32[]{:S(2)}) %collective-permute-start.6) | collective-permute-done | bytes 36896 | tf_op jit(solution)/shard_map/ppermute | solution.py:327
  (2 shorter events, 0.0 us)
Async XLA Ops:
  0.6 3.2 %copy-start.3 = (bf16[2,8,2,1,512]{4,2,3,1,0:T(2,128)(2,1)S(1)}, bf16[2,8,2,1,512]{4,2,3,1,0:T(2,128)(2,1)}, u32[]{:S(2)}) copy-start(bf16[2,8,2,1,512]{4,2,3,1,0:T(2,128)(2,1)} %param.6) | copy-start | bytes 98308
  0.6 9.0 %collective-permute-start.1 = (f32[64,128]{1,0:T(8,128)}, f32[64,128]{1,0:T(8,128)S(1)}, u32[]{:S(2)}, u32[]{:S(2)}) collective-permute-start(f32[64,128]{1,0:T(8,128)} %bitcast.12), channel_id=1, source_target_pairs={{0,8},{1,2},{2,1},{3,4},{4,3},{5,6},{6,5},{7,15},{8,0},{9,10},{10,... | collective-permute-start | bytes 98312 | tf_op jit(solution)/shard_map/ppermute | solution.py:253
  3.6 6.0 %collective-permute-start = (f32[64,128]{1,0:T(8,128)}, f32[64,128]{1,0:T(8,128)S(1)}, u32[]{:S(2)}, u32[]{:S(2)}) collective-permute-start(f32[64,128]{1,0:T(8,128)} %bitcast.13), channel_id=1, source_target_pairs={{0,1},{1,0},{2,3},{3,2},{4,5},{5,4},{6,7},{7,6},{8,9},{9,8},{10,11... | collective-permute-start | bytes 98312 | tf_op jit(solution)/shard_map/ppermute | solution.py:252
  4.8 4.9 %copy-start = (f32[2,8,4,128]{3,2,1,0:T(4,128)S(1)}, f32[2,8,4,128]{3,2,1,0:T(4,128)}, u32[]{:S(2)}) copy-start(f32[2,8,4,128]{3,2,1,0:T(4,128)} %param.7) | copy-start | bytes 98308
  4.8 12.5 %all-to-all-start = ((bf16[32,16,128]{2,1,0:T(8,128)(2,1)}), bf16[32,16,128]{2,1,0:T(8,128)(2,1)S(1)}, u32[]{:S(2)}, u32[]{:S(2)}) async-start(bf16[32,16,128]{2,1,0:T(8,128)(2,1)} %bitcast.20), calls=%async_computation | async-start | bytes 262144 | tf_op jit(solution)/shard_map/all_to_all | solution.py:292
  9.7 7.6 %copy-start.1 = (f32[8,2,4,128]{3,2,1,0:T(4,128)S(1)}, f32[8,2,4,128]{3,2,1,0:T(4,128)}, u32[]{:S(2)}) copy-start(f32[8,2,4,128]{3,2,1,0:T(4,128)} %param.9) | copy-start | bytes 98308
  9.7 7.6 %copy-start.2 = (f32[8,2,4,128]{3,2,1,0:T(4,128)S(1)}, f32[8,2,4,128]{3,2,1,0:T(4,128)}, u32[]{:S(2)}) copy-start(f32[8,2,4,128]{3,2,1,0:T(4,128)} %param.8) | copy-start | bytes 98308
  9.9 5.1 %collective-permute-start.4 = (f32[64,128]{1,0:T(8,128)S(1)}, f32[64,128]{1,0:T(8,128)S(1)}, u32[]{:S(2)}, u32[]{:S(2)}) collective-permute-start(f32[64,128]{1,0:T(8,128)S(1)} %shard_map.79.refs_0_), channel_id=1, source_target_pairs={{0,24},{8,16},{16,8},{24,0},{1,25},{9,17},{17,9},{25,1},{2,26},{10... | collective-permute-start | bytes 98312 | tf_op jit(solution)/shard_map/ppermute | solution.py:309
  12.6 4.1 %collective-permute-start.3 = (f32[64,128]{1,0:T(8,128)S(1)}, f32[64,128]{1,0:T(8,128)S(1)}, u32[]{:S(2)}, u32[]{:S(2)}) collective-permute-start(f32[64,128]{1,0:T(8,128)S(1)} %shard_map.79.refs_0_), channel_id=1, source_target_pairs={{0,16},{8,24},{16,0},{24,8},{1,17},{9,25},{17,1},{25,9},{2,18},{10... | collective-permute-start | bytes 98312 | tf_op jit(solution)/shard_map/ppermute | solution.py:309
  13.2 3.9 %collective-permute-start.2 = (f32[64,128]{1,0:T(8,128)S(1)}, f32[64,128]{1,0:T(8,128)S(1)}, u32[]{:S(2)}, u32[]{:S(2)}) collective-permute-start(f32[64,128]{1,0:T(8,128)S(1)} %shard_map.79.refs_0_), channel_id=1, source_target_pairs={{0,8},{8,0},{16,24},{24,16},{1,9},{9,1},{17,25},{25,17},{2,10},{10... | collective-permute-start | bytes 98312 | tf_op jit(solution)/shard_map/ppermute | solution.py:309
  17.4 4.0 %collective-permute-start.6 = (f32[72,128]{1,0:T(8,128)S(1)}, f32[72,128]{1,0:T(8,128)S(1)}, u32[]{:S(2)}, u32[]{:S(2)}) collective-permute-start(f32[72,128]{1,0:T(8,128)S(1)} %get-tuple-element.11), channel_id=1, source_target_pairs={{0,8},{1,2},{2,1},{3,4},{4,3},{5,6},{6,5},{7,15},{8,0},{9,10},{10,... | collective-permute-start | bytes 110600 | tf_op jit(solution)/shard_map/ppermute | solution.py:327
  18.7 1.2 %collective-permute-start.5 = (f32[64,128]{1,0:T(8,128)S(1)}, f32[64,128]{1,0:T(8,128)S(1)}, u32[]{:S(2)}, u32[]{:S(2)}) collective-permute-start(f32[64,128]{1,0:T(8,128)S(1)} %get-tuple-element.10.own_ref), channel_id=1, source_target_pairs={{0,1},{1,0},{2,3},{3,2},{4,5},{5,4},{6,7},{7,6},{8,9},{9,8},{10,11... | collective-permute-start | bytes 98312 | tf_op jit(solution)/shard_map/ppermute | solution.py:326

commit v11 on v10

--- a/solution.py
+++ b/solution.py
@@ -38,8 +38,8 @@
     doms, rows, groups, chosen_ref, pert_ref, rate_ref, count_ref, out_ref, rates_ref, tiles_ref, rate_here, count_here, sems
 ):
     fetches = [
-        pltpu.make_async_copy(rate_ref, rate_here, sems.at[groups]),
-        pltpu.make_async_copy(count_ref, count_here, sems.at[groups + 1]),
+        pltpu.make_async_copy(rate_ref, rate_here, sems.at[1]),
+        pltpu.make_async_copy(count_ref, count_here, sems.at[2]),
     ]
     for copy in fetches:
         copy.start()
@@ -60,8 +60,9 @@
             preferred_element_type=jnp.float32,
         ).astype(jnp.bfloat16)
         for core in range(2):
-            tiles_ref[core, CHIPS.index(chip)] = both[core * lons : (core + 1) * lons]
-    stores = [pltpu.make_async_copy(tiles_ref, out_ref.at[:, g], sems.at[g]) for g in range(groups)]
+            for g in range(groups):
+                tiles_ref[core, g, CHIPS.index(chip)] = both[core * lons : (core + 1) * lons]
+    stores = [pltpu.make_async_copy(tiles_ref, out_ref, sems.at[0])]
     for copy in stores:
         copy.start()
     for copy in fetches:
@@ -277,10 +278,10 @@
         in_specs=[VMEM, VMEM, ANY, ANY],
         out_specs=[ANY, VMEM],
         scratch_shapes=[
-            pltpu.VMEM((2, doms // 2, lons // doms, fields), jnp.bfloat16),
+            pltpu.VMEM((2, groups, doms // 2, lons // doms, fields), jnp.bfloat16),
             pltpu.VMEM((1, levels), jnp.float32),
             pltpu.VMEM((1, levels), jnp.int32),
-            pltpu.SemaphoreType.DMA((groups + 2,)),
+            pltpu.SemaphoreType.DMA((3,)),
         ],
     )(
         in_vmem(chosen),

time: 21.7 us -> 21.7 us (level)
  no operation moved by 1% of the time
where the time goes in v11:
time: 21.7 us; the launch traced here: 21.4 us
  starting transfers between devices  13.1 us (60%)
  waiting for transfers between devices  4.91 us (23%)
  Pallas kernels  2.07 us (10%)
  between operations  0.74 us (3%)
  local copies, waits for them, and re-layouts  0.64 us (3%)
    all_to_all x1, starting transfers between devices, small_device(): lax.all_to_all(tiles.reshape(-1, *tiles.shape[3:]), ('grp', 'dom'), split...  4.84 us
    ppermute x3, waiting for transfers between devices, small_device(): lax.ppermute(local, 'grp', [(i, i ^ j) for i in range(groups)])  3.65 us
    ppermute x3, starting transfers between devices, small_device(): lax.ppermute(local, 'grp', [(i, i ^ j) for i in range(groups)])  3.55 us
    ppermute x1, starting transfers between devices, beside(): far = lax.ppermute(x, ('grp', 'dom'), far_pairs(groups, doms))  3 us
    ppermute x1, starting transfers between devices, small_device(): far = lax.ppermute(for_far, ('grp', 'dom'), far_pairs(groups, doms))  1.28 us
    pallas_call x1, Pallas kernels, small_device(): pl.pallas_call(functools.partial(pack_kernel, doms, tile, groups), out_sh...  0.88 us
    pallas_call x1, Pallas kernels, small_device(): pl.pallas_call(functools.partial(end_kernel, members, tile), out_shape=ja...  0.83 us
    ppermute x1, waiting for transfers between devices, small_device(): far = lax.ppermute(for_far, ('grp', 'dom'), far_pairs(groups, doms))  0.69 us
  transfers between devices with their start and end apart: 8, of which 6 were waited for; matrix products, arithmetic and copies ran while one was open for 3% of the time, Pallas kernels for 9%

profile of v11, /device:TPU:0, one launch (start us, length us, event | category | flops | bytes accessed | tf_op | source)
XLA Modules:
  0.0 21.4 jit_solution(7786793850370819690)
XLA Ops:
  0.6 0.0 copy-start.3
  0.6 3.0 %collective-permute-start.1 = (f32[64,128]{1,0:T(8,128)}, f32[64,128]{1,0:T(8,128)S(1)}, u32[]{:S(2)}, u32[]{:S(2)}) collective-permute-start(f32[64,128]{1,0:T(8,128)} %bitcast.12), channel_id=1, source_target_pairs={{0,8},{1,2},{2,1},{3,4},{4,3},{5,6},{6,5},{7,15},{8,0},{9,10},{10,... | collective-permute-start | bytes 98312 | tf_op jit(solution)/shard_map/ppermute | solution.py:254
  3.6 0.2 collective-permute-start
  3.9 0.0 copy-done.3
  3.9 0.9 %shard_map.78 = (bf16[2,4,4,16,128]{4,3,2,1,0:T(8,128)(2,1)}, f32[4,8,128]{2,1,0:T(8,128)S(1)}) custom-call(bf16[32,128]{1,0:T(8,128)(2,1)S(1)} %shard_map.77.chosen_ref, bf16[16,2,512]{2,1,0:T(2,128)(2,1)S(1)} %bitcast.19, f32[1,8]{1,0:T(1,128)} %bitcast.22, s32[1,8]{1,0:T(1,128)} %bitcast.23), custom_call_target="tpu_custom_call" | custom-call | tf_op jit(solution)/shard_map/pallas_call | solution.py:272
  4.8 0.0 copy-start
  4.8 4.8 %all-to-all-start = ((bf16[32,16,128]{2,1,0:T(8,128)(2,1)}), bf16[32,16,128]{2,1,0:T(8,128)(2,1)S(1)}, u32[]{:S(2)}, u32[]{:S(2)}) async-start(bf16[32,16,128]{2,1,0:T(8,128)(2,1)} %bitcast.20), calls=%async_computation | async-start | bytes 262144 | tf_op jit(solution)/shard_map/all_to_all | solution.py:293
  9.6 0.0 collective-permute-done.1.far_ref
  9.6 0.0 collective-permute-done.near_ref
  9.6 0.0 copy-done
  9.7 0.0 copy-start.1
  9.7 0.0 copy-start.2
  9.7 0.2 %shard_map.79.refs_0_ = f32[64,128]{1,0:T(8,128)S(1)} custom-call(f32[4,8,128]{2,1,0:T(8,128)S(1)} %get-tuple-element.8.rates_ref, f32[64,128]{1,0:T(8,128)S(1)} %bitcast.14, f32[64,128]{1,0:T(8,128)S(1)} %collective-permute-done.near_ref, f32[64,128]{1,0:T(8,128)S(1)} %collective-permute-done.1.far_ref), custom_call_target="tpu_custom_call" | custom-call | flops 10000000000 | tf_op jit(solution)/shard_map/pallas_call | solution.py:302
  9.9 2.7 %collective-permute-start.4 = (f32[64,128]{1,0:T(8,128)S(1)}, f32[64,128]{1,0:T(8,128)S(1)}, u32[]{:S(2)}, u32[]{:S(2)}) collective-permute-start(f32[64,128]{1,0:T(8,128)S(1)} %shard_map.79.refs_0_), channel_id=1, source_target_pairs={{0,24},{8,16},{16,8},{24,0},{1,25},{9,17},{17,9},{25,1},{2,26},{10... | collective-permute-start | bytes 98312 | tf_op jit(solution)/shard_map/ppermute | solution.py:310
  12.6 0.6 %collective-permute-start.3 = (f32[64,128]{1,0:T(8,128)S(1)}, f32[64,128]{1,0:T(8,128)S(1)}, u32[]{:S(2)}, u32[]{:S(2)}) collective-permute-start(f32[64,128]{1,0:T(8,128)S(1)} %shard_map.79.refs_0_), channel_id=1, source_target_pairs={{0,16},{8,24},{16,0},{24,8},{1,17},{9,25},{17,1},{25,9},{2,18},{10... | collective-permute-start | bytes 98312 | tf_op jit(solution)/shard_map/ppermute | solution.py:310
  13.2 0.3 %collective-permute-start.2 = (f32[64,128]{1,0:T(8,128)S(1)}, f32[64,128]{1,0:T(8,128)S(1)}, u32[]{:S(2)}, u32[]{:S(2)}) collective-permute-start(f32[64,128]{1,0:T(8,128)S(1)} %shard_map.79.refs_0_), channel_id=1, source_target_pairs={{0,8},{8,0},{16,24},{24,16},{1,9},{9,1},{17,25},{25,17},{2,10},{10... | collective-permute-start | bytes 98312 | tf_op jit(solution)/shard_map/ppermute | solution.py:310
  13.5 1.5 %collective-permute-done.4.refs_3_ = f32[64,128]{1,0:T(8,128)S(1)} collective-permute-done((f32[64,128]{1,0:T(8,128)S(1)}, f32[64,128]{1,0:T(8,128)S(1)}, u32[]{:S(2)}, u32[]{:S(2)}) %collective-permute-start.4) | collective-permute-done | bytes 32800 | tf_op jit(solution)/shard_map/ppermute | solution.py:310
  15.0 1.7 %collective-permute-done.3.refs_2_ = f32[64,128]{1,0:T(8,128)S(1)} collective-permute-done((f32[64,128]{1,0:T(8,128)S(1)}, f32[64,128]{1,0:T(8,128)S(1)}, u32[]{:S(2)}, u32[]{:S(2)}) %collective-permute-start.3) | collective-permute-done | bytes 32800 | tf_op jit(solution)/shard_map/ppermute | solution.py:310
  16.7 0.4 %collective-permute-done.2.refs_1_ = f32[64,128]{1,0:T(8,128)S(1)} collective-permute-done((f32[64,128]{1,0:T(8,128)S(1)}, f32[64,128]{1,0:T(8,128)S(1)}, u32[]{:S(2)}, u32[]{:S(2)}) %collective-permute-start.2) | collective-permute-done | bytes 32800 | tf_op jit(solution)/shard_map/ppermute | solution.py:310
  17.1 0.2 all-to-all-done
  17.3 0.0 copy-done.1
  17.3 0.0 copy-done.2
  17.3 0.1 shard_map.80
  17.4 1.3 %collective-permute-start.6 = (f32[72,128]{1,0:T(8,128)S(1)}, f32[72,128]{1,0:T(8,128)S(1)}, u32[]{:S(2)}, u32[]{:S(2)}) collective-permute-start(f32[72,128]{1,0:T(8,128)S(1)} %get-tuple-element.11), channel_id=1, source_target_pairs={{0,8},{1,2},{2,1},{3,4},{4,3},{5,6},{6,5},{7,15},{8,0},{9,10},{10,... | collective-permute-start | bytes 110600 | tf_op jit(solution)/shard_map/ppermute | solution.py:328
  18.7 0.2 collective-permute-start.5
  18.9 0.6 %copy.10 = f32[8,2,4,128]{3,2,1,0:T(4,128)} copy(f32[8,2,4,128]{3,2,1,0:T(4,128)S(1)} %bitcast.10) | data formatting | bytes 65536
  19.5 0.4 %collective-permute-done.5.near_ref = f32[64,128]{1,0:T(8,128)S(1)} collective-permute-done((f32[64,128]{1,0:T(8,128)S(1)}, f32[64,128]{1,0:T(8,128)S(1)}, u32[]{:S(2)}, u32[]{:S(2)}) %collective-permute-start.5) | collective-permute-done | bytes 32800 | tf_op jit(solution)/shard_map/ppermute | solution.py:327
  19.9 0.8 %shard_map.81._ = f32[64,128]{1,0:T(8,128)} custom-call(f32[4,8,128]{2,1,0:T(8,128)S(1)} %get-tuple-element.8.rates_ref, f32[64,128]{1,0:T(8,128)S(1)} %get-tuple-element.10.own_ref, f32[64,128]{1,0:T(8,128)S(1)} %collective-permute-done.5.near_ref, f32[64,128]{1,0:T(8,128)S(1)} %bitcast.15), custom_call_target="tpu_custom_call" | custom-call | tf_op jit(solution)/shard_map/pallas_call | solution.py:329
  20.7 0.7 %collective-permute-done.6.far_ref = f32[72,128]{1,0:T(8,128)S(1)} collective-permute-done((f32[72,128]{1,0:T(8,128)S(1)}, f32[72,128]{1,0:T(8,128)S(1)}, u32[]{:S(2)}, u32[]{:S(2)}) %collective-permute-start.6) | collective-permute-done | bytes 36896 | tf_op jit(solution)/shard_map/ppermute | solution.py:328
  (2 shorter events, 0.0 us)
Async XLA Ops:
  0.6 3.2 %copy-start.3 = (bf16[2,8,2,1,512]{4,2,3,1,0:T(2,128)(2,1)S(1)}, bf16[2,8,2,1,512]{4,2,3,1,0:T(2,128)(2,1)}, u32[]{:S(2)}) copy-start(bf16[2,8,2,1,512]{4,2,3,1,0:T(2,128)(2,1)} %param.6) | copy-start | bytes 98308
  0.6 9.0 %collective-permute-start.1 = (f32[64,128]{1,0:T(8,128)}, f32[64,128]{1,0:T(8,128)S(1)}, u32[]{:S(2)}, u32[]{:S(2)}) collective-permute-start(f32[64,128]{1,0:T(8,128)} %bitcast.12), channel_id=1, source_target_pairs={{0,8},{1,2},{2,1},{3,4},{4,3},{5,6},{6,5},{7,15},{8,0},{9,10},{10,... | collective-permute-start | bytes 98312 | tf_op jit(solution)/shard_map/ppermute | solution.py:254
  3.6 6.0 %collective-permute-start = (f32[64,128]{1,0:T(8,128)}, f32[64,128]{1,0:T(8,128)S(1)}, u32[]{:S(2)}, u32[]{:S(2)}) collective-permute-start(f32[64,128]{1,0:T(8,128)} %bitcast.13), channel_id=1, source_target_pairs={{0,1},{1,0},{2,3},{3,2},{4,5},{5,4},{6,7},{7,6},{8,9},{9,8},{10,11... | collective-permute-start | bytes 98312 | tf_op jit(solution)/shard_map/ppermute | solution.py:253
  4.8 4.9 %copy-start = (f32[2,8,4,128]{3,2,1,0:T(4,128)S(1)}, f32[2,8,4,128]{3,2,1,0:T(4,128)}, u32[]{:S(2)}) copy-start(f32[2,8,4,128]{3,2,1,0:T(4,128)} %param.7) | copy-start | bytes 98308
  4.8 12.5 %all-to-all-start = ((bf16[32,16,128]{2,1,0:T(8,128)(2,1)}), bf16[32,16,128]{2,1,0:T(8,128)(2,1)S(1)}, u32[]{:S(2)}, u32[]{:S(2)}) async-start(bf16[32,16,128]{2,1,0:T(8,128)(2,1)} %bitcast.20), calls=%async_computation | async-start | bytes 262144 | tf_op jit(solution)/shard_map/all_to_all | solution.py:293
  9.7 7.6 %copy-start.1 = (f32[8,2,4,128]{3,2,1,0:T(4,128)S(1)}, f32[8,2,4,128]{3,2,1,0:T(4,128)}, u32[]{:S(2)}) copy-start(f32[8,2,4,128]{3,2,1,0:T(4,128)} %param.9) | copy-start | bytes 98308
  9.7 7.6 %copy-start.2 = (f32[8,2,4,128]{3,2,1,0:T(4,128)S(1)}, f32[8,2,4,128]{3,2,1,0:T(4,128)}, u32[]{:S(2)}) copy-start(f32[8,2,4,128]{3,2,1,0:T(4,128)} %param.8) | copy-start | bytes 98308
  9.9 5.1 %collective-permute-start.4 = (f32[64,128]{1,0:T(8,128)S(1)}, f32[64,128]{1,0:T(8,128)S(1)}, u32[]{:S(2)}, u32[]{:S(2)}) collective-permute-start(f32[64,128]{1,0:T(8,128)S(1)} %shard_map.79.refs_0_), channel_id=1, source_target_pairs={{0,24},{8,16},{16,8},{24,0},{1,25},{9,17},{17,9},{25,1},{2,26},{10... | collective-permute-start | bytes 98312 | tf_op jit(solution)/shard_map/ppermute | solution.py:310
  12.6 4.1 %collective-permute-start.3 = (f32[64,128]{1,0:T(8,128)S(1)}, f32[64,128]{1,0:T(8,128)S(1)}, u32[]{:S(2)}, u32[]{:S(2)}) collective-permute-start(f32[64,128]{1,0:T(8,128)S(1)} %shard_map.79.refs_0_), channel_id=1, source_target_pairs={{0,16},{8,24},{16,0},{24,8},{1,17},{9,25},{17,1},{25,9},{2,18},{10... | collective-permute-start | bytes 98312 | tf_op jit(solution)/shard_map/ppermute | solution.py:310
  13.2 3.9 %collective-permute-start.2 = (f32[64,128]{1,0:T(8,128)S(1)}, f32[64,128]{1,0:T(8,128)S(1)}, u32[]{:S(2)}, u32[]{:S(2)}) collective-permute-start(f32[64,128]{1,0:T(8,128)S(1)} %shard_map.79.refs_0_), channel_id=1, source_target_pairs={{0,8},{8,0},{16,24},{24,16},{1,9},{9,1},{17,25},{25,17},{2,10},{10... | collective-permute-start | bytes 98312 | tf_op jit(solution)/shard_map/ppermute | solution.py:310
  17.4 4.0 %collective-permute-start.6 = (f32[72,128]{1,0:T(8,128)S(1)}, f32[72,128]{1,0:T(8,128)S(1)}, u32[]{:S(2)}, u32[]{:S(2)}) collective-permute-start(f32[72,128]{1,0:T(8,128)S(1)} %get-tuple-element.11), channel_id=1, source_target_pairs={{0,8},{1,2},{2,1},{3,4},{4,3},{5,6},{6,5},{7,15},{8,0},{9,10},{10,... | collective-permute-start | bytes 110600 | tf_op jit(solution)/shard_map/ppermute | solution.py:328
  18.7 1.2 %collective-permute-start.5 = (f32[64,128]{1,0:T(8,128)S(1)}, f32[64,128]{1,0:T(8,128)S(1)}, u32[]{:S(2)}, u32[]{:S(2)}) collective-permute-start(f32[64,128]{1,0:T(8,128)S(1)} %get-tuple-element.10.own_ref), channel_id=1, source_target_pairs={{0,1},{1,0},{2,3},{3,2},{4,5},{5,4},{6,7},{7,6},{8,9},{9,8},{10,11... | collective-permute-start | bytes 98312 | tf_op jit(solution)/shard_map/ppermute | solution.py:327

commit v12 on v10

--- a/solution.py
+++ b/solution.py
@@ -47,10 +47,11 @@
     lons = cells // (doms * rows)
     pert = pert_ref[...].astype(jnp.float32)
     fields = jnp.concatenate([pert[:, v, :] for v in range(variables)], axis=0)
+    fields = fields.astype(jnp.bfloat16)
     row_of = (lax.broadcasted_iota(jnp.int32, fields.shape, 1) // lons) % rows
     spread = jnp.concatenate(
-        [jnp.where(row_of == r, fields, 0.0) for r in range(rows)], axis=0
-    ).astype(jnp.bfloat16)
+        [jnp.where(row_of == r, fields, jnp.bfloat16(0)) for r in range(rows)], axis=0
+    )
     chosen, pair = chosen_ref[...], chosen_ref.shape[1]
     for chip in range(doms // 2):
         both = lax.dot_general(

time: 21.7 us -> 21.7 us (level)
  no operation moved by 1% of the time
where the time goes in v12:
time: 21.7 us; the launch traced here: 21.5 us
  starting transfers between devices  13.1 us (60%)
  waiting for transfers between devices  4.91 us (23%)
  Pallas kernels  2.09 us (10%)
  between operations  0.74 us (3%)
  local copies, waits for them, and re-layouts  0.64 us (3%)
    all_to_all x1, starting transfers between devices, small_device(): lax.all_to_all(tiles.reshape(-1, *tiles.shape[3:]), ('grp', 'dom'), split...  4.84 us
    ppermute x3, waiting for transfers between devices, small_device(): lax.ppermute(local, 'grp', [(i, i ^ j) for i in range(groups)])  3.65 us
    ppermute x3, starting transfers between devices, small_device(): lax.ppermute(local, 'grp', [(i, i ^ j) for i in range(groups)])  3.55 us
    ppermute x1, starting transfers between devices, beside(): far = lax.ppermute(x, ('grp', 'dom'), far_pairs(groups, doms))  3 us
    ppermute x1, starting transfers between devices, small_device(): far = lax.ppermute(for_far, ('grp', 'dom'), far_pairs(groups, doms))  1.28 us
    pallas_call x1, Pallas kernels, small_device(): pl.pallas_call(functools.partial(pack_kernel, doms, tile, groups), out_sh...  0.9 us
    pallas_call x1, Pallas kernels, small_device(): pl.pallas_call(functools.partial(end_kernel, members, tile), out_shape=ja...  0.83 us
    ppermute x1, waiting for transfers between devices, small_device(): far = lax.ppermute(for_far, ('grp', 'dom'), far_pairs(groups, doms))  0.69 us
  transfers between devices with their start and end apart: 8, of which 6 were waited for; matrix products, arithmetic and copies ran while one was open for 3% of the time, Pallas kernels for 9%

profile of v12, /device:TPU:0, one launch (start us, length us, event | category | flops | bytes accessed | tf_op | source)
XLA Modules:
  0.0 21.5 jit_solution(7918028744834999295)
XLA Ops:
  0.6 0.0 copy-start.3
  0.6 3.0 %collective-permute-start.1 = (f32[64,128]{1,0:T(8,128)}, f32[64,128]{1,0:T(8,128)S(1)}, u32[]{:S(2)}, u32[]{:S(2)}) collective-permute-start(f32[64,128]{1,0:T(8,128)} %bitcast.12), channel_id=1, source_target_pairs={{0,8},{1,2},{2,1},{3,4},{4,3},{5,6},{6,5},{7,15},{8,0},{9,10},{10,... | collective-permute-start | bytes 98312 | tf_op jit(solution)/shard_map/ppermute | solution.py:254
  3.6 0.2 collective-permute-start
  3.9 0.0 copy-done.3
  3.9 0.9 %shard_map.78 = (bf16[2,4,4,16,128]{4,3,2,1,0:T(8,128)(2,1)}, f32[4,8,128]{2,1,0:T(8,128)S(1)}) custom-call(bf16[32,128]{1,0:T(8,128)(2,1)S(1)} %shard_map.77.chosen_ref, bf16[16,2,512]{2,1,0:T(2,128)(2,1)S(1)} %bitcast.19, f32[1,8]{1,0:T(1,128)} %bitcast.22, s32[1,8]{1,0:T(1,128)} %bitcast.23), custom_call_target="tpu_custom_call" | custom-call | tf_op jit(solution)/shard_map/pallas_call | solution.py:272
  4.8 0.0 copy-start
  4.8 4.8 %all-to-all-start = ((bf16[32,16,128]{2,1,0:T(8,128)(2,1)}), bf16[32,16,128]{2,1,0:T(8,128)(2,1)S(1)}, u32[]{:S(2)}, u32[]{:S(2)}) async-start(bf16[32,16,128]{2,1,0:T(8,128)(2,1)} %bitcast.20), calls=%async_computation | async-start | bytes 262144 | tf_op jit(solution)/shard_map/all_to_all | solution.py:293
  9.6 0.0 collective-permute-done.1.far_ref
  9.6 0.0 collective-permute-done.near_ref
  9.7 0.0 copy-done
  9.7 0.0 copy-start.1
  9.7 0.0 copy-start.2
  9.7 0.2 %shard_map.79.refs_0_ = f32[64,128]{1,0:T(8,128)S(1)} custom-call(f32[4,8,128]{2,1,0:T(8,128)S(1)} %get-tuple-element.8.rates_ref, f32[64,128]{1,0:T(8,128)S(1)} %bitcast.14, f32[64,128]{1,0:T(8,128)S(1)} %collective-permute-done.near_ref, f32[64,128]{1,0:T(8,128)S(1)} %collective-permute-done.1.far_ref), custom_call_target="tpu_custom_call" | custom-call | flops 10000000000 | tf_op jit(solution)/shard_map/pallas_call | solution.py:302
  9.9 2.7 %collective-permute-start.4 = (f32[64,128]{1,0:T(8,128)S(1)}, f32[64,128]{1,0:T(8,128)S(1)}, u32[]{:S(2)}, u32[]{:S(2)}) collective-permute-start(f32[64,128]{1,0:T(8,128)S(1)} %shard_map.79.refs_0_), channel_id=1, source_target_pairs={{0,24},{8,16},{16,8},{24,0},{1,25},{9,17},{17,9},{25,1},{2,26},{10... | collective-permute-start | bytes 98312 | tf_op jit(solution)/shard_map/ppermute | solution.py:310
  12.6 0.6 %collective-permute-start.3 = (f32[64,128]{1,0:T(8,128)S(1)}, f32[64,128]{1,0:T(8,128)S(1)}, u32[]{:S(2)}, u32[]{:S(2)}) collective-permute-start(f32[64,128]{1,0:T(8,128)S(1)} %shard_map.79.refs_0_), channel_id=1, source_target_pairs={{0,16},{8,24},{16,0},{24,8},{1,17},{9,25},{17,1},{25,9},{2,18},{10... | collective-permute-start | bytes 98312 | tf_op jit(solution)/shard_map/ppermute | solution.py:310
  13.2 0.3 %collective-permute-start.2 = (f32[64,128]{1,0:T(8,128)S(1)}, f32[64,128]{1,0:T(8,128)S(1)}, u32[]{:S(2)}, u32[]{:S(2)}) collective-permute-start(f32[64,128]{1,0:T(8,128)S(1)} %shard_map.79.refs_0_), channel_id=1, source_target_pairs={{0,8},{8,0},{16,24},{24,16},{1,9},{9,1},{17,25},{25,17},{2,10},{10... | collective-permute-start | bytes 98312 | tf_op jit(solution)/shard_map/ppermute | solution.py:310
  13.5 1.5 %collective-permute-done.4.refs_3_ = f32[64,128]{1,0:T(8,128)S(1)} collective-permute-done((f32[64,128]{1,0:T(8,128)S(1)}, f32[64,128]{1,0:T(8,128)S(1)}, u32[]{:S(2)}, u32[]{:S(2)}) %collective-permute-start.4) | collective-permute-done | bytes 32800 | tf_op jit(solution)/shard_map/ppermute | solution.py:310
  15.0 1.7 %collective-permute-done.3.refs_2_ = f32[64,128]{1,0:T(8,128)S(1)} collective-permute-done((f32[64,128]{1,0:T(8,128)S(1)}, f32[64,128]{1,0:T(8,128)S(1)}, u32[]{:S(2)}, u32[]{:S(2)}) %collective-permute-start.3) | collective-permute-done | bytes 32800 | tf_op jit(solution)/shard_map/ppermute | solution.py:310
  16.7 0.4 %collective-permute-done.2.refs_1_ = f32[64,128]{1,0:T(8,128)S(1)} collective-permute-done((f32[64,128]{1,0:T(8,128)S(1)}, f32[64,128]{1,0:T(8,128)S(1)}, u32[]{:S(2)}, u32[]{:S(2)}) %collective-permute-start.2) | collective-permute-done | bytes 32800 | tf_op jit(solution)/shard_map/ppermute | solution.py:310
  17.1 0.2 all-to-all-done
  17.3 0.0 copy-done.1
  17.3 0.0 copy-done.2
  17.3 0.1 shard_map.80
  17.4 1.3 %collective-permute-start.6 = (f32[72,128]{1,0:T(8,128)S(1)}, f32[72,128]{1,0:T(8,128)S(1)}, u32[]{:S(2)}, u32[]{:S(2)}) collective-permute-start(f32[72,128]{1,0:T(8,128)S(1)} %get-tuple-element.11), channel_id=1, source_target_pairs={{0,8},{1,2},{2,1},{3,4},{4,3},{5,6},{6,5},{7,15},{8,0},{9,10},{10,... | collective-permute-start | bytes 110600 | tf_op jit(solution)/shard_map/ppermute | solution.py:328
  18.7 0.2 collective-permute-start.5
  18.9 0.6 %copy.10 = f32[8,2,4,128]{3,2,1,0:T(4,128)} copy(f32[8,2,4,128]{3,2,1,0:T(4,128)S(1)} %bitcast.10) | data formatting | bytes 65536
  19.5 0.4 %collective-permute-done.5.near_ref = f32[64,128]{1,0:T(8,128)S(1)} collective-permute-done((f32[64,128]{1,0:T(8,128)S(1)}, f32[64,128]{1,0:T(8,128)S(1)}, u32[]{:S(2)}, u32[]{:S(2)}) %collective-permute-start.5) | collective-permute-done | bytes 32800 | tf_op jit(solution)/shard_map/ppermute | solution.py:327
  19.9 0.8 %shard_map.81._ = f32[64,128]{1,0:T(8,128)} custom-call(f32[4,8,128]{2,1,0:T(8,128)S(1)} %get-tuple-element.8.rates_ref, f32[64,128]{1,0:T(8,128)S(1)} %get-tuple-element.10.own_ref, f32[64,128]{1,0:T(8,128)S(1)} %collective-permute-done.5.near_ref, f32[64,128]{1,0:T(8,128)S(1)} %bitcast.15), custom_call_target="tpu_custom_call" | custom-call | tf_op jit(solution)/shard_map/pallas_call | solution.py:329
  20.8 0.7 %collective-permute-done.6.far_ref = f32[72,128]{1,0:T(8,128)S(1)} collective-permute-done((f32[72,128]{1,0:T(8,128)S(1)}, f32[72,128]{1,0:T(8,128)S(1)}, u32[]{:S(2)}, u32[]{:S(2)}) %collective-permute-start.6) | collective-permute-done | bytes 36896 | tf_op jit(solution)/shard_map/ppermute | solution.py:328
  (2 shorter events, 0.0 us)
Async XLA Ops:
  0.6 3.2 %copy-start.3 = (bf16[2,8,2,1,512]{4,2,3,1,0:T(2,128)(2,1)S(1)}, bf16[2,8,2,1,512]{4,2,3,1,0:T(2,128)(2,1)}, u32[]{:S(2)}) copy-start(bf16[2,8,2,1,512]{4,2,3,1,0:T(2,128)(2,1)} %param.6) | copy-start | bytes 98308
  0.6 9.0 %collective-permute-start.1 = (f32[64,128]{1,0:T(8,128)}, f32[64,128]{1,0:T(8,128)S(1)}, u32[]{:S(2)}, u32[]{:S(2)}) collective-permute-start(f32[64,128]{1,0:T(8,128)} %bitcast.12), channel_id=1, source_target_pairs={{0,8},{1,2},{2,1},{3,4},{4,3},{5,6},{6,5},{7,15},{8,0},{9,10},{10,... | collective-permute-start | bytes 98312 | tf_op jit(solution)/shard_map/ppermute | solution.py:254
  3.6 6.0 %collective-permute-start = (f32[64,128]{1,0:T(8,128)}, f32[64,128]{1,0:T(8,128)S(1)}, u32[]{:S(2)}, u32[]{:S(2)}) collective-permute-start(f32[64,128]{1,0:T(8,128)} %bitcast.13), channel_id=1, source_target_pairs={{0,1},{1,0},{2,3},{3,2},{4,5},{5,4},{6,7},{7,6},{8,9},{9,8},{10,11... | collective-permute-start | bytes 98312 | tf_op jit(solution)/shard_map/ppermute | solution.py:253
  4.8 4.9 %copy-start = (f32[2,8,4,128]{3,2,1,0:T(4,128)S(1)}, f32[2,8,4,128]{3,2,1,0:T(4,128)}, u32[]{:S(2)}) copy-start(f32[2,8,4,128]{3,2,1,0:T(4,128)} %param.7) | copy-start | bytes 98308
  4.8 12.5 %all-to-all-start = ((bf16[32,16,128]{2,1,0:T(8,128)(2,1)}), bf16[32,16,128]{2,1,0:T(8,128)(2,1)S(1)}, u32[]{:S(2)}, u32[]{:S(2)}) async-start(bf16[32,16,128]{2,1,0:T(8,128)(2,1)} %bitcast.20), calls=%async_computation | async-start | bytes 262144 | tf_op jit(solution)/shard_map/all_to_all | solution.py:293
  9.7 7.6 %copy-start.1 = (f32[8,2,4,128]{3,2,1,0:T(4,128)S(1)}, f32[8,2,4,128]{3,2,1,0:T(4,128)}, u32[]{:S(2)}) copy-start(f32[8,2,4,128]{3,2,1,0:T(4,128)} %param.9) | copy-start | bytes 98308
  9.7 7.6 %copy-start.2 = (f32[8,2,4,128]{3,2,1,0:T(4,128)S(1)}, f32[8,2,4,128]{3,2,1,0:T(4,128)}, u32[]{:S(2)}) copy-start(f32[8,2,4,128]{3,2,1,0:T(4,128)} %param.8) | copy-start | bytes 98308
  9.9 5.1 %collective-permute-start.4 = (f32[64,128]{1,0:T(8,128)S(1)}, f32[64,128]{1,0:T(8,128)S(1)}, u32[]{:S(2)}, u32[]{:S(2)}) collective-permute-start(f32[64,128]{1,0:T(8,128)S(1)} %shard_map.79.refs_0_), channel_id=1, source_target_pairs={{0,24},{8,16},{16,8},{24,0},{1,25},{9,17},{17,9},{25,1},{2,26},{10... | collective-permute-start | bytes 98312 | tf_op jit(solution)/shard_map/ppermute | solution.py:310
  12.6 4.1 %collective-permute-start.3 = (f32[64,128]{1,0:T(8,128)S(1)}, f32[64,128]{1,0:T(8,128)S(1)}, u32[]{:S(2)}, u32[]{:S(2)}) collective-permute-start(f32[64,128]{1,0:T(8,128)S(1)} %shard_map.79.refs_0_), channel_id=1, source_target_pairs={{0,16},{8,24},{16,0},{24,8},{1,17},{9,25},{17,1},{25,9},{2,18},{10... | collective-permute-start | bytes 98312 | tf_op jit(solution)/shard_map/ppermute | solution.py:310
  13.2 3.9 %collective-permute-start.2 = (f32[64,128]{1,0:T(8,128)S(1)}, f32[64,128]{1,0:T(8,128)S(1)}, u32[]{:S(2)}, u32[]{:S(2)}) collective-permute-start(f32[64,128]{1,0:T(8,128)S(1)} %shard_map.79.refs_0_), channel_id=1, source_target_pairs={{0,8},{8,0},{16,24},{24,16},{1,9},{9,1},{17,25},{25,17},{2,10},{10... | collective-permute-start | bytes 98312 | tf_op jit(solution)/shard_map/ppermute | solution.py:310
  17.4 4.0 %collective-permute-start.6 = (f32[72,128]{1,0:T(8,128)S(1)}, f32[72,128]{1,0:T(8,128)S(1)}, u32[]{:S(2)}, u32[]{:S(2)}) collective-permute-start(f32[72,128]{1,0:T(8,128)S(1)} %get-tuple-element.11), channel_id=1, source_target_pairs={{0,8},{1,2},{2,1},{3,4},{4,3},{5,6},{6,5},{7,15},{8,0},{9,10},{10,... | collective-permute-start | bytes 110600 | tf_op jit(solution)/shard_map/ppermute | solution.py:328
  18.7 1.2 %collective-permute-start.5 = (f32[64,128]{1,0:T(8,128)S(1)}, f32[64,128]{1,0:T(8,128)S(1)}, u32[]{:S(2)}, u32[]{:S(2)}) collective-permute-start(f32[64,128]{1,0:T(8,128)S(1)} %get-tuple-element.10.own_ref), channel_id=1, source_target_pairs={{0,1},{1,0},{2,3},{3,2},{4,5},{5,4},{6,7},{7,6},{8,9},{9,8},{10,11... | collective-permute-start | bytes 98312 | tf_op jit(solution)/shard_map/ppermute | solution.py:327
